TPU v7x, 32 devices: a whole 2x2x4 slice. The times are simulated.
32 devices in a mesh: fsdp: 4 (over y, core), ctx: 4 (over z), tp: 2 (over x).
Axes of the slice: x: 2, y: 2, z: 4, core: 2. Of those that a mesh axis runs over, the one named last changes fastest.
Arguments:
- tokens: bfloat16 [4, 2048, 768], P('fsdp', 'ctx'), may hold values from -6 to 6
- segments: int32 [4, 2048], P('fsdp'), may hold values from 0 to 6, as said below
- routes: int32 [4, 2048, 2], P('fsdp', 'ctx'), may hold values from 0 to 7, all different within a row; in each aligned block of 512 rows (0 to 511, 512 to 1023, ..., all dimensions but the last counted through in order) at most 192 rows name the same one
- query_weight: bfloat16 [768, 768], P('fsdp', 'tp'), may hold values from -0.21875 to 0.21875
- key_weight: bfloat16 [768, 768], P('fsdp', 'tp'), may hold values from -0.21875 to 0.21875
- value_weight: bfloat16 [768, 768], P('fsdp', 'tp'), may hold values from -0.21875 to 0.21875
- out_weight: bfloat16 [768, 768], P('tp', 'fsdp'), may hold values from -3.5 to 3.5
- attn_gain: bfloat16 [768], P('fsdp'), may hold values from 0.099609375 to 1.8984375
- ffn_gain: bfloat16 [768], P('fsdp'), may hold values from 0.099609375 to 1.8984375
- router_weight: bfloat16 [768, 8], P('fsdp'), may hold values from -0.21875 to 0.21875
- shared_gate: bfloat16 [768, 2048], P('fsdp', 'tp'), may hold values from -0.21875 to 0.21875
- shared_up: bfloat16 [768, 2048], P('fsdp', 'tp'), may hold values from -0.21875 to 0.21875
- shared_down: bfloat16 [2048, 768], P('tp', 'fsdp'), may hold values from -0.125 to 0.125
- expert_gate: bfloat16 [8, 768, 2048], P(None, 'fsdp', 'tp'), may hold values from -0.21875 to 0.21875
- expert_up: bfloat16 [8, 768, 2048], P(None, 'fsdp', 'tp'), may hold values from -0.21875 to 0.21875
- expert_down: bfloat16 [8, 2048, 768], P(None, 'tp', 'fsdp'), may hold values from -0.125 to 0.125
- cotangent: bfloat16 [4, 2048, 768], P('fsdp', 'ctx'), may hold values from -6 to 6
Outputs:
- output: bfloat16 [4, 2048, 768], P('fsdp', 'ctx')
- input_grad: bfloat16 [4, 2048, 768], P('fsdp', 'ctx')
- grad_query_weight: float32 [768, 768], P('fsdp', 'tp')
- grad_key_weight: float32 [768, 768], P('fsdp', 'tp')
- grad_value_weight: float32 [768, 768], P('fsdp', 'tp')
- grad_out_weight: float32 [768, 768], P('tp', 'fsdp')
- grad_attn_gain: float32 [768], P('fsdp')
- grad_ffn_gain: float32 [768], P('fsdp')
- grad_router_weight: float32 [768, 8], P('fsdp')
- grad_shared_gate: float32 [768, 2048], P('fsdp', 'tp')
- grad_shared_up: float32 [768, 2048], P('fsdp', 'tp')
- grad_shared_down: float32 [2048, 768], P('tp', 'fsdp')
- grad_expert_gate: float32 [8, 768, 2048], P(None, 'fsdp', 'tp')
- grad_expert_up: float32 [8, 768, 2048], P(None, 'fsdp', 'tp')
- grad_expert_down: float32 [8, 2048, 768], P(None, 'tp', 'fsdp')
Inputs may be any that keep to these rules, and one draw needn't show every extreme that they name: `segments`: document numbers never fall along a sequence. `routes`: each token names 2 different experts; in each aligned block of 512 positions of a sequence no expert is named more than 192 times, and in some block one expert is named exactly 192 times.
All inputs are finite; a program needn't handle non-finite values.
Results may differ from a plain program's by a relative error of at most 0.02.
Values may be sent and summed in bfloat16 or wider, within the bound.
No kernel may reach another device: no remote copies, remote signals or barrier semaphores. Data moves between devices by JAX's collectives and lax.ppermute only.
A program may use at most 256 MiB of HBM per device.

v0:
```python
import jax
import jax.numpy as jnp
from jax import lax
from jax.sharding import PartitionSpec as P

HD = 64
WINDOW = 1024


EPS = 1e-06


def from_behind(block, axis, distance):
    devices = range(lax.axis_size(axis))
    route = [(i - distance, i) for i in devices if i - distance in devices]
    return lax.ppermute(block, axis, route)


def rotation_tables(positions, head_size):
    half = head_size // 2
    rates = 10000.0 ** (-2.0 * jnp.arange(half, dtype=jnp.float32) / head_size)
    angles = positions.astype(jnp.float32)[:, None] * rates[None, :]
    return (jnp.cos(angles)[:, None, :], jnp.sin(angles)[:, None, :])


def rotate(values, cosine, sine):
    half = values.shape[-1] // 2
    first = values[..., :half]
    second = values[..., half:]
    return jnp.concatenate(
        [first * cosine - second * sine, second * cosine + first * sine], axis=-1
    )


def unrotate(grads, cosine, sine):
    half = grads.shape[-1] // 2
    first = grads[..., :half]
    second = grads[..., half:]
    return jnp.concatenate(
        [first * cosine + second * sine, second * cosine - first * sine], axis=-1
    )


def normalize(values, gain):
    scale = lax.rsqrt(jnp.mean(values * values, axis=-1, keepdims=True) + EPS)
    return (values * scale * gain, scale)


def norm_back(grad, values, scale, gain):
    grad_gain = jnp.sum(grad * values * scale, axis=(0, 1))
    scaled = grad * gain
    grad_values = scale * scaled - values * scale * scale * scale * jnp.mean(
        scaled * values, axis=-1, keepdims=True
    )
    return (grad_values, grad_gain)


def silu_slope(values):
    sigma = jax.nn.sigmoid(values)
    return sigma * (1.0 + values * (1.0 - sigma))


def project(left, right):
    return jnp.einsum("sbd,dc->sbc", left, right, preferred_element_type=jnp.float32)


def project_back(left, right):
    return jnp.einsum("sbc,dc->sbd", left, right, preferred_element_type=jnp.float32)


def weight_grad(left, right):
    return jnp.einsum("sbd,sbc->dc", left, right, preferred_element_type=jnp.float32)


def local(
    tokens,
    segments,
    routes,
    query_weight,
    key_weight,
    value_weight,
    out_weight,
    attn_gain,
    ffn_gain,
    router_weight,
    shared_gate,
    shared_up,
    shared_down,
    expert_gate,
    expert_up,
    expert_down,
    cotangent,
):
    (
        query_full,
        key_full,
        value_full,
        out_full,
        attn_gain_full,
        ffn_gain_full,
        router_full,
        shared_gate_full,
        shared_up_full,
        shared_down_full,
        expert_gate_full,
        expert_up_full,
        expert_down_full,
    ) = (
        lax.all_gather(query_weight, "fsdp", axis=0, tiled=True),
        lax.all_gather(key_weight, "fsdp", axis=0, tiled=True),
        lax.all_gather(value_weight, "fsdp", axis=0, tiled=True),
        lax.all_gather(out_weight, "fsdp", axis=1, tiled=True),
        lax.all_gather(attn_gain, "fsdp", axis=0, tiled=True),
        lax.all_gather(ffn_gain, "fsdp", axis=0, tiled=True),
        lax.all_gather(router_weight, "fsdp", axis=0, tiled=True),
        lax.all_gather(shared_gate, "fsdp", axis=0, tiled=True),
        lax.all_gather(shared_up, "fsdp", axis=0, tiled=True),
        lax.all_gather(shared_down, "fsdp", axis=1, tiled=True),
        lax.all_gather(expert_gate, "fsdp", axis=1, tiled=True),
        lax.all_gather(expert_up, "fsdp", axis=1, tiled=True),
        lax.all_gather(expert_down, "fsdp", axis=2, tiled=True),
    )
    sequences, block, width = tokens.shape
    heads = query_full.shape[1] // HD
    top_count = routes.shape[2]
    experts = router_full.shape[1]
    capacity = 3 * top_count * block // (2 * experts)
    attn_scale = attn_gain_full.astype(jnp.float32)
    ffn_scale = ffn_gain_full.astype(jnp.float32)
    place = lax.axis_index("ctx")
    positions = place * block + jnp.arange(block, dtype=jnp.int32)
    cosine, sine = rotation_tables(positions, HD)
    score_scale = HD ** (-0.5)
    inputs = tokens.astype(jnp.float32)
    hidden, scale_attn = normalize(inputs, attn_scale)
    hidden_low = hidden.astype(jnp.bfloat16)
    query = rotate(
        project(hidden_low, query_full).reshape(sequences, block, heads, HD), cosine, sine
    ).astype(jnp.bfloat16)
    keys = rotate(
        project(hidden_low, key_full).reshape(sequences, block, heads, HD), cosine, sine
    ).astype(jnp.bfloat16)
    values = (
        project(hidden_low, value_full).astype(jnp.bfloat16).reshape(sequences, block, heads, HD)
    )
    key_parts = [keys]
    value_parts = [values]
    for reach in (1, 2):
        far_keys, far_values = from_behind((keys, values), "ctx", reach)
        key_parts.insert(0, far_keys)
        value_parts.insert(0, far_values)
    all_keys = jnp.concatenate(key_parts, axis=1)
    all_values = jnp.concatenate(value_parts, axis=1)
    segment_pad = jnp.concatenate(
        [jnp.full((sequences, 2 * block), -1, jnp.int32), segments], axis=1
    )
    key_segment = lax.dynamic_slice_in_dim(segment_pad, place * block, 3 * block, 1)
    query_segment = lax.dynamic_slice_in_dim(segments, place * block, block, 1)
    key_place = (place - 2) * block + jnp.arange(3 * block, dtype=jnp.int32)
    allowed = (
        (query_segment[:, :, None] == key_segment[:, None, :])
        & (key_place[None, None, :] <= positions[None, :, None])
        & (positions[None, :, None] - key_place[None, None, :] < WINDOW)
    )

    def scores_of(query_one, keys_one, allowed_one):
        raw = (
            jnp.einsum("qhd,khd->hqk", query_one, keys_one, preferred_element_type=jnp.float32)
            * score_scale
        )
        return jnp.where(allowed_one[None], raw, -1e30)

    def attend(items):
        query_one, keys_one, values_one, allowed_one = items
        scores = scores_of(query_one, keys_one, allowed_one)
        top = jnp.max(scores, axis=-1, keepdims=True)
        expo = jnp.exp(scores - top)
        total = jnp.sum(expo, axis=-1, keepdims=True)
        weights = (expo / total).astype(jnp.bfloat16)
        result = jnp.einsum("hqk,khd->qhd", weights, values_one, preferred_element_type=jnp.float32)
        return (result, top + jnp.log(total))

    attended, log_total = lax.map(attend, (query, all_keys, all_values, allowed))
    attended_low = attended.reshape(sequences, block, heads * HD).astype(jnp.bfloat16)
    attn_sum = lax.psum(project(attended_low, out_full), "tp")
    mixed = inputs + attn_sum
    normed, scale_ffn = normalize(mixed, ffn_scale)
    normed_low = normed.astype(jnp.bfloat16)
    logits = project(normed_low, router_full)
    chosen = jnp.take_along_axis(logits, routes, axis=2)
    gates = jax.nn.softmax(chosen, axis=-1)
    flat_routes = routes.reshape(sequences, block * top_count)
    hits = (flat_routes[:, :, None] == jnp.arange(experts, dtype=jnp.int32)[None, None, :]).astype(
        jnp.int32
    )
    rank = jnp.sum((jnp.cumsum(hits, axis=1) - hits) * hits, axis=2)
    slot_pick = flat_routes * capacity + rank
    seq_index = jnp.arange(sequences, dtype=jnp.int32)[:, None]
    owners = jnp.arange(block * top_count, dtype=jnp.int32)[None, :]
    slot_owner = (
        jnp.full((sequences, experts * capacity), block * top_count, jnp.int32)
        .at[seq_index, slot_pick]
        .set(owners)
    )
    slot_token = slot_owner // top_count
    padded_normed = jnp.concatenate(
        [normed_low, jnp.zeros((sequences, 1, width), jnp.bfloat16)], axis=1
    )
    routed = jnp.take_along_axis(padded_normed, slot_token[:, :, None], axis=1).reshape(
        sequences, experts, capacity, width
    )
    expert_gating = jnp.einsum(
        "secd,edf->secf", routed, expert_gate_full, preferred_element_type=jnp.float32
    )
    expert_linear = jnp.einsum(
        "secd,edf->secf", routed, expert_up_full, preferred_element_type=jnp.float32
    )
    expert_active = (jax.nn.silu(expert_gating) * expert_linear).astype(jnp.bfloat16)
    expert_result = jnp.einsum(
        "secf,efd->secd", expert_active, expert_down_full, preferred_element_type=jnp.float32
    ).reshape(sequences, experts * capacity, width)
    picked = jnp.take_along_axis(expert_result, slot_pick[:, :, None], axis=1).reshape(
        sequences, block, top_count, width
    )
    routed_sum = jnp.sum(gates[..., None] * picked, axis=2)
    shared_gating = project(normed_low, shared_gate_full)
    shared_linear = project(normed_low, shared_up_full)
    shared_active = (jax.nn.silu(shared_gating) * shared_linear).astype(jnp.bfloat16)
    shared_result = project(shared_active, shared_down_full)
    ffn_sum = lax.psum((routed_sum + shared_result).astype(jnp.bfloat16), "tp").astype(jnp.float32)
    output = (mixed + ffn_sum).astype(jnp.bfloat16)
    grad_out = cotangent.astype(jnp.float32)
    grad_shared_active = project_back(cotangent, shared_down_full)
    grad_shared_down = weight_grad(shared_active, cotangent)
    grad_shared_gating = (grad_shared_active * shared_linear * silu_slope(shared_gating)).astype(
        jnp.bfloat16
    )
    grad_shared_linear = (grad_shared_active * jax.nn.silu(shared_gating)).astype(jnp.bfloat16)
    grad_shared_gate = weight_grad(normed_low, grad_shared_gating)
    grad_shared_up = weight_grad(normed_low, grad_shared_linear)
    grad_normed = project_back(grad_shared_gating, shared_gate_full) + project_back(
        grad_shared_linear, shared_up_full
    )
    grad_routed = (
        (gates[..., None] * grad_out[:, :, None, :])
        .reshape(sequences, block * top_count, width)
        .astype(jnp.bfloat16)
    )
    grad_gates_part = jnp.sum(grad_out[:, :, None, :] * picked, axis=-1)
    grad_pad = jnp.concatenate(
        [grad_routed, jnp.zeros((sequences, 1, width), jnp.bfloat16)], axis=1
    )
    grad_slots = jnp.take_along_axis(grad_pad, slot_owner[:, :, None], axis=1).reshape(
        sequences, experts, capacity, width
    )
    grad_expert_active = jnp.einsum(
        "secd,efd->secf", grad_slots, expert_down_full, preferred_element_type=jnp.float32
    )
    grad_expert_down = jnp.einsum(
        "secf,secd->efd", expert_active, grad_slots, preferred_element_type=jnp.float32
    )
    grad_expert_gating = (grad_expert_active * expert_linear * silu_slope(expert_gating)).astype(
        jnp.bfloat16
    )
    grad_expert_linear = (grad_expert_active * jax.nn.silu(expert_gating)).astype(jnp.bfloat16)
    grad_expert_gate = jnp.einsum(
        "secd,secf->edf", routed, grad_expert_gating, preferred_element_type=jnp.float32
    )
    grad_expert_up = jnp.einsum(
        "secd,secf->edf", routed, grad_expert_linear, preferred_element_type=jnp.float32
    )
    grad_routed_rows = (
        jnp.einsum(
            "secf,edf->secd",
            grad_expert_gating,
            expert_gate_full,
            preferred_element_type=jnp.float32,
        )
        + jnp.einsum(
            "secf,edf->secd", grad_expert_linear, expert_up_full, preferred_element_type=jnp.float32
        )
    ).reshape(sequences, experts * capacity, width)
    grad_tokens = jnp.take_along_axis(grad_routed_rows, slot_pick[:, :, None], axis=1).reshape(
        sequences, block, top_count, width
    )
    grad_normed = grad_normed + jnp.sum(grad_tokens, axis=2)
    grad_normed, grad_gates = (
        lax.psum(grad_normed.astype(jnp.bfloat16), "tp").astype(jnp.float32),
        lax.psum(grad_gates_part.astype(jnp.bfloat16), "tp").astype(jnp.float32),
    )
    grad_chosen = gates * (grad_gates - jnp.sum(gates * grad_gates, axis=-1, keepdims=True))
    route_hits = (routes[..., None] == jnp.arange(experts, dtype=jnp.int32)).astype(jnp.float32)
    grad_logits = jnp.sum(grad_chosen[..., None] * route_hits, axis=2).astype(jnp.bfloat16)
    grad_router = weight_grad(normed_low, grad_logits)
    grad_normed = grad_normed + project_back(grad_logits, router_full)
    grad_mixed_norm, grad_ffn_gain = norm_back(grad_normed, mixed, scale_ffn, ffn_scale)
    grad_mixed = grad_out + grad_mixed_norm
    grad_mixed_low = grad_mixed.astype(jnp.bfloat16)
    grad_out_weight = weight_grad(attended_low, grad_mixed_low)
    grad_attended = (
        project_back(grad_mixed_low, out_full)
        .astype(jnp.bfloat16)
        .reshape(sequences, block, heads, HD)
    )

    def attend_back(items):
        query_one, keys_one, values_one, allowed_one, log_one, grad_one = items
        scores = scores_of(query_one, keys_one, allowed_one)
        weights = jnp.exp(scores - log_one)
        grad_weights = jnp.einsum(
            "qhd,khd->hqk", grad_one, values_one, preferred_element_type=jnp.float32
        )
        grad_scores = (
            weights * (grad_weights - jnp.sum(weights * grad_weights, axis=-1, keepdims=True))
        ).astype(jnp.bfloat16)
        grad_query_one = (
            jnp.einsum("hqk,khd->qhd", grad_scores, keys_one, preferred_element_type=jnp.float32)
            * score_scale
        )
        grad_keys_one = (
            jnp.einsum("hqk,qhd->khd", grad_scores, query_one, preferred_element_type=jnp.float32)
            * score_scale
        )
        grad_values_one = jnp.einsum(
            "hqk,qhd->khd",
            weights.astype(jnp.bfloat16),
            grad_one,
            preferred_element_type=jnp.float32,
        )
        return (grad_query_one, grad_keys_one, grad_values_one)

    grad_query, grad_keys_all, grad_values_all = lax.map(
        attend_back, (query, all_keys, all_values, allowed, log_total, grad_attended)
    )
    grad_keys = grad_keys_all[:, 2 * block :]
    grad_values = grad_values_all[:, 2 * block :]
    for reach in (1, 2):
        start = (2 - reach) * block
        back_keys, back_values = (
            from_behind(
                grad_keys_all[:, start : start + block].astype(jnp.bfloat16), "ctx", -reach
            ).astype(jnp.float32),
            from_behind(
                grad_values_all[:, start : start + block].astype(jnp.bfloat16), "ctx", -reach
            ).astype(jnp.float32),
        )
        grad_keys = grad_keys + back_keys
        grad_values = grad_values + back_values
    grad_query_pre = (
        unrotate(grad_query, cosine, sine)
        .reshape(sequences, block, heads * HD)
        .astype(jnp.bfloat16)
    )
    grad_key_pre = (
        unrotate(grad_keys, cosine, sine).reshape(sequences, block, heads * HD).astype(jnp.bfloat16)
    )
    grad_value_pre = grad_values.reshape(sequences, block, heads * HD).astype(jnp.bfloat16)
    grad_query_weight = weight_grad(hidden_low, grad_query_pre)
    grad_key_weight = weight_grad(hidden_low, grad_key_pre)
    grad_value_weight = weight_grad(hidden_low, grad_value_pre)
    grad_hidden = (
        project_back(grad_query_pre, query_full)
        + project_back(grad_key_pre, key_full)
        + project_back(grad_value_pre, value_full)
    )
    grad_hidden = lax.psum(grad_hidden.astype(jnp.bfloat16), "tp").astype(jnp.float32)
    grad_inputs_norm, grad_attn_gain = norm_back(grad_hidden, inputs, scale_attn, attn_scale)
    input_grad = (grad_mixed + grad_inputs_norm).astype(jnp.bfloat16)
    (
        shard_query,
        shard_key,
        shard_value,
        shard_out,
        shard_attn_gain,
        shard_ffn_gain,
        shard_router,
        shard_shared_gate,
        shard_shared_up,
        shard_shared_down,
        shard_expert_gate,
        shard_expert_up,
        shard_expert_down,
    ) = (
        lax.psum_scatter(
            grad_query_weight.astype(jnp.bfloat16), "fsdp", scatter_dimension=0, tiled=True
        ).astype(jnp.float32),
        lax.psum_scatter(
            grad_key_weight.astype(jnp.bfloat16), "fsdp", scatter_dimension=0, tiled=True
        ).astype(jnp.float32),
        lax.psum_scatter(
            grad_value_weight.astype(jnp.bfloat16), "fsdp", scatter_dimension=0, tiled=True
        ).astype(jnp.float32),
        lax.psum_scatter(
            grad_out_weight.astype(jnp.bfloat16), "fsdp", scatter_dimension=1, tiled=True
        ).astype(jnp.float32),
        lax.psum_scatter(
            grad_attn_gain.astype(jnp.bfloat16), "fsdp", scatter_dimension=0, tiled=True
        ).astype(jnp.float32),
        lax.psum_scatter(
            grad_ffn_gain.astype(jnp.bfloat16), "fsdp", scatter_dimension=0, tiled=True
        ).astype(jnp.float32),
        lax.psum_scatter(
            grad_router.astype(jnp.bfloat16), "fsdp", scatter_dimension=0, tiled=True
        ).astype(jnp.float32),
        lax.psum_scatter(
            grad_shared_gate.astype(jnp.bfloat16), "fsdp", scatter_dimension=0, tiled=True
        ).astype(jnp.float32),
        lax.psum_scatter(
            grad_shared_up.astype(jnp.bfloat16), "fsdp", scatter_dimension=0, tiled=True
        ).astype(jnp.float32),
        lax.psum_scatter(
            grad_shared_down.astype(jnp.bfloat16), "fsdp", scatter_dimension=1, tiled=True
        ).astype(jnp.float32),
        lax.psum_scatter(
            grad_expert_gate.astype(jnp.bfloat16), "fsdp", scatter_dimension=1, tiled=True
        ).astype(jnp.float32),
        lax.psum_scatter(
            grad_expert_up.astype(jnp.bfloat16), "fsdp", scatter_dimension=1, tiled=True
        ).astype(jnp.float32),
        lax.psum_scatter(
            grad_expert_down.astype(jnp.bfloat16), "fsdp", scatter_dimension=2, tiled=True
        ).astype(jnp.float32),
    )
    summed = (
        lax.psum(shard_query.astype(jnp.bfloat16), "ctx").astype(jnp.float32),
        lax.psum(shard_key.astype(jnp.bfloat16), "ctx").astype(jnp.float32),
        lax.psum(shard_value.astype(jnp.bfloat16), "ctx").astype(jnp.float32),
        lax.psum(shard_out.astype(jnp.bfloat16), "ctx").astype(jnp.float32),
        lax.psum(shard_attn_gain.astype(jnp.bfloat16), "ctx").astype(jnp.float32),
        lax.psum(shard_ffn_gain.astype(jnp.bfloat16), "ctx").astype(jnp.float32),
        lax.psum(shard_router.astype(jnp.bfloat16), "ctx").astype(jnp.float32),
        lax.psum(shard_shared_gate.astype(jnp.bfloat16), "ctx").astype(jnp.float32),
        lax.psum(shard_shared_up.astype(jnp.bfloat16), "ctx").astype(jnp.float32),
        lax.psum(shard_shared_down.astype(jnp.bfloat16), "ctx").astype(jnp.float32),
        lax.psum(shard_expert_gate.astype(jnp.bfloat16), "ctx").astype(jnp.float32),
        lax.psum(shard_expert_up.astype(jnp.bfloat16), "ctx").astype(jnp.float32),
        lax.psum(shard_expert_down.astype(jnp.bfloat16), "ctx").astype(jnp.float32),
    )
    return (
        output,
        input_grad,
        summed[0],
        summed[1],
        summed[2],
        summed[3],
        summed[4],
        summed[5],
        summed[6],
        summed[7],
        summed[8],
        summed[9],
        summed[10],
        summed[11],
        summed[12],
    )


def solution(mesh):
    in_specs = (
        P("fsdp", "ctx", None),
        P("fsdp", None),
        P("fsdp", "ctx", None),
        P("fsdp", "tp"),
        P("fsdp", "tp"),
        P("fsdp", "tp"),
        P("tp", "fsdp"),
        P("fsdp"),
        P("fsdp"),
        P("fsdp", None),
        P("fsdp", "tp"),
        P("fsdp", "tp"),
        P("tp", "fsdp"),
        P(None, "fsdp", "tp"),
        P(None, "fsdp", "tp"),
        P(None, "tp", "fsdp"),
        P("fsdp", "ctx", None),
    )
    out_specs = (
        P("fsdp", "ctx", None),
        P("fsdp", "ctx", None),
        P("fsdp", "tp"),
        P("fsdp", "tp"),
        P("fsdp", "tp"),
        P("tp", "fsdp"),
        P("fsdp"),
        P("fsdp"),
        P("fsdp", None),
        P("fsdp", "tp"),
        P("fsdp", "tp"),
        P("tp", "fsdp"),
        P(None, "fsdp", "tp"),
        P(None, "fsdp", "tp"),
        P(None, "tp", "fsdp"),
    )
    return jax.shard_map(local, mesh=mesh, in_specs=in_specs, out_specs=out_specs, check_vma=False)
```

profile of v0, /device:TPU:0, one launch (start us, length us, event | category | flops | bytes accessed | tf_op | source)
XLA Modules:
  0.0 1432.8 jit_solution(9661507536041592855)
XLA Ops:
  11.8 8.3 all-reduce.11
  21.5 6.9 all_gather.41
  28.7 7.7 all_gather.42
  49.3 7.4 all_gather.40
  60.3 7.9 all_gather.43
  69.2 9.3 fusion.123
  78.6 9.0 fusion
  87.6 8.5 fusion.49
  102.8 5.2 all-gather
  122.0 39.6 %all-reduce.18.cloned.1.call-done = f32[1,512,768]{2,1,0:T(8,128)} async-done(((f32[1,512,768]{2,1,0:T(8,128)}), f32[1,512,768]{2,1,0:T(8,128)}) %all-reduce.18.cloned.1.call-update) | async-done | bytes 1572880 | tf_op jit(solution)/shard_map/psum | solution.py:185
  165.2 6.5 gather_fusion.2
  172.1 5.0 gather_fusion
  186.0 7.4 multiply_convert_fusion.2
  196.6 60.7 %all-gather.8.cloned.1.call-done = bf16[8,768,1024]{2,1,0:T(8,128)(2,1)} async-done(((bf16[8,192,1024]{2,1,0:T(8,128)(2,1)}), bf16[8,768,1024]{2,1,0:T(8,128)(2,1)}) %all-gather.8.cloned.1.call-update) | async-done | bytes 12582928 | tf_op jit(solution)/shard_map/all_gather | solution.py:119
  257.3 10.6 fusion.44
  267.9 73.0 %all-gather.10.cloned.1.call-done = bf16[8,768,1024]{2,1,0:T(8,128)(2,1)} async-done(((bf16[8,192,1024]{2,1,0:T(8,128)(2,1)}), bf16[8,768,1024]{2,1,0:T(8,128)(2,1)}) %all-gather.10.cloned.1.call-update) | async-done | bytes 12582928 | tf_op jit(solution)/shard_map/all_gather | solution.py:120
  341.0 6.3 fusion.43
  352.5 72.1 %all-gather.12.cloned.1.call-done = bf16[8,1024,768]{1,2,0:T(8,128)(2,1)} async-done(((bf16[8,1024,192]{1,2,0:T(8,128)(2,1)}), bf16[8,1024,768]{1,2,0:T(8,128)(2,1)}) %all-gather.12.cloned.1.call-update) | async-done | bytes 12582928 | tf_op jit(solution)/shard_map/all_gather | solution.py:121
  424.6 11.0 fusion.126
  435.7 8.3 gather_fusion.3
  448.5 4.9 psum.129
  454.1 5.6 gather_fusion.1
  459.7 14.1 fusion.7
  473.9 13.3 fusion.128
  487.2 12.4 fusion.27
  499.5 6.9 gather_fusion.4
  512.5 5.3 reduce_sum.146
  530.9 26.1 %all-reduce.20.cloned.1.call-done = bf16[1,512,768]{2,1,0:T(8,128)(2,1)} async-done(((bf16[1,512,768]{2,1,0:T(8,128)(2,1)}), bf16[1,512,768]{2,1,0:T(8,128)(2,1)}) %all-reduce.20.cloned.1.call-update) | async-done | bytes 786448 | tf_op jit(solution)/shard_map/psum | solution.py:288
  562.4 16.1 %multiply_reduce_fusion = (f32[6,512]{1,0:T(8,128)S(1)}, f32[6,512,1536]{2,1,0:T(8,128)}) fusion(f32[6,512,1536]{2,1,0:T(8,128)} %get-tuple-element.128, f32[6,512]{1,0:T(8,128)S(1)} %log_add_fusion, bf16[512,6,64]{0,2,1:T(8,128)(2,1)S(1)} %bitcast.284, bf16[1,512,6,64]{1,3,2,0:T(8,128)(2,1)S(1)} %bitcast.299, bf16[1,512,6,64]{1,3,2,0:T(8,128)(2,1)S(1)} %copy-done.58, ...), kind=kOutput, calls=%fused_computation.7 | convolution fusion | flops 621671424 | bytes 39346176 | tf_op jit(solution)/shard_map/while/body/eval_jaxpr/qhd,khd->hqk/dot_general | solution.py:310
  578.5 13.2 multiply_convert_fusion
  600.6 7.2 fusion.48
  609.9 17.5 %collective-permute-done.5 = bf16[1,512,6,64]{1,3,2,0:T(8,128)(2,1)} collective-permute-done((bf16[1,512,6,64]{1,3,2,0:T(8,128)(2,1)}, bf16[1,512,6,64]{1,3,2,0:T(8,128)(2,1)}, u32[]{:S(2)}, u32[]{:S(2)}) %collective-permute-start.5) | collective-permute-done | bytes 393248 | tf_op jit(solution)/shard_map/ppermute | solution.py:16
  630.8 9.7 fusion.124
  644.8 10.9 collective-permute-done.6
  655.7 13.0 collective-permute-done.7
  673.9 9.9 convolution_convert_fusion
  685.4 10.0 convolution_convert_fusion.2
  695.5 10.2 convolution_convert_fusion.1
  714.5 6.2 multiply_reduce_fusion.2
  720.7 5.1 fusion.45
  729.4 85.7 %reduce-scatter.32.cloned.1.call-done = bf16[8,1024,192]{1,2,0:T(8,128)(2,1)} async-done(((bf16[8,1024,768]{1,2,0:T(8,128)(2,1)}), bf16[8,1024,192]{1,2,0:T(8,128)(2,1)}) %reduce-scatter.32.cloned.1.call-update) | async-done | bytes 3145744 | tf_op jit(solution)/shard_map/reduce_scatter | solution.py:420
  815.1 101.6 %reduce-scatter.28.cloned.1.call-done = bf16[8,192,1024]{2,1,0:T(8,128)(2,1)} async-done(((bf16[8,768,1024]{2,1,0:T(8,128)(2,1)}), bf16[8,192,1024]{2,1,0:T(8,128)(2,1)}) %reduce-scatter.28.cloned.1.call-update) | async-done | bytes 3145744 | tf_op jit(solution)/shard_map/reduce_scatter | solution.py:414
  916.7 101.6 %reduce-scatter.30.cloned.1.call-done = bf16[8,192,1024]{2,1,0:T(8,128)(2,1)} async-done(((bf16[8,768,1024]{2,1,0:T(8,128)(2,1)}), bf16[8,192,1024]{2,1,0:T(8,128)(2,1)}) %reduce-scatter.30.cloned.1.call-update) | async-done | bytes 3145744 | tf_op jit(solution)/shard_map/reduce_scatter | solution.py:417
  1019.0 22.0 %reduce-scatter.34.cloned.1.call-done = bf16[192,8]{1,0:T(8,128)(2,1)} async-done(((bf16[768,8]{1,0:T(8,128)(2,1)}), bf16[192,8]{1,0:T(8,128)(2,1)}) %reduce-scatter.34.cloned.1.call-update) | async-done | bytes 3088
  1044.2 6.1 all-reduce.10
  1050.4 12.8 all-reduce.8
  1068.6 338.1 %all-reduce.22.cloned.1.call-done = (bf16[192,384]{1,0:T(8,128)(2,1)}, bf16[192,384]{1,0:T(8,128)(2,1)}, bf16[192,384]{1,0:T(8,128)(2,1)}, bf16[384,192]{0,1:T(8...) async-done(((bf16[192,384]{1,0:T(8,128)(2,1)}, ...) | async-done | bytes 11206672 | tf_op jit(solution)/shard_map/psum | solution.py:425
  1406.8 5.5 convert_element_type.428
  (411 shorter events, 152.3 us)
Async XLA Ops:
  8.0 153.6 %all-reduce.18.cloned.1.call-start = ((), (), s32[]{:S(2)}) async-start(), calls=%async_computation.11 | async-start | bytes 3145728 | tf_op jit(solution)/shard_map/psum | solution.py:185
  20.2 36.6 %copy-start.85 = (f32[768]{0:T(1024)}, f32[768]{0:T(1024)S(1)}, u32[]{:S(2)}) copy-start(f32[768]{0:T(1024)S(1)} %convert_element_type.359) | copy-start | bytes 9220
  21.5 35.2 %copy-start.91 = (f32[512]{0:T(512)}, f32[512]{0:T(512)S(1)}, u32[]{:S(2)}) copy-start(f32[512]{0:T(512)S(1)} %add_rsqrt_fusion.1) | copy-start | bytes 6148
  39.7 29.5 %copy-start.34 = (bf16[1,512,6,32]{1,3,2,0:T(8,128)(2,1)}, bf16[1,512,6,32]{1,3,2,0:T(8,128)(2,1)S(1)}, u32[]{:S(2)}) copy-start(bf16[1,512,6,32]{1,3,2,0:T(8,128)(2,1)S(1)} %get-tuple-element.115) | copy-start | bytes 589828
  39.7 29.5 %copy-start.36 = (bf16[1,512,6,32]{1,3,2,0:T(8,128)(2,1)}, bf16[1,512,6,32]{1,3,2,0:T(8,128)(2,1)S(1)}, u32[]{:S(2)}) copy-start(bf16[1,512,6,32]{1,3,2,0:T(8,128)(2,1)S(1)} %get-tuple-element.116) | copy-start | bytes 589828
  39.7 29.5 %copy-start.44 = (bf16[512,6,32]{0,2,1:T(8,128)(2,1)}, bf16[512,6,32]{0,2,1:T(8,128)(2,1)S(1)}, u32[]{:S(2)}) copy-start(bf16[512,6,32]{0,2,1:T(8,128)(2,1)S(1)} %get-tuple-element.121) | copy-start | bytes 589828
  39.8 29.5 %copy-start.46 = (bf16[512,6,32]{0,2,1:T(8,128)(2,1)}, bf16[512,6,32]{0,2,1:T(8,128)(2,1)S(1)}, u32[]{:S(2)}) copy-start(bf16[512,6,32]{0,2,1:T(8,128)(2,1)S(1)} %get-tuple-element.122) | copy-start | bytes 589828
  40.6 28.6 %collective-permute-start.2 = (bf16[1,512,6,64]{1,3,2,0:T(8,128)(2,1)}, bf16[1,512,6,64]{1,3,2,0:T(8,128)(2,1)S(1)}, u32[]{:S(2)}, u32[]{:S(2)}) collective-permute-start(bf16[1,512,6,64]{1,3,2,0:T(8,128)(2,1)} %pad_maximum_fusion.1), channel_id=1, source_target_pairs={{0,4},{2,6},{1,5},{3,7},{8,12},{10,14},{9,13},{11,15},{16,20},{18,... | collective-permute-start | bytes 1179656 | tf_op jit(solution)/shard_map/ppermute | solution.py:16
  45.1 24.1 %collective-permute-start.3 = (bf16[1,512,6,64]{1,3,2,0:T(8,128)(2,1)}, bf16[1,512,6,64]{1,3,2,0:T(8,128)(2,1)}, u32[]{:S(2)}, u32[]{:S(2)}) collective-permute-start(bf16[1,512,6,64]{1,3,2,0:T(8,128)(2,1)} %pad_maximum_fusion.1), channel_id=1, source_target_pairs={{0,2},{2,4},{4,6},{1,3},{3,5},{5,7},{8,10},{10,12},{12,14},{9,11},... | collective-permute-start | bytes 1179656 | tf_op jit(solution)/shard_map/ppermute | solution.py:16
  57.6 30.1 %copy-start.53 = (bf16[512,384]{0,1:T(8,128)(2,1)}, bf16[512,384]{0,1:T(8,128)(2,1)S(1)}, u32[]{:S(2)}) copy-start(bf16[512,384]{0,1:T(8,128)(2,1)S(1)} %convolution_convert_fusion.11) | copy-start | bytes 1179652
  57.6 30.0 %collective-permute-start = (bf16[1,512,6,64]{1,3,2,0:T(8,128)(2,1)S(1)}, bf16[1,512,6,64]{1,3,2,0:T(8,128)(2,1)S(1)}, u32[]{:S(2)}, u32[]{:S(2)}) collective-permute-start(bf16[1,512,6,64]{1,3,2,0:T(8,128)(2,1)S(1)} %bitcast.296), channel_id=1, source_target_pairs={{0,4},{2,6},{1,5},{3,7},{8,12},{10,14},{9,13},{11,15},{16,20},{18,... | collective-permute-start | bytes 1179656 | tf_op jit(solution)/shard_map/ppermute | solution.py:16
  58.9 28.7 %collective-permute-start.1 = (bf16[1,512,6,64]{1,3,2,0:T(8,128)(2,1)S(1)}, bf16[1,512,6,64]{1,3,2,0:T(8,128)(2,1)S(1)}, u32[]{:S(2)}, u32[]{:S(2)}) collective-permute-start(bf16[1,512,6,64]{1,3,2,0:T(8,128)(2,1)S(1)} %bitcast.297), channel_id=1, source_target_pairs={{0,2},{2,4},{4,6},{1,3},{3,5},{5,7},{8,10},{10,12},{12,14},{9,11},... | collective-permute-start | bytes 1179656 | tf_op jit(solution)/shard_map/ppermute | solution.py:16
  98.7 78.5 %all-gather.16.cloned.1.call-start = ((), (), s32[]{:S(2)}) async-start(), calls=%async_computation.16 | async-start | bytes 1966080 | tf_op jit(solution)/shard_map/all_gather | solution.py:117
  99.3 82.7 %all-gather.14.cloned.1.call-start = ((), (), s32[]{:S(2)}) async-start(), calls=%async_computation.15 | async-start | bytes 1966080 | tf_op jit(solution)/shard_map/all_gather | solution.py:116
  99.9 86.1 %all-gather.18.cloned.1.call-start = ((), (), s32[]{:S(2)}) async-start(), calls=%async_computation.17 | async-start | bytes 1966080 | tf_op jit(solution)/shard_map/all_gather | solution.py:118
  100.5 156.9 %all-gather.8.cloned.1.call-start = ((), (), s32[]{:S(2)}) async-start(), calls=%async_computation.12 | async-start | bytes 15728640 | tf_op jit(solution)/shard_map/all_gather | solution.py:119
  101.2 239.8 %all-gather.10.cloned.1.call-start = ((), (), s32[]{:S(2)}) async-start(), calls=%async_computation.13 | async-start | bytes 15728640 | tf_op jit(solution)/shard_map/all_gather | solution.py:120
  102.0 322.6 %all-gather.12.cloned.1.call-start = ((), (), s32[]{:S(2)}) async-start(), calls=%async_computation.14 | async-start | bytes 15728640 | tf_op jit(solution)/shard_map/all_gather | solution.py:121
  102.8 454.2 %all-reduce.20.cloned.1.call-start = ((), (), s32[]{:S(2)}) async-start(), calls=%async_computation.18 | async-start | bytes 1572864 | tf_op jit(solution)/shard_map/psum | solution.py:288
  102.8 60.7 %copy-start.83 = (f32[768]{0:T(1024)}, f32[768]{0:T(1024)S(1)}, u32[]{:S(2)}) copy-start(f32[768]{0:T(1024)S(1)} %convert_element_type.367) | copy-start | bytes 9220
  108.1 56.7 %copy-start.72 = (bf16[768,8]{0,1:T(8,128)(2,1)}, bf16[768,8]{0,1:T(8,128)(2,1)S(1)}, u32[]{:S(2)}) copy-start(bf16[768,8]{0,1:T(8,128)(2,1)S(1)} %reshape.1196) | copy-start | bytes 36868
  122.0 219.0 %copy-start.63 = (pred[8,192]{1,0:T(8,128)(4,1)}, pred[8,192]{1,0:T(8,128)(4,1)S(1)}, u32[]{:S(2)}) copy-start(pred[8,192]{1,0:T(8,128)(4,1)S(1)} %compare_and_fusion.1) | copy-start | bytes 4612
  122.0 337.7 %copy-start.96 = (pred[8,192]{1,0:T(8,128)(4,1)}, pred[8,192]{1,0:T(8,128)(4,1)S(1)}, u32[]{:S(2)}) copy-start(pred[8,192]{1,0:T(8,128)(4,1)S(1)} %compare_and_fusion) | copy-start | bytes 4612
  177.1 163.9 %copy-start.1 = (bf16[1536,768]{1,0:T(8,128)(2,1)}, bf16[1536,768]{1,0:T(8,128)(2,1)S(1)}, u32[]{:S(2)}) copy-start(bf16[1536,768]{1,0:T(8,128)(2,1)S(1)} %gather_fusion) | copy-start | bytes 7077892
  352.5 83.1 %copy-start.8 = (bf16[8,192,1024]{2,1,0:T(8,128)(2,1)}, bf16[8,192,1024]{2,1,0:T(8,128)(2,1)S(1)}, u32[]{:S(2)}) copy-start(bf16[8,192,1024]{2,1,0:T(8,128)(2,1)S(1)} %fusion.15) | copy-start | bytes 9437188
  453.4 77.4 %copy-start.81 = (f32[1,512,2]{1,2,0:T(2,128)}, f32[1,512,2]{1,2,0:T(2,128)S(1)}, u32[]{:S(2)}) copy-start(f32[1,512,2]{1,2,0:T(2,128)S(1)} %get-tuple-element.93) | copy-start | bytes 12292
  522.5 206.7 %reduce-scatter.22.cloned.1.call-start = ((), (), s32[]{:S(2)}) async-start(), calls=%async_computation.23 | async-start | bytes 1966080 | tf_op jit(solution)/shard_map/reduce_scatter | solution.py:405
  524.8 204.5 %reduce-scatter.24.cloned.1.call-start = ((), (), s32[]{:S(2)}) async-start(), calls=%async_computation.24 | async-start | bytes 1966080 | tf_op jit(solution)/shard_map/reduce_scatter | solution.py:408
  527.0 202.3 %reduce-scatter.26.cloned.1.call-start = ((), (), s32[]{:S(2)}) async-start(), calls=%async_computation.25 | async-start | bytes 1966080 | tf_op jit(solution)/shard_map/reduce_scatter | solution.py:411
  527.1 29.9 %copy-start.73 = (bf16[768,8]{0,1:T(8,128)(2,1)S(1)}, bf16[768,8]{0,1:T(8,128)(2,1)}, u32[]{:S(2)}) copy-start(bf16[768,8]{0,1:T(8,128)(2,1)} %copy-done.72) | copy-start | bytes 36868
  527.1 29.9 %copy-start.84 = (f32[768]{0:T(1024)S(1)}, f32[768]{0:T(1024)}, u32[]{:S(2)}) copy-start(f32[768]{0:T(1024)} %copy-done.83) | copy-start | bytes 9220
  527.1 29.9 %copy-start.90 = (f32[512]{0:T(512)S(1)}, f32[512]{0:T(512)}, u32[]{:S(2)}) copy-start(f32[512]{0:T(512)} %copy-done.89) | copy-start | bytes 6148
  530.8 198.5 %reduce-scatter.20.cloned.1.call-start = ((), (), s32[]{:S(2)}) async-start(), calls=%async_computation.22 | async-start | bytes 737280 | tf_op jit(solution)/shard_map/reduce_scatter | solution.py:393
  560.6 38.4 %copy-start.11 = (f32[1,512,768]{2,1,0:T(8,128)}, f32[1,512,768]{2,1,0:T(8,128)S(1)}, u32[]{:S(2)}) copy-start(f32[1,512,768]{2,1,0:T(8,128)S(1)} %convert_add_fusion.1) | copy-start | bytes 4718596
  596.4 13.5 collective-permute-start.4
  597.7 29.7 %collective-permute-start.5 = (bf16[1,512,6,64]{1,3,2,0:T(8,128)(2,1)}, bf16[1,512,6,64]{1,3,2,0:T(8,128)(2,1)}, u32[]{:S(2)}, u32[]{:S(2)}) collective-permute-start(bf16[1,512,6,64]{1,3,2,0:T(8,128)(2,1)} %get-tuple-element.108), channel_id=1, source_target_pairs={{4,0},{6,2},{5,1},{7,3},{12,8},{14,10},{13,9},{15,11},{20,16},{22,... | collective-permute-start | bytes 1179656 | tf_op jit(solution)/shard_map/ppermute | solution.py:16
  600.5 128.9 %reduce-scatter.16.cloned.1.call-start = ((), (), s32[]{:S(2)}) async-start(), calls=%async_computation.20 | async-start | bytes 737280 | tf_op jit(solution)/shard_map/reduce_scatter | solution.py:387
  630.7 98.6 %reduce-scatter.14.cloned.1.call-start = ((), (), s32[]{:S(2)}) async-start(), calls=%async_computation.19 | async-start | bytes 737280 | tf_op jit(solution)/shard_map/reduce_scatter | solution.py:384
  642.1 87.3 %reduce-scatter.18.cloned.1.call-start = ((), (), s32[]{:S(2)}) async-start(), calls=%async_computation.21 | async-start | bytes 737280 | tf_op jit(solution)/shard_map/reduce_scatter | solution.py:390
  642.2 13.5 collective-permute-start.6
  643.5 25.1 %collective-permute-start.7 = (bf16[1,512,6,64]{1,3,2,0:T(8,128)(2,1)S(1)}, bf16[1,512,6,64]{1,3,2,0:T(8,128)(2,1)S(1)}, u32[]{:S(2)}, u32[]{:S(2)}) collective-permute-start(bf16[1,512,6,64]{1,3,2,0:T(8,128)(2,1)S(1)} %get-tuple-element.110), channel_id=1, source_target_pairs={{4,0},{6,2},{5,1},{7,3},{12,8},{14,10},{13,9},{15,11},{20,16},{22,... | collective-permute-start | bytes 1179656 | tf_op jit(solution)/shard_map/ppermute | solution.py:16
  673.6 141.5 %reduce-scatter.32.cloned.1.call-start = ((), (), s32[]{:S(2)}) async-start(), calls=%async_computation.28 | async-start | bytes 15728640 | tf_op jit(solution)/shard_map/reduce_scatter | solution.py:420
  683.8 232.9 %reduce-scatter.28.cloned.1.call-start = ((), (), s32[]{:S(2)}) async-start(), calls=%async_computation.26 | async-start | bytes 15728640 | tf_op jit(solution)/shard_map/reduce_scatter | solution.py:414
  695.5 322.7 %reduce-scatter.30.cloned.1.call-start = ((), (), s32[]{:S(2)}) async-start(), calls=%async_computation.27 | async-start | bytes 15728640 | tf_op jit(solution)/shard_map/reduce_scatter | solution.py:417
  705.7 335.3 %reduce-scatter.34.cloned.1.call-start = ((), (), s32[]{:S(2)}) async-start(), calls=%async_computation.29 | async-start | bytes 245760
  720.7 321.2 %all-reduce.24.cloned.1.call-start = ((), (), s32[]{:S(2)}) async-start(), calls=%async_computation.31 | async-start | bytes 3145728 | tf_op jit(solution)/shard_map/psum | solution.py:230
  729.2 677.6 %all-reduce.22.cloned.1.call-start = ((), (), s32[]{:S(2)}) async-start(), calls=%async_computation.30 | async-start | bytes 22413312 | tf_op jit(solution)/shard_map/psum | solution.py:425
  1018.2 46.7 %copy-start.5 = (f32[1,512,768]{2,1,0:T(8,128)S(1)}, f32[1,512,768]{2,1,0:T(8,128)}, u32[]{:S(2)}) copy-start(f32[1,512,768]{2,1,0:T(8,128)} %copy-done.3) | copy-start | bytes 4718596
  (87 other events, 725.8 us)
Sparse Core Ops, SparseCore 0:
  98.8 62.6 all-reduce.17
  522.6 34.3 all-reduce.19
  729.3 49.0 all-reduce.23
  1018.4 388.3 all-reduce.21
Sparse Core Ops, SparseCore 1:
  100.8 30.7 all-gather.15
  133.1 19.5 all-gather.13
  154.2 19.5 all-gather.17
  175.4 81.9 all-gather.7
  259.0 81.9 all-gather.9
  342.6 81.9 all-gather.11
  525.7 28.1 reduce-scatter.21
  556.3 28.1 reduce-scatter.23
  586.9 28.1 reduce-scatter.25
  617.6 21.9 reduce-scatter.19
  642.0 22.0 reduce-scatter.15
  667.1 22.0 reduce-scatter.13
  691.5 22.0 reduce-scatter.17
  716.1 98.9 reduce-scatter.31
  817.7 98.9 reduce-scatter.27
  919.3 98.9 reduce-scatter.29
  1021.3 19.7 reduce-scatter.33
where the time goes:
time: 1440 us; the launch traced here: 1430 us
  waiting for transfers between devices  968 us (67%)
  matrix products  205 us (14%)
  other arithmetic  80.5 us (6%)
  local copies, waits for them, and re-layouts  75 us (5%)
  blocking collectives  67.1 us (5%)
  between operations  19.2 us (1%)
  starting transfers between devices  17.9 us (1%)
    psum x1, waiting for transfers between devices, local(): lax.psum(shard_query.astype(jnp.bfloat16), 'ctx').astype(jnp.float32)  338 us
    reduce_scatter x1, waiting for transfers between devices, local(): lax.psum_scatter(grad_expert_gate.astype(jnp.bfloat16), 'fsdp', scatter_d...  102 us
    reduce_scatter x1, waiting for transfers between devices, local(): lax.psum_scatter(grad_expert_up.astype(jnp.bfloat16), 'fsdp', scatter_dim...  102 us
    reduce_scatter x1, waiting for transfers between devices, local(): lax.psum_scatter(grad_expert_down.astype(jnp.bfloat16), 'fsdp', scatter_d...  85.7 us
    all_gather x1, waiting for transfers between devices, local(): lax.all_gather(expert_up, 'fsdp', axis=1, tiled=True)  73 us
    all_gather x1, waiting for transfers between devices, local(): lax.all_gather(expert_down, 'fsdp', axis=2, tiled=True)  72.1 us
    all_gather x1, waiting for transfers between devices, local(): lax.all_gather(expert_gate, 'fsdp', axis=1, tiled=True)  60.7 us
    ppermute x8, waiting for transfers between devices, from_behind(): return lax.ppermute(block, axis, route)  43.5 us
  transfers between devices with their start and end apart: 29, of which 14 were waited for; matrix products, arithmetic and copies ran while one was open for 15% of the time, Pallas kernels for 0%

commit v1 on v0

v1 whole, which is shorter than its diff:
```python
import functools

import jax
import jax.numpy as jnp
from jax import lax
from jax.experimental import pallas as pl
from jax.experimental.pallas import tpu as pltpu
from jax.sharding import PartitionSpec as P

HD = 64
WINDOW = 1024
EPS = 1e-06
F32 = jnp.float32
BF16 = jnp.bfloat16
VMEM_BYTES = 56 * 1024 * 1024


def dot(left, right):
    return lax.dot_general(left, right, (((1,), (0,)), ((), ())), preferred_element_type=F32)


def dot_nt(left, right):
    return lax.dot_general(left, right, (((1,), (1,)), ((), ())), preferred_element_type=F32)


def dot_tn(left, right):
    return lax.dot_general(left, right, (((0,), (0,)), ((), ())), preferred_element_type=F32)


def core_swap(block):
    size = lax.axis_size("fsdp")
    return lax.ppermute(block, "fsdp", [(i, i ^ 1) for i in range(size)])


def pair_shift(block, distance):
    size = lax.axis_size("fsdp")
    pairs = size // 2
    route = [(i, ((i // 2 + distance) % pairs) * 2 + i % 2) for i in range(size)]
    return lax.ppermute(block, "fsdp", route)


def tp_shift(block, distance):
    size = lax.axis_size("tp")
    return lax.ppermute(block, "tp", [(i, (i + distance) % size) for i in range(size)])


def ctx_shift(block, distance):
    size = lax.axis_size("ctx")
    return lax.ppermute(block, "ctx", [(i, (i + distance) % size) for i in range(size)])


def ctx_open(block, distance):
    size = lax.axis_size("ctx")
    route = [(i, i + distance) for i in range(size) if 0 <= i + distance < size]
    return lax.ppermute(block, "ctx", route)


def pick(stack, index):
    return lax.dynamic_index_in_dim(stack, index, 0, keepdims=False)


def place(pieces, me):
    count = len(pieces)
    if count == 1:
        return pieces[0][None]
    if count == 2:
        first, second = pieces
        return jnp.where(me == 0, jnp.stack([first, second]), jnp.stack([second, first]))
    result = jnp.zeros((count,) + pieces[0].shape, pieces[0].dtype)
    for d, piece in enumerate(pieces):
        result = lax.dynamic_update_index_in_dim(result, piece, (me - d) % count, 0)
    return result


def all_sum(block, axis):
    size = lax.axis_size(axis)
    reach = 1
    while reach < size:
        other = lax.ppermute(block, axis, [(i, i ^ reach) for i in range(size)])
        block = block + other
        reach *= 2
    return block


def whole(shape):
    return pl.BlockSpec(shape, lambda *_: (0,) * len(shape))


def params():
    return pltpu.CompilerParams(vmem_limit_bytes=VMEM_BYTES)


def swap_halves(values):
    width = values.shape[-1]
    lane = lax.broadcasted_iota(jnp.int32, values.shape, 1)
    up = pltpu.roll(values, width - HD // 2, 1)
    down = pltpu.roll(values, HD // 2, 1)
    return jnp.where(lane % HD < HD // 2, up, down)


def widen(table, width):
    copies = -(-width // table.shape[1])
    return jnp.concatenate([table] * copies, axis=1)[:, :width]


def project_kernel(with_query, tok_ref, gain_ref, w_ref, cos_ref, sin_ref, hid_ref, k_ref, v_ref, *q_ref):
    inputs = tok_ref[...].astype(F32)
    scale = lax.rsqrt(jnp.mean(inputs * inputs, axis=-1, keepdims=True) + EPS)
    hidden = (inputs * scale * gain_ref[...]).astype(BF16)
    hid_ref[...] = hidden
    width = k_ref.shape[1]
    cosine = widen(cos_ref[...], width)
    sine = widen(sin_ref[...], width)
    keys = dot(hidden, w_ref[:, :width])
    k_ref[...] = (keys * cosine + swap_halves(keys) * sine).astype(BF16)
    v_ref[...] = dot(hidden, w_ref[:, width : 2 * width]).astype(BF16)
    if with_query:
        query = dot(hidden, w_ref[:, 2 * width : 3 * width])
        turned = (query * cosine + swap_halves(query) * sine).astype(BF16)
        q_ref[0][...] = turned * jnp.asarray(HD**-0.5, BF16)


def project(tokens, gain, weights, cosine, sine, width, with_query):
    rows, features = tokens.shape
    row = jax.ShapeDtypeStruct((rows, width), BF16)
    outs = [jax.ShapeDtypeStruct((rows, features), BF16), row, row] + [row] * with_query
    return pl.pallas_call(
        functools.partial(project_kernel, with_query),
        out_shape=outs,
        compiler_params=params(),
    )(tokens, gain, weights, cosine, sine)


def mask_bias(kseg, qseg, keys, queries):
    key = lax.broadcasted_iota(jnp.int32, (keys, queries), 0)
    query = lax.broadcasted_iota(jnp.int32, (keys, queries), 1)
    allowed = (key > query) & (key <= query + WINDOW) & (kseg == qseg)
    return jnp.where(allowed, 0.0, -1e30).astype(F32)


def head_only(values, head):
    lane = lax.broadcasted_iota(jnp.int32, values.shape, 1)
    return jnp.where(lane // HD == head, values, jnp.zeros_like(values))


def attend_kernel(tile, q_ref, k_ref, v_ref, kseg_ref, qseg_ref, out_ref, lse_ref, bias_ref):
    rows = q_ref.shape[0]
    span = WINDOW + tile
    tiles = rows // tile

    @pl.when(pl.program_id(0) == 0)
    def _():
        for j in range(tiles):
            bias_ref[j] = mask_bias(
                kseg_ref[pl.ds(j * tile, span), :], qseg_ref[:, pl.ds(j * tile, tile)], span, tile
            )

    keys = k_ref[...]
    values_t = v_ref[...].T
    for j in range(tiles):
        start = j * tile
        query = q_ref[pl.ds(start, tile), :]
        parts = []
        for head in range(2):
            scores = dot_nt(keys[start : start + span], head_only(query, head)) + bias_ref[j]
            top = jnp.max(scores, axis=0, keepdims=True)
            expo = jnp.exp(scores - top)
            total = jnp.sum(expo, axis=0, keepdims=True)
            part = dot(
                values_t[head * HD : (head + 1) * HD, start : start + span], expo.astype(BF16)
            )
            parts.append(part / total)
            lse_ref[0, pl.ds(head, 1), pl.ds(start, tile)] = top + jnp.log(total)
        out_ref[pl.ds(start, tile), :] = jnp.concatenate(parts, axis=0).T.astype(BF16)


def attend(query, keys, values, kseg, qseg):
    rows, width = query.shape
    span = keys.shape[0]
    tile = min(256, rows)
    pairs = -(-width // (2 * HD))
    columns = lambda count: pl.BlockSpec((count, 2 * HD), lambda i: (0, i))
    return pl.pallas_call(
        functools.partial(attend_kernel, tile),
        grid=(pairs,),
        in_specs=[columns(rows), columns(span), columns(span), whole((span, 1)), whole((1, rows))],
        out_specs=[columns(rows), pl.BlockSpec((1, 2, rows), lambda i: (i, 0, 0))],
        out_shape=[
            jax.ShapeDtypeStruct((rows, width), BF16),
            jax.ShapeDtypeStruct((pairs, 2, rows), F32),
        ],
        scratch_shapes=[pltpu.VMEM((rows // tile, WINDOW + tile, tile), F32)],
        compiler_params=params(),
    )(query, keys, values, kseg, qseg)


def attend_back_kernel(
    tile, q_ref, k_ref, v_ref, g_ref, lse_ref, kseg_ref, qseg_ref, cos_ref, sin_ref,
    dq_ref, dk_ref, dv_ref, bias_ref, dk_acc, dv_acc,
):
    rows = q_ref.shape[0]
    span = WINDOW + tile
    tiles = rows // tile
    total_keys = k_ref.shape[0]

    @pl.when(pl.program_id(0) == 0)
    def _():
        for j in range(tiles):
            bias_ref[j] = mask_bias(
                kseg_ref[pl.ds(j * tile, span), :], qseg_ref[:, pl.ds(j * tile, tile)], span, tile
            )

    keys = k_ref[...]
    values = v_ref[...]
    keys_t = keys.T
    dk_acc[...] = jnp.zeros_like(dk_acc)
    dv_acc[...] = jnp.zeros_like(dv_acc)
    cosine = cos_ref[...]
    sine = sin_ref[...]
    lead = total_keys - rows
    for j in range(tiles):
        start = j * tile
        query = q_ref[pl.ds(start, tile), :]
        grad = g_ref[pl.ds(start, tile), :]
        parts = []
        for head in range(2):
            query_one = head_only(query, head)
            grad_one = head_only(grad, head)
            scores = dot_nt(keys[start : start + span], query_one) + bias_ref[j]
            probs = jnp.exp(scores - lse_ref[0, pl.ds(head, 1), pl.ds(start, tile)])
            grad_probs = dot_nt(values[start : start + span], grad_one)
            delta = jnp.sum(probs * grad_probs, axis=0, keepdims=True)
            grad_scores = (probs * (grad_probs - delta)).astype(BF16)
            dv_acc[pl.ds(start, span), :] += dot(probs.astype(BF16), grad_one)
            dk_acc[pl.ds(start, span), :] += dot(grad_scores, query_one)
            parts.append(
                dot(keys_t[head * HD : (head + 1) * HD, start : start + span], grad_scores)
            )
        dq = jnp.concatenate(parts, axis=0).T * HD**-0.5
        places = pl.ds(lead + start, tile)
        dq_ref[pl.ds(start, tile), :] = (
            dq * cos_ref[places, :] - swap_halves(dq) * sin_ref[places, :]
        ).astype(BF16)
    dk = dk_acc[...]
    dk_ref[...] = (dk * cosine - swap_halves(dk) * sine).astype(BF16)
    dv_ref[...] = dv_acc[...].astype(BF16)


def attend_back(query, keys, values, grad, lse, kseg, qseg, cosine, sine):
    rows, width = query.shape
    span = keys.shape[0]
    tile = min(256, rows)
    pairs = -(-width // (2 * HD))
    columns = lambda count: pl.BlockSpec((count, 2 * HD), lambda i: (0, i))
    return pl.pallas_call(
        functools.partial(attend_back_kernel, tile),
        grid=(pairs,),
        in_specs=[
            columns(rows), columns(span), columns(span), columns(rows),
            pl.BlockSpec((1, 2, rows), lambda i: (i, 0, 0)),
            whole((span, 1)), whole((1, rows)), whole((span, 2 * HD)), whole((span, 2 * HD)),
        ],
        out_specs=[columns(rows), columns(span), columns(span)],
        out_shape=[
            jax.ShapeDtypeStruct((rows, width), BF16),
            jax.ShapeDtypeStruct((span, width), BF16),
            jax.ShapeDtypeStruct((span, width), BF16),
        ],
        scratch_shapes=[
            pltpu.VMEM((rows // tile, WINDOW + tile, tile), F32),
            pltpu.VMEM((span, 2 * HD), F32),
            pltpu.VMEM((span, 2 * HD), F32),
        ],
        compiler_params=params(),
    )(query, keys, values, grad, lse, kseg, qseg, cosine, sine)


def expert_kernel(
    capacity, parts, n_saved, e_ref, xo_ref, xp_ref, co_ref, cp_ref, to_ref, tp_ref,
    wgu_ref, wd_ref, sw_ref, rt_ref, *refs,
):
    out_ref, dx_ref, sx_ref, sr_ref, sh_ref, sa_ref, sb_ref, ssx_ref, ssh_ref, ssa_ref, ssb_ref = refs[n_saved:]
    e = e_ref[0]
    block, width = xo_ref.shape
    hidden = wd_ref.shape[1]
    units = sw_ref.shape[1] // 3
    experts = to_ref.shape[0]
    tok = block // parts
    xs = (xo_ref[...], xp_ref[...])
    cs = (co_ref[...], cp_ref[...])
    tables = (to_ref[...], tp_ref[...])
    row = lax.broadcasted_iota(jnp.int32, (experts, block), 0)
    slot = lax.broadcasted_iota(jnp.int32, (capacity, block), 0).astype(F32)
    hits, routed, cots, gate_slots = [], [], [], []
    for one, cot, table in zip(xs, cs, tables):
        logits = dot_nt(rt_ref[...], one)[:experts]
        named = table >= 0.0
        top = jnp.max(jnp.where(named, logits, -1e30), axis=0, keepdims=True)
        expo = jnp.where(named, jnp.exp(logits - top), 0.0)
        gates = expo / jnp.sum(expo, axis=0, keepdims=True)
        mine = row == e
        gate = jnp.sum(jnp.where(mine, gates, 0.0), axis=0, keepdims=True)
        position = jnp.sum(jnp.where(mine, table, 0.0), axis=0, keepdims=True)
        hit = slot == position
        spread = jnp.where(hit, 1.0, 0.0).astype(BF16)
        hits.append((hit, spread))
        routed.append(dot(spread, one).astype(BF16))
        cots.append(dot(spread, cot))
        gate_slots.append(jnp.sum(jnp.where(hit, gate, 0.0), axis=1, keepdims=True))
    routed = jnp.concatenate(routed, axis=0)
    cots = jnp.concatenate(cots, axis=0)
    gate_slots = jnp.concatenate(gate_slots, axis=0)
    grads = (gate_slots * cots).astype(BF16)
    share = sx_ref.shape[3]
    for q in range(sx_ref.shape[1]):
        sx_ref[0, q] = routed[:, q * share : (q + 1) * share]
        sr_ref[0, q] = grads[:, q * share : (q + 1) * share]
    both = dot(routed, wgu_ref[...])
    gating, linear = both[:, :hidden], both[:, hidden:]
    sigma = jax.nn.sigmoid(gating)
    silu = gating * sigma
    active = (silu * linear).astype(BF16)
    sh_ref[0] = active
    result = dot_nt(active, wd_ref[...])
    grad_active = dot(grads, wd_ref[...])
    grad_gating = (grad_active * linear * (sigma * (1.0 + gating * (1.0 - sigma)))).astype(BF16)
    grad_linear = (grad_active * silu).astype(BF16)
    sa_ref[0] = grad_gating
    sb_ref[0] = grad_linear
    grad_rows = dot_nt(grad_gating, wgu_ref[:, :hidden]) + dot_nt(grad_linear, wgu_ref[:, hidden:])
    grad_gates = jnp.sum(result * cots, axis=1, keepdims=True)
    weighted = jnp.concatenate([(gate_slots * result).astype(BF16), grad_rows.astype(BF16)], axis=1)

    shared = dot(xs[0], sw_ref[:, : 2 * units])
    gating, linear = shared[:, :units], shared[:, units:]
    sigma = jax.nn.sigmoid(gating)
    silu = gating * sigma
    active = (silu * linear).astype(BF16)
    grad_active = dot(cs[0], sw_ref[:, 2 * units :])
    grad_gating = (grad_active * linear * (sigma * (1.0 + gating * (1.0 - sigma)))).astype(BF16)
    grad_linear = (grad_active * silu).astype(BF16)
    ssx_ref[0] = xs[0]
    ssh_ref[0] = active
    ssa_ref[0] = grad_gating
    ssb_ref[0] = grad_linear
    shared_out = dot_nt(active, sw_ref[:, 2 * units :])
    shared_dx = dot_nt(grad_gating, sw_ref[:, :units]) + dot_nt(grad_linear, sw_ref[:, units : 2 * units])

    line = lax.broadcasted_iota(jnp.int32, (16, width), 0)
    for s in range(2):
        hit, spread = hits[s]
        rows = slice(s * capacity, (s + 1) * capacity)
        back = dot_tn(spread, weighted[rows])
        out, dx = back[:, :width], back[:, width:]
        gate_row = jnp.sum(jnp.where(hit, grad_gates[rows], 0.0), axis=0, keepdims=True)
        if s == 0:
            out = out + shared_out
            dx = dx + shared_dx
        for j in range(parts):
            piece = slice(j * tok, (j + 1) * tok)
            out_ref[s, j] = out[piece].astype(BF16)
            dx_ref[s, j, :tok] = dx[piece].astype(BF16)
            spare = jnp.zeros((1, width - tok), F32)
            padded = jnp.concatenate([gate_row[:, piece], spare], axis=1)
            dx_ref[s, j, tok:] = jnp.where(line == e, padded, 0.0).astype(BF16)


def expert_step(step, steps, capacity, pairs, parts, e, xs, cs, tables, wgu, wd, sw, router_t, saved):
    block, width = xs[0].shape
    hidden = wd.shape[1]
    units = sw.shape[1] // 3
    slots = 2 * capacity
    tok = block // parts
    shapes = [
        (pairs, slots, width // pairs), (pairs, slots, width // pairs),
        (slots, hidden), (slots, hidden), (slots, hidden),
        (block, width), (block, units), (block, units), (block, units),
    ]
    saved_specs = [pl.BlockSpec((1,) + s, functools.partial(lambda n, *_: (step,) + (0,) * n, len(s))) for s in shapes]
    outs = [
        jax.ShapeDtypeStruct((2, parts, tok, width), BF16),
        jax.ShapeDtypeStruct((2, parts, tok + 16, width), BF16),
    ] + [jax.ShapeDtypeStruct((steps,) + s, BF16) for s in shapes]
    operands = [e, xs[0], xs[1], cs[0], cs[1], tables[0], tables[1], wgu, wd, sw, router_t]
    in_specs = [pl.BlockSpec(memory_space=pltpu.SMEM)] + [whole(o.shape) for o in operands[1:]]
    first = len(operands)
    flops = 2 * slots * width * hidden * 6 + 2 * block * width * (units * 6 + capacity * 8)
    return pl.pallas_call(
        functools.partial(expert_kernel, capacity, parts, len(saved)),
        grid=(1,),
        in_specs=in_specs + [pl.BlockSpec(memory_space=pl.ANY)] * len(saved),
        out_specs=[whole(outs[0].shape), whole(outs[1].shape)] + saved_specs,
        out_shape=outs,
        input_output_aliases={first + i: 2 + i for i in range(len(saved))},
        compiler_params=params(),
        cost_estimate=pl.CostEstimate(flops=flops, bytes_accessed=20_000_000, transcendentals=0),
    )(*operands, *saved)


def norm_back(grad, values, scale, gain):
    grad_gain = jnp.sum(grad * values * scale, axis=0)
    scaled = grad * gain
    grad_values = scale * scaled - values * scale * scale * scale * jnp.mean(
        scaled * values, axis=-1, keepdims=True
    )
    return grad_values, grad_gain


def local(
    tokens,
    segments,
    routes,
    query_weight,
    key_weight,
    value_weight,
    out_weight,
    attn_gain,
    ffn_gain,
    router_weight,
    shared_gate,
    shared_up,
    shared_down,
    expert_gate,
    expert_up,
    expert_down,
    cotangent,
):
    fsdp, ctx, tp = (lax.axis_size(a) for a in ("fsdp", "ctx", "tp"))
    pairs = fsdp // 2
    me = lax.axis_index("fsdp")
    pair, core = me // 2, me % 2
    plane = lax.axis_index("ctx")
    lane = lax.axis_index("tp")
    tokens, cotangent, routes = tokens[0], cotangent[0], routes[0]
    block, width = tokens.shape
    share, cols = query_weight.shape
    experts = expert_gate.shape[0]
    hidden_units = expert_gate.shape[2]
    units = shared_gate.shape[1] // ctx
    top_count = routes.shape[1]
    capacity = 3 * top_count * block // (2 * experts)
    tok = block // tp
    mine = core + 2 * plane
    theirs = 1 - core + 2 * plane

    def pair_gather(piece):
        return place([piece] + [pair_shift(piece, d) for d in range(1, pairs)], pair)

    def full_rows(piece):
        rows = pair_gather(piece)
        both = place([rows, core_swap(rows)], core)
        return jnp.moveaxis(both, 0, 1).reshape(fsdp * piece.shape[0], piece.shape[1])

    prev_one = ctx_open(tokens, 1)
    prev_two = ctx_open(prev_one, 1)

    small = jnp.concatenate(
        [router_weight, attn_gain[:, None], ffn_gain[:, None],
         jnp.zeros((share, 128 - experts - 2), BF16)], axis=1)
    attn_full = full_rows(
        jnp.concatenate([key_weight, value_weight, query_weight, out_weight.T, small], axis=1))
    qkv_full = attn_full[:, : 3 * cols]
    out_full = attn_full[:, 3 * cols : 4 * cols]
    router_full = attn_full[:, 4 * cols : 4 * cols + experts]
    small_t = attn_full[:, 4 * cols : 4 * cols + 16].T
    router_t = jnp.concatenate([small_t[:experts], jnp.zeros((16 - experts, width), BF16)], axis=0)
    attn_scale = small_t[experts : experts + 1].astype(F32)
    ffn_scale = small_t[experts + 1 : experts + 2].astype(F32)

    chosen = routes.T
    hits = jnp.zeros((experts, block), jnp.bool_)
    for j in range(top_count):
        hits = hits | (chosen[j : j + 1] == jnp.arange(experts, dtype=jnp.int32)[:, None])
    spot = jnp.arange(block, dtype=jnp.int32)
    before = (spot[:, None] < spot[None, :]).astype(BF16)
    rank = dot(hits.astype(BF16), before)
    table = jnp.where(hits, rank, -1.0)
    tables = [table]
    for d in range(1, ctx):
        tables.append(ctx_shift(tables[-1], 1))
    peer_tables = core_swap(jnp.stack(tables))

    def expert_rows(stack, offset=0):
        own = pick(stack, mine + offset)
        other = core_swap(pick(stack, theirs + offset))
        chip = place([own, other], core)
        rows = pair_gather(chip)
        return rows.reshape(fsdp * own.shape[0], own.shape[1])

    gate_full = expert_rows(expert_gate)
    up_full = expert_rows(expert_up)
    wgu = jnp.concatenate([gate_full, up_full], axis=1)
    wd = expert_rows(jnp.swapaxes(lax.dynamic_slice_in_dim(expert_down, 2 * plane, 2, 0), 1, 2), -2 * plane)
    at = plane * units
    shared_mine = jnp.concatenate(
        [
            lax.dynamic_slice_in_dim(shared_gate, at, units, 1),
            lax.dynamic_slice_in_dim(shared_up, at, units, 1),
            lax.dynamic_slice_in_dim(shared_down, at, units, 0).T,
        ],
        axis=1,
    )
    sw = full_rows(shared_mine)

    cot_piece = lax.dynamic_slice_in_dim(cotangent, lane * tok, tok, 0)

    def tp_gather(piece):
        return place([piece] + [tp_shift(piece, j) for j in range(1, tp)], lane).reshape(
            tp * piece.shape[0], piece.shape[1])

    cots = [cotangent] + [None] * (ctx - 1)
    moving = cot_piece
    for j in range(1, ctx):
        moving = ctx_shift(moving, -1)
        cots[ctx - j] = tp_gather(moving)
    peer_cots = [core_swap(c) for c in cots]

    positions = (plane - 2) * block + jnp.arange(3 * block, dtype=jnp.int32)
    index = jnp.arange(2 * HD, dtype=jnp.int32)
    rates = 10000.0 ** (-2.0 * (index % (HD // 2)).astype(F32) / HD)
    angles = positions.astype(F32)[:, None] * rates[None, :]
    cosine = jnp.cos(angles)
    sine = jnp.where(index % HD < HD // 2, -1.0, 1.0) * jnp.sin(angles)
    segment_pad = jnp.concatenate([jnp.full((2 * block,), -1, jnp.int32), segments[0]])
    kseg = lax.dynamic_slice_in_dim(segment_pad, plane * block, 3 * block, 0)
    qseg = kseg[2 * block :][None, :]
    kseg = kseg[:, None]

    hid, key_parts, value_parts = [], [], []
    for j, source in ((2, tokens), (1, prev_one), (0, prev_two)):
        rows = slice(j * block, (j + 1) * block)
        got = project(source, attn_scale, qkv_full, cosine[rows], sine[rows], cols, j == 2)
        hid.insert(0, got[0])
        key_parts.insert(0, got[1])
        value_parts.insert(0, got[2])
        if j == 2:
            query = got[3]
    keys = jnp.concatenate(key_parts, axis=0)
    values = jnp.concatenate(value_parts, axis=0)
    attended, lse = attend(query, keys, values, kseg, qseg)
    partial = dot_nt(attended, out_full).reshape(tp, tok, width)
    mixed = pick(partial, lane)
    for j in range(1, tp):
        mixed = mixed + tp_shift(pick(partial, (lane + j) % tp).astype(BF16), j).astype(F32)
    inputs_mine = lax.dynamic_slice_in_dim(tokens, lane * tok, tok, 0).astype(F32)
    mixed = inputs_mine + mixed
    scale_ffn = lax.rsqrt(jnp.mean(mixed * mixed, axis=-1, keepdims=True) + EPS)
    normed_low = (mixed * scale_ffn * ffn_scale).astype(BF16)

    e = mine.astype(jnp.int32)[None]
    saved = []
    moving = normed_low
    out_sum = None
    dx_sum = None
    for d in range(ctx):
        if d:
            moving = ctx_shift(moving, 1)
        own_x = tp_gather(moving)
        peer_x = core_swap(own_x)
        got = expert_step(
            d, ctx, capacity, pairs, tp, e, (own_x, peer_x), (cots[d], peer_cots[d]),
            (tables[d], peer_tables[d]), wgu, wd, sw, router_t, saved)
        out_part, dx_part, saved = got[0], got[1], got[2:]

        def home(part):
            total = part[0].astype(F32) + core_swap(part[1]).astype(F32)
            kept = pick(total, lane)
            for j in range(1, tp):
                sent = pick(total, (lane + j) % tp).astype(BF16)
                kept = kept + tp_shift(sent, j).astype(F32)
            if d == 0:
                return kept
            return ctx_shift(kept.astype(BF16), -d).astype(F32)

        dx_home, out_home = home(dx_part), home(out_part)
        dx_sum = dx_home if dx_sum is None else dx_sum + dx_home
        out_sum = out_home if out_sum is None else out_sum + out_home
    sx, sr, sh, sa, sb, ssx, ssh, ssa, ssb = saved

    def contract(left, right):
        rows = left.shape[0] * left.shape[1]
        return dot_tn(left.reshape(rows, left.shape[2]), right.reshape(rows, right.shape[2]))

    def expert_grad(left, right):
        def piece(index):
            return contract(lax.dynamic_index_in_dim(left, index, 1, keepdims=False), right)

        sent = [pair_shift(piece((pair + j) % pairs).astype(BF16), j) for j in range(1, pairs)]
        total = piece(pair)
        for one in sent:
            total = total + one.astype(F32)
        total = total.astype(BF16).reshape(2, share, right.shape[2])
        own = pick(total, core)
        other = core_swap(pick(total, 1 - core))
        moving = place([own, other], core)
        pieces = [moving]
        for _ in range(1, ctx):
            moving = ctx_shift(moving, 1)
            pieces.append(moving)
        result = jnp.zeros((ctx,) + moving.shape, F32)
        for d, one in enumerate(pieces):
            result = lax.dynamic_update_index_in_dim(result, one.astype(F32), (plane - d) % ctx, 0)
        return result.reshape(experts, share, right.shape[2])

    def row_scatter(total):
        columns = total.shape[1]
        total = total.reshape(pairs, 2, share, columns)
        kept = lax.dynamic_index_in_dim(total, core, 1, keepdims=False)
        sent = lax.dynamic_index_in_dim(total, 1 - core, 1, keepdims=False).astype(BF16)
        total = kept + core_swap(sent).astype(F32)
        kept = pick(total, pair)
        for j in range(1, pairs):
            kept = kept + pair_shift(pick(total, (pair + j) % pairs).astype(BF16), j).astype(F32)
        return kept

    cot_stack = jnp.stack(cots)
    shared_grads = jnp.concatenate(
        [contract(ssx, ssa), contract(ssx, ssb), contract(cot_stack, ssh)], axis=1)
    moving = row_scatter(shared_grads).astype(BF16)
    pieces = [moving]
    for _ in range(1, ctx):
        moving = ctx_shift(moving, 1)
        pieces.append(moving)
    result = jnp.zeros((ctx,) + moving.shape, F32)
    for d, one in enumerate(pieces):
        result = lax.dynamic_update_index_in_dim(result, one.astype(F32), (plane - d) % ctx, 0)
    result = result.reshape(ctx, share, 3, units).transpose(2, 1, 0, 3).reshape(3, share, ctx * units)
    grad_shared_gate, grad_shared_up, grad_shared_down = result[0], result[1], result[2].T

    grad_expert_down = jnp.swapaxes(expert_grad(sr, sh), 1, 2)
    grad_expert_gate = expert_grad(sx, sa)
    grad_expert_up = expert_grad(sx, sb)

    output = tp_gather((mixed + out_sum).astype(BF16))

    grad_out = lax.dynamic_slice_in_dim(cotangent, lane * tok, tok, 0).astype(F32)
    grad_normed = dx_sum[:tok]
    grad_gates = dx_sum[tok : tok + experts, :tok].T
    named = lax.dynamic_slice_in_dim(hits, lane * tok, tok, 1).T
    logits = dot(normed_low, router_full)
    logits = jnp.where(named, logits, -1e30)
    expo = jnp.where(named, jnp.exp(logits - jnp.max(logits, axis=-1, keepdims=True)), 0.0)
    gates = expo / jnp.sum(expo, axis=-1, keepdims=True)
    grad_logits = (
        gates * (grad_gates - jnp.sum(gates * grad_gates, axis=-1, keepdims=True))
    ).astype(BF16)
    grad_router = dot_tn(grad_logits, normed_low)
    grad_normed = grad_normed + dot_nt(grad_logits, router_full)
    grad_mixed_norm, grad_ffn_gain = norm_back(grad_normed, mixed, scale_ffn, ffn_scale)
    grad_mixed = grad_out + grad_mixed_norm
    grad_mixed_low = tp_gather(grad_mixed.astype(BF16))
    grad_out_weight = dot_tn(grad_mixed_low, attended)
    grad_attended = dot(grad_mixed_low, out_full).astype(BF16)

    dq, dk, dv = attend_back(
        query, keys, values, grad_attended, lse, kseg, qseg, cosine, sine)
    hid_all = jnp.concatenate(hid, axis=0)
    attn_grads = jnp.concatenate(
        [dot_tn(hid_all, dk), dot_tn(hid_all, dv), dot_tn(hid[2], dq), grad_out_weight], axis=1)
    rows = row_scatter(attn_grads)
    total = rows.reshape(ctx, share // ctx, 4 * cols)
    kept = pick(total, plane)
    for j in range(1, ctx):
        kept = kept + ctx_shift(pick(total, (plane + j) % ctx).astype(BF16), j).astype(F32)
    kept = kept.astype(BF16)
    attn_rows = place([kept] + [ctx_shift(kept, j) for j in range(1, ctx)], plane)
    attn_rows = attn_rows.reshape(share, 4 * cols).astype(F32)
    grad_key_weight = attn_rows[:, :cols]
    grad_value_weight = attn_rows[:, cols : 2 * cols]
    grad_query_weight = attn_rows[:, 2 * cols : 3 * cols]
    grad_out_rows = attn_rows[:, 3 * cols :].T

    def hidden_back(j):
        piece = slice(j * block, (j + 1) * block)
        total = dot_nt(dk[piece], qkv_full[:, :cols]) + dot_nt(dv[piece], qkv_full[:, cols : 2 * cols])
        if j == 2:
            total = total + dot_nt(dq, qkv_full[:, 2 * cols :])
        total = total.reshape(tp, tok, width)
        kept = pick(total, lane)
        for i in range(1, tp):
            kept = kept + tp_shift(pick(total, (lane + i) % tp).astype(BF16), i).astype(F32)
        return kept

    carried = ctx_open(hidden_back(0).astype(BF16), -1).astype(F32)
    carried = ctx_open((hidden_back(1) + carried).astype(BF16), -1).astype(F32)
    grad_hidden = hidden_back(2) + carried
    scale_attn = lax.rsqrt(jnp.mean(inputs_mine * inputs_mine, axis=-1, keepdims=True) + EPS)
    grad_inputs_norm, grad_attn_gain = norm_back(grad_hidden, inputs_mine, scale_attn, attn_scale)
    input_grad = tp_gather((grad_mixed + grad_inputs_norm).astype(BF16))

    def sum_all(rows):
        for axis in ("fsdp", "tp", "ctx"):
            rows = all_sum(rows, axis)
        return lax.dynamic_slice_in_dim(rows, me * share, share, 1)

    early = sum_all(jnp.concatenate(
        [grad_router, grad_ffn_gain[None], jnp.zeros((16 - experts - 1, width), F32)], axis=0))
    late = sum_all(jnp.broadcast_to(grad_attn_gain[None], (8, width)))
    return (
        output[None],
        input_grad[None],
        grad_query_weight,
        grad_key_weight,
        grad_value_weight,
        grad_out_rows,
        late[0],
        early[experts],
        early[:experts].T,
        grad_shared_gate,
        grad_shared_up,
        grad_shared_down,
        grad_expert_gate,
        grad_expert_up,
        grad_expert_down,
    )


def solution(mesh):
    in_specs = (
        P("fsdp", "ctx", None),
        P("fsdp", None),
        P("fsdp", "ctx", None),
        P("fsdp", "tp"),
        P("fsdp", "tp"),
        P("fsdp", "tp"),
        P("tp", "fsdp"),
        P("fsdp"),
        P("fsdp"),
        P("fsdp", None),
        P("fsdp", "tp"),
        P("fsdp", "tp"),
        P("tp", "fsdp"),
        P(None, "fsdp", "tp"),
        P(None, "fsdp", "tp"),
        P(None, "tp", "fsdp"),
        P("fsdp", "ctx", None),
    )
    out_specs = (
        P("fsdp", "ctx", None),
        P("fsdp", "ctx", None),
        P("fsdp", "tp"),
        P("fsdp", "tp"),
        P("fsdp", "tp"),
        P("tp", "fsdp"),
        P("fsdp"),
        P("fsdp"),
        P("fsdp", None),
        P("fsdp", "tp"),
        P("fsdp", "tp"),
        P("tp", "fsdp"),
        P(None, "fsdp", "tp"),
        P(None, "fsdp", "tp"),
        P(None, "tp", "fsdp"),
    )
    return jax.shard_map(local, mesh=mesh, in_specs=in_specs, out_specs=out_specs, check_vma=False)
```

time: 1440 us -> 724 us (0.50)
  waiting for transfers between devices: 968 us -> 312 us
  matrix products: 205 us -> 27.5 us
  Pallas kernels: 0 us -> 94 us
  starting transfers between devices: 17.9 us -> 98.9 us
  blocking collectives: 67.1 us -> 0 us
  local copies, waits for them, and re-layouts: 75 us -> 102 us
  between operations: 19.2 us -> 2.96 us
    psum x4 -> x0, waiting for transfers between devices: 404 us -> none  [the longest x1 338 us: local(): lax.psum(shard_query.astype(jnp.bfloat16), 'ctx').astype(jnp.float32)]
    reduce_scatter x10 -> x0, waiting for transfers between devices: 289 us -> none  [the longest x1 102 us: local(): lax.psum_scatter(grad_expert_gate.astype(jnp.bfloat16), 'fsdp', scatter_d...]
    ppermute x8 -> x106, waiting for transfers between devices: 43.5 us -> 312 us  [the longest x33 97.3 us: ctx_shift(): lax.ppermute(block, 'ctx', [(i, (i + distance) % size) for i in range(siz...]
    all_gather x6 -> x0, waiting for transfers between devices: 206 us -> none  [the longest x1 73 us: local(): lax.all_gather(expert_up, 'fsdp', axis=1, tiled=True)]
    dot_general x39 -> x26, matrix products: 205 us -> 27.5 us  [the longest x14 17.2 us: dot_tn(): lax.dot_general(left, right, (((0,), (0,)), ((), ())), preferred_element_...]
    pallas_call x0 -> x9, Pallas kernels: none -> 94 us  [the longest x4 51.2 us: expert_step(): pl.pallas_call(functools.partial(expert_kernel, capacity, parts, len(save...]
    ppermute x8 -> x106, starting transfers between devices: 16.5 us -> 98.9 us  [the longest x33 39.6 us: ctx_shift(): lax.ppermute(block, 'ctx', [(i, (i + distance) % size) for i in range(siz...]
    all_gather x5 -> x0, blocking collectives: 35 us -> none  [the longest x1 7.87 us: local(): lax.all_gather(out_weight, 'fsdp', axis=1, tiled=True)]
  transfers between devices with their start and end apart: 29 -> 106, of which waited for: 14 -> 39; matrix products, arithmetic and copies ran while one was open for 15% -> 26% of each run, Pallas kernels for 0% -> 13%
where the time goes in v1:
time: 724 us; the launch traced here: 715 us
  waiting for transfers between devices  312 us (43%)
  local copies, waits for them, and re-layouts  102 us (14%)
  starting transfers between devices  98.9 us (14%)
  Pallas kernels  94 us (13%)
  other arithmetic  78 us (11%)
  matrix products  27.5 us (4%)
    ppermute x33, waiting for transfers between devices, ctx_shift(): lax.ppermute(block, 'ctx', [(i, (i + distance) % size) for i in range(siz...  97.3 us
    ppermute x10, waiting for transfers between devices, all_sum(): other = lax.ppermute(block, axis, [(i, i ^ reach) for i in range(size)])  79.5 us
    ppermute x10, waiting for transfers between devices, pair_shift(): return lax.ppermute(block, 'fsdp', route)  60 us
    pallas_call x4, Pallas kernels, expert_step(): pl.pallas_call(functools.partial(expert_kernel, capacity, parts, len(save...  51.2 us
    ppermute x22, waiting for transfers between devices, tp_shift(): lax.ppermute(block, 'tp', [(i, (i + distance) % size) for i in range(size)])  47.5 us
    ppermute x33, starting transfers between devices, ctx_shift(): lax.ppermute(block, 'ctx', [(i, (i + distance) % size) for i in range(siz...  39.6 us
    ppermute x4, waiting for transfers between devices, ctx_open(): return lax.ppermute(block, 'ctx', route)  27.3 us
    ppermute x22, starting transfers between devices, tp_shift(): lax.ppermute(block, 'tp', [(i, (i + distance) % size) for i in range(size)])  24.7 us
  transfers between devices with their start and end apart: 106, of which 39 were waited for; matrix products, arithmetic and copies ran while one was open for 26% of the time, Pallas kernels for 13%

profile of v1, /device:TPU:0, one launch (start us, length us, event | category | flops | bytes accessed | tf_op | source)
XLA Modules:
  0.0 714.8 jit_solution(6389373391997136938)
XLA Ops:
  9.2 3.6 collective-permute-start.25
  27.5 3.4 collective-permute-done.9.to_ref
  32.8 3.6 collective-permute-done.10.to_ref
  47.1 4.6 collective-permute-start.2
  57.0 5.5 collective-permute-done.15
  67.6 4.1 collective-permute-done.36
  73.4 6.0 collective-permute-done.13
  80.2 15.1 %collective-permute-done.17 = bf16[2,192,1024]{2,1,0:T(8,128)(2,1)S(1)} collective-permute-done((bf16[2,192,1024]{2,1,0:T(8,128)(2,1)S(1)}, bf16[2,192,1024]{2,1,0:T(8,128)(2,1)S(1)}, u32[]{:S(2)}, u32[]{:S(2)}) %collective-permute-start.17) | collective-permute-done | bytes 786464 | tf_op jit(solution)/shard_map/ppermute | solution.py:39
  105.7 7.5 %collective-permute-done.3.tok_ref = bf16[512,768]{1,0:T(8,128)(2,1)S(1)} collective-permute-done((bf16[512,768]{1,0:T(8,128)(2,1)}, bf16[512,768]{1,0:T(8,128)(2,1)S(1)}, u32[]{:S(2)}, u32[]{:S(2)}) %collective-permute-start.3) | collective-permute-done | bytes 786464 | tf_op jit(solution)/shard_map/ppermute | solution.py:55
  114.1 3.7 shard_map.281
  119.9 4.4 shard_map.280
  124.4 3.8 shard_map.282
  130.8 13.4 %shard_map.283 = (bf16[512,384]{1,0:T(8,128)(2,1)}, f32[3,2,512]{2,1,0:T(2,128)}) custom-call(bf16[512,384]{1,0:T(8,128)(2,1)} %get-tuple-element.74.q_ref, bf16[1536,384]{1,0:T(8,128)(2,1)} %copy-done.19, bf16[1536,384]{1,0:T(8,128)(2,1)} %copy-done.18, s32[1536,1]{1,0:T(8,128)} %broadcast_in_dim.228.kseg_ref, s32[1,512]{1,0:T(1,128)} %bitcast.583), custom_call_target="tpu_custom_call" | custom-call | tf_op jit(solution)/shard_map/pallas_call | solution.py:183
  149.8 5.7 collective-permute-done.4
  160.2 4.4 collective-permute-done.5
  170.4 6.1 collective-permute-done.23
  181.3 12.8 %shard_map.284 = (bf16[2,2,256,768]{3,2,1,0:T(8,128)(2,1)}, bf16[2,2,272,768]{3,2,1,0:T(8,128)(2,1)}, bf16[4,2,384,384]{3,2,1,0:T(8,128)(2,1)}, bf16[4,2,384,384...) custom-call(s32[1]{0:T(128)} %bitcast.19.e_ref, ...), custom_call_target="tpu_custom_call" | custom-call | flops 6039797760 | bytes 20000000 | tf_op jit(solution)/shard_map/pallas_call | solution.py:388
  200.4 9.5 %collective-permute-done.41 = bf16[256,768]{1,0:T(8,128)(2,1)S(1)} collective-permute-done((bf16[256,768]{1,0:T(8,128)(2,1)}, bf16[256,768]{1,0:T(8,128)(2,1)S(1)}, u32[]{:S(2)}, u32[]{:S(2)}) %collective-permute-start.41) | collective-permute-done | bytes 393248 | tf_op jit(solution)/shard_map/ppermute | solution.py:49
  210.9 12.7 %shard_map.285 = (bf16[2,2,256,768]{3,2,1,0:T(8,128)(2,1)}, bf16[2,2,272,768]{3,2,1,0:T(8,128)(2,1)}, bf16[4,2,384,384]{3,2,1,0:T(8,128)(2,1)}, bf16[4,2,384,384...) custom-call(s32[1]{0:T(128)} %bitcast.19.e_ref, ...), custom_call_target="tpu_custom_call", output_to_operand_aliasing={{2}: (11, {}), {3}: (12, {}), {4}: (13, {}), {5}: (14, {}),... | custom-call | flops 6039797760 | bytes 20000000 | tf_op jit(solution)/shard_map/pallas_call | solution.py:388
  230.5 13.0 %shard_map.286 = (bf16[2,2,256,768]{3,2,1,0:T(8,128)(2,1)}, bf16[2,2,272,768]{3,2,1,0:T(8,128)(2,1)}, bf16[4,2,384,384]{3,2,1,0:T(8,128)(2,1)}, bf16[4,2,384,384...) custom-call(s32[1]{0:T(128)} %bitcast.19.e_ref, ...), custom_call_target="tpu_custom_call", output_to_operand_aliasing={{2}: (11, {}), {3}: (12, {}), {4}: (13, {}), {5}: (14, {}),... | custom-call | flops 6039797760 | bytes 20000000 | tf_op jit(solution)/shard_map/pallas_call | solution.py:388
  254.3 12.8 %shard_map.287 = (bf16[2,2,256,768]{3,2,1,0:T(8,128)(2,1)}, bf16[2,2,272,768]{3,2,1,0:T(8,128)(2,1)}, bf16[4,2,384,384]{3,2,1,0:T(8,128)(2,1)}, bf16[4,2,384,384...) custom-call(s32[1]{0:T(128)} %bitcast.19.e_ref, ...), custom_call_target="tpu_custom_call", output_to_operand_aliasing={{2}: (11, {}), {3}: (12, {}), {4}: (13, {}), {5}: (14, {}),... | custom-call | flops 6039797760 | bytes 20000000 | tf_op jit(solution)/shard_map/pallas_call | solution.py:388
  297.5 6.6 collective-permute-done.31
  308.8 7.6 %collective-permute-done.53 = bf16[272,768]{1,0:T(8,128)(2,1)S(1)} collective-permute-done((bf16[272,768]{1,0:T(8,128)(2,1)S(1)}, bf16[272,768]{1,0:T(8,128)(2,1)S(1)}, u32[]{:S(2)}, u32[]{:S(2)}) %collective-permute-start.53) | collective-permute-done | bytes 417824 | tf_op jit(solution)/shard_map/ppermute | solution.py:44
  317.2 7.4 %collective-permute-done.91 = bf16[384,1024]{1,0:T(8,128)(2,1)S(1)} collective-permute-done((bf16[384,1024]{1,0:T(8,128)(2,1)S(1)}, bf16[384,1024]{1,0:T(8,128)(2,1)S(1)}, u32[]{:S(2)}, u32[]{:S(2)}) %collective-permute-start.91) | collective-permute-done | bytes 786464 | tf_op jit(solution)/shard_map/ppermute | solution.py:39
  327.5 13.9 %collective-permute-done.96 = bf16[384,1024]{1,0:T(8,128)(2,1)S(1)} collective-permute-done((bf16[384,1024]{1,0:T(8,128)(2,1)S(1)}, bf16[384,1024]{1,0:T(8,128)(2,1)S(1)}, u32[]{:S(2)}, u32[]{:S(2)}) %collective-permute-start.96) | collective-permute-done | bytes 786464 | tf_op jit(solution)/shard_map/ppermute | solution.py:39
  343.7 12.1 %collective-permute-done.101 = bf16[384,1024]{1,0:T(8,128)(2,1)S(1)} collective-permute-done((bf16[384,1024]{1,0:T(8,128)(2,1)S(1)}, bf16[384,1024]{1,0:T(8,128)(2,1)S(1)}, u32[]{:S(2)}, u32[]{:S(2)}) %collective-permute-start.101) | collective-permute-done | bytes 786464 | tf_op jit(solution)/shard_map/ppermute | solution.py:39
  363.9 4.5 collective-permute-done.56
  371.6 3.5 broadcast.259.clone
  377.4 3.5 broadcast.259.clone.1
  383.2 3.5 broadcast.259.clone.2
  389.2 3.3 collective-permute-start.60
  393.5 8.3 %collective-permute-done.88 = bf16[192,768]{1,0:T(8,128)(2,1)S(1)} collective-permute-done((bf16[192,768]{1,0:T(8,128)(2,1)S(1)}, bf16[192,768]{1,0:T(8,128)(2,1)S(1)}, u32[]{:S(2)}, u32[]{:S(2)}) %collective-permute-start.88) | collective-permute-done | bytes 294944 | tf_op jit(solution)/shard_map/ppermute | solution.py:49
  401.8 6.9 collective-permute-start.89
  414.3 27.2 %collective-permute-done.57 = bf16[272,768]{1,0:T(8,128)(2,1)S(1)} collective-permute-done((bf16[272,768]{1,0:T(8,128)(2,1)S(1)}, bf16[272,768]{1,0:T(8,128)(2,1)S(1)}, u32[]{:S(2)}, u32[]{:S(2)}) %collective-permute-start.57) | collective-permute-done | bytes 417824 | tf_op jit(solution)/shard_map/ppermute | solution.py:49
  453.8 16.5 %collective-permute-done.90 = bf16[192,768]{1,0:T(8,128)(2,1)S(1)} collective-permute-done((bf16[192,768]{1,0:T(8,128)(2,1)S(1)}, bf16[192,768]{1,0:T(8,128)(2,1)S(1)}, u32[]{:S(2)}, u32[]{:S(2)}) %collective-permute-start.90) | collective-permute-done | bytes 294944 | tf_op jit(solution)/shard_map/ppermute | solution.py:49
  471.1 4.6 reshape.847
  475.7 11.5 %collective-permute-done.84 = f32[16,768]{1,0:T(8,128)S(1)} collective-permute-done((f32[16,768]{1,0:T(8,128)S(1)}, f32[16,768]{1,0:T(8,128)S(1)}, u32[]{:S(2)}, u32[]{:S(2)}) %collective-permute-start.84) | collective-permute-done | bytes 49184 | tf_op jit(solution)/shard_map/ppermute | solution.py:79
  487.9 6.3 fusion.110
  513.0 17.5 %shard_map.288 = (bf16[512,384]{1,0:T(8,128)(2,1)}, bf16[1536,384]{1,0:T(8,128)(2,1)}, bf16[1536,384]{1,0:T(8,128)(2,1)}) custom-call(bf16[512,384]{1,0:T(8,128)(2,1)} %get-tuple-element.74.q_ref, bf16[1536,384]{1,0:T(8,128)(2,1)} %copy-done.19, bf16[1536,384]{1,0:T(8,128)(2,1)} %copy-done.18, bf16[512,384]{1,0:T(8,128)(2,1)} %convolution_convert_fusion.3.g_ref, ...), custom_call_target="tpu_custom_call" | custom-call | tf_op jit(solution)/shard_map/pallas_call | solution.py:255
  545.7 5.5 collective-permute-done.64
  555.3 6.2 copy.95
  568.3 3.3 collective-permute-start.104
  575.3 19.8 %collective-permute-done.66 = bf16[256,768]{1,0:T(8,128)(2,1)S(1)} collective-permute-done((bf16[256,768]{1,0:T(8,128)(2,1)S(1)}, bf16[256,768]{1,0:T(8,128)(2,1)S(1)}, u32[]{:S(2)}, u32[]{:S(2)}) %collective-permute-start.66) | collective-permute-done | bytes 393248 | tf_op jit(solution)/shard_map/ppermute | solution.py:55
  611.1 45.6 %collective-permute-done.79 = f32[8,768]{1,0:T(8,128)S(1)} collective-permute-done((f32[8,768]{1,0:T(8,128)S(1)}, f32[8,768]{1,0:T(8,128)S(1)}, u32[]{:S(2)}, u32[]{:S(2)}) %collective-permute-start.79) | collective-permute-done | bytes 24608 | tf_op jit(solution)/shard_map/ppermute | solution.py:79
  656.7 4.7 collective-permute-done.40
  664.9 14.9 %collective-permute-done.80 = f32[8,768]{1,0:T(8,128)S(1)} collective-permute-done((f32[8,768]{1,0:T(8,128)S(1)}, f32[8,768]{1,0:T(8,128)S(1)}, u32[]{:S(2)}, u32[]{:S(2)}) %collective-permute-start.80) | collective-permute-done | bytes 24608 | tf_op jit(solution)/shard_map/ppermute | solution.py:79
  691.3 8.2 %collective-permute-done.71 = bf16[48,1536]{1,0:T(8,128)(2,1)S(1)} collective-permute-done((bf16[48,1536]{1,0:T(8,128)(2,1)S(1)}, bf16[48,1536]{1,0:T(8,128)(2,1)S(1)}, u32[]{:S(2)}, u32[]{:S(2)}) %collective-permute-start.71) | collective-permute-done | bytes 147488 | tf_op jit(solution)/shard_map/ppermute | solution.py:49
  706.8 6.3 collective-permute-done.74
  (570 shorter events, 277.0 us)
Async XLA Ops:
  4.4 42.5 %collective-permute-start = (bf16[192,1664]{1,0:T(8,128)(2,1)S(1)}, bf16[192,1664]{1,0:T(8,128)(2,1)S(1)}, u32[]{:S(2)}, u32[]{:S(2)}) collective-permute-start(bf16[192,1664]{1,0:T(8,128)(2,1)S(1)} %concatenate.145), channel_id=1, source_target_pairs={{0,16},{8,24},{16,0},{24,8},{1,17},{9,25},{17,1},{25,9},{2,18},{10... | collective-permute-start | bytes 1916936 | tf_op jit(solution)/shard_map/ppermute | solution.py:39
  9.2 34.7 %collective-permute-start.25 = (bf16[256,768]{1,0:T(8,128)(2,1)}, bf16[256,768]{1,0:T(8,128)(2,1)}, u32[]{:S(2)}, u32[]{:S(2)}) collective-permute-start(bf16[256,768]{1,0:T(8,128)(2,1)} %dynamic-slice_bitcast_fusion.3), channel_id=1, source_target_pairs={{0,6},{2,0},{4,2},{6,4},{1,7},{3,1},{5,3},{7,5},{8,14},{10,8},{12,... | collective-permute-start | bytes 1179656 | tf_op jit(solution)/shard_map/ppermute | solution.py:49
  14.9 26.4 %collective-permute-start.14 = (bf16[192,1024]{1,0:T(8,128)(2,1)}, bf16[192,1024]{1,0:T(8,128)(2,1)S(1)}, u32[]{:S(2)}, u32[]{:S(2)}) collective-permute-start(bf16[192,1024]{1,0:T(8,128)(2,1)} %get-tuple-element.155), channel_id=1, source_target_pairs={{0,8},{8,0},{16,24},{24,16},{1,9},{9,1},{17,25},{25,17},{2,10},{10... | collective-permute-start | bytes 1179656 | tf_op jit(solution)/shard_map/ppermute | solution.py:32
  47.1 32.5 %collective-permute-start.2 = (bf16[512,768]{1,0:T(8,128)(2,1)S(1)}, bf16[512,768]{1,0:T(8,128)(2,1)}, u32[]{:S(2)}, u32[]{:S(2)}) collective-permute-start(bf16[512,768]{1,0:T(8,128)(2,1)S(1)} %bitcast.492), channel_id=1, source_target_pairs={{0,2},{2,4},{4,6},{1,3},{3,5},{5,7},{8,10},{10,12},{12,14},{9,11},... | collective-permute-start | bytes 2359304 | tf_op jit(solution)/shard_map/ppermute | solution.py:55
  54.9 24.4 %collective-permute-start.13 = (bf16[2,192,1024]{2,1,0:T(8,128)(2,1)S(1)}, bf16[2,192,1024]{2,1,0:T(8,128)(2,1)S(1)}, u32[]{:S(2)}, u32[]{:S(2)}) collective-permute-start(bf16[2,192,1024]{2,1,0:T(8,128)(2,1)S(1)} %maximum_select_fusion.8), channel_id=1, source_target_pairs={{0,16},{8,24},{16,0},{24,8},{1,17},{9,25},{17,1},{25,9},{2,18},{10... | collective-permute-start | bytes 2359304 | tf_op jit(solution)/shard_map/ppermute | solution.py:39
  56.1 39.1 %collective-permute-start.17 = (bf16[2,192,1024]{2,1,0:T(8,128)(2,1)S(1)}, bf16[2,192,1024]{2,1,0:T(8,128)(2,1)S(1)}, u32[]{:S(2)}, u32[]{:S(2)}) collective-permute-start(bf16[2,192,1024]{2,1,0:T(8,128)(2,1)S(1)} %maximum_select_fusion.12), channel_id=1, source_target_pairs={{0,16},{8,24},{16,0},{24,8},{1,17},{9,25},{17,1},{25,9},{2,18},{10... | collective-permute-start | bytes 2359304 | tf_op jit(solution)/shard_map/ppermute | solution.py:39
  57.0 44.8 %collective-permute-start.1 = (bf16[2,192,1664]{2,1,0:T(8,128)(2,1)S(1)}, bf16[2,192,1664]{2,1,0:T(8,128)(2,1)S(1)}, u32[]{:S(2)}, u32[]{:S(2)}) collective-permute-start(bf16[2,192,1664]{2,1,0:T(8,128)(2,1)S(1)} %maximum_select_fusion.4), channel_id=1, source_target_pairs={{0,8},{8,0},{16,24},{24,16},{1,9},{9,1},{17,25},{25,17},{2,10},{10... | collective-permute-start | bytes 3833864 | tf_op jit(solution)/shard_map/ppermute | solution.py:32
  71.7 25.1 %collective-permute-start.27 = (bf16[256,768]{1,0:T(8,128)(2,1)S(1)}, bf16[256,768]{1,0:T(8,128)(2,1)}, u32[]{:S(2)}, u32[]{:S(2)}) collective-permute-start(bf16[256,768]{1,0:T(8,128)(2,1)S(1)} %collective-permute-done.26), channel_id=1, source_target_pairs={{0,6},{2,0},{4,2},{6,4},{1,7},{3,1},{5,3},{7,5},{8,14},{10,8},{12,... | collective-permute-start | bytes 1179656 | tf_op jit(solution)/shard_map/ppermute | solution.py:49
  79.3 97.3 %collective-permute-start.7 = (bf16[512,768]{1,0:T(8,128)(2,1)}, bf16[512,768]{1,0:T(8,128)(2,1)}, u32[]{:S(2)}, u32[]{:S(2)}) collective-permute-start(bf16[512,768]{1,0:T(8,128)(2,1)} %bitcast.23.co_ref), channel_id=1, source_target_pairs={{0,8},{8,0},{16,24},{24,16},{1,9},{9,1},{17,25},{25,17},{2,10},{10... | collective-permute-start | bytes 2359304 | tf_op jit(solution)/shard_map/ppermute | solution.py:32
  79.6 173.3 %collective-permute-start.45 = (bf16[512,768]{1,0:T(8,128)(2,1)}, bf16[512,768]{1,0:T(8,128)(2,1)}, u32[]{:S(2)}, u32[]{:S(2)}) collective-permute-start(bf16[512,768]{1,0:T(8,128)(2,1)} %bitcast.95.co_ref), channel_id=1, source_target_pairs={{0,8},{8,0},{16,24},{24,16},{1,9},{9,1},{17,25},{25,17},{2,10},{10... | collective-permute-start | bytes 2359304 | tf_op jit(solution)/shard_map/ppermute | solution.py:32
  96.8 50.6 %collective-permute-start.28 = (bf16[256,768]{1,0:T(8,128)(2,1)}, bf16[256,768]{1,0:T(8,128)(2,1)}, u32[]{:S(2)}, u32[]{:S(2)}) collective-permute-start(bf16[256,768]{1,0:T(8,128)(2,1)} %collective-permute-done.27), channel_id=1, source_target_pairs={{0,1},{1,0},{2,3},{3,2},{4,5},{5,4},{6,7},{7,6},{8,9},{9,8},{10,11... | collective-permute-start | bytes 1179656 | tf_op jit(solution)/shard_map/ppermute | solution.py:44
  176.5 52.9 %collective-permute-start.37 = (bf16[512,768]{1,0:T(8,128)(2,1)S(1)}, bf16[512,768]{1,0:T(8,128)(2,1)S(1)}, u32[]{:S(2)}, u32[]{:S(2)}) collective-permute-start(bf16[512,768]{1,0:T(8,128)(2,1)S(1)} %bitcast.512), channel_id=1, source_target_pairs={{0,8},{8,0},{16,24},{24,16},{1,9},{9,1},{17,25},{25,17},{2,10},{10... | collective-permute-start | bytes 2359304 | tf_op jit(solution)/shard_map/ppermute | solution.py:32
  176.7 22.6 %collective-permute-start.29 = (bf16[512,768]{1,0:T(8,128)(2,1)S(1)}, bf16[512,768]{1,0:T(8,128)(2,1)S(1)}, u32[]{:S(2)}, u32[]{:S(2)}) collective-permute-start(bf16[512,768]{1,0:T(8,128)(2,1)S(1)} %bitcast.514), channel_id=1, source_target_pairs={{0,8},{8,0},{16,24},{24,16},{1,9},{9,1},{17,25},{25,17},{2,10},{10... | collective-permute-start | bytes 2359304 | tf_op jit(solution)/shard_map/ppermute | solution.py:32
  180.3 29.6 %collective-permute-start.24 = (bf16[512,768]{1,0:T(8,128)(2,1)S(1)}, bf16[512,768]{1,0:T(8,128)(2,1)}, u32[]{:S(2)}, u32[]{:S(2)}) collective-permute-start(bf16[512,768]{1,0:T(8,128)(2,1)S(1)} %bitcast.521), channel_id=1, source_target_pairs={{0,8},{8,0},{16,24},{24,16},{1,9},{9,1},{17,25},{25,17},{2,10},{10... | collective-permute-start | bytes 2359304 | tf_op jit(solution)/shard_map/ppermute | solution.py:32
  200.2 29.4 %collective-permute-start.35 = (bf16[512,768]{1,0:T(8,128)(2,1)S(1)}, bf16[512,768]{1,0:T(8,128)(2,1)S(1)}, u32[]{:S(2)}, u32[]{:S(2)}) collective-permute-start(bf16[512,768]{1,0:T(8,128)(2,1)S(1)} %bitcast.519), channel_id=1, source_target_pairs={{0,8},{8,0},{16,24},{24,16},{1,9},{9,1},{17,25},{25,17},{2,10},{10... | collective-permute-start | bytes 2359304 | tf_op jit(solution)/shard_map/ppermute | solution.py:32
  209.9 39.4 %collective-permute-start.50 = (bf16[2,272,768]{2,1,0:T(8,128)(2,1)}, bf16[2,272,768]{2,1,0:T(8,128)(2,1)}, u32[]{:S(2)}, u32[]{:S(2)}) collective-permute-start(bf16[2,272,768]{2,1,0:T(8,128)(2,1)} %slice_bitcast_fusion.3), channel_id=1, source_target_pairs={{0,8},{8,0},{16,24},{24,16},{1,9},{9,1},{17,25},{25,17},{2,10},{10... | collective-permute-start | bytes 2506760 | tf_op jit(solution)/shard_map/ppermute | solution.py:32
  229.4 23.8 %collective-permute-start.43 = (bf16[512,768]{1,0:T(8,128)(2,1)S(1)}, bf16[512,768]{1,0:T(8,128)(2,1)}, u32[]{:S(2)}, u32[]{:S(2)}) collective-permute-start(bf16[512,768]{1,0:T(8,128)(2,1)S(1)} %bitcast.517), channel_id=1, source_target_pairs={{0,8},{8,0},{16,24},{24,16},{1,9},{9,1},{17,25},{25,17},{2,10},{10... | collective-permute-start | bytes 2359304 | tf_op jit(solution)/shard_map/ppermute | solution.py:32
  229.6 63.9 %collective-permute-start.52 = (bf16[2,272,768]{2,1,0:T(8,128)(2,1)}, bf16[2,272,768]{2,1,0:T(8,128)(2,1)}, u32[]{:S(2)}, u32[]{:S(2)}) collective-permute-start(bf16[2,272,768]{2,1,0:T(8,128)(2,1)} %slice_bitcast_fusion.2), channel_id=1, source_target_pairs={{0,8},{8,0},{16,24},{24,16},{1,9},{9,1},{17,25},{25,17},{2,10},{10... | collective-permute-start | bytes 2506760 | tf_op jit(solution)/shard_map/ppermute | solution.py:32
  245.7 25.9 %collective-permute-start.30 = (bf16[2,256,768]{2,1,0:T(8,128)(2,1)S(1)}, bf16[2,256,768]{2,1,0:T(8,128)(2,1)S(1)}, u32[]{:S(2)}, u32[]{:S(2)}) collective-permute-start(bf16[2,256,768]{2,1,0:T(8,128)(2,1)S(1)} %copy-done.60), channel_id=1, source_target_pairs={{0,8},{8,0},{16,24},{24,16},{1,9},{9,1},{17,25},{25,17},{2,10},{10... | collective-permute-start | bytes 2359304 | tf_op jit(solution)/shard_map/ppermute | solution.py:32
  249.3 57.2 %collective-permute-start.55 = (bf16[2,272,768]{2,1,0:T(8,128)(2,1)}, bf16[2,272,768]{2,1,0:T(8,128)(2,1)}, u32[]{:S(2)}, u32[]{:S(2)}) collective-permute-start(bf16[2,272,768]{2,1,0:T(8,128)(2,1)} %slice_bitcast_fusion.1), channel_id=1, source_target_pairs={{0,8},{8,0},{16,24},{24,16},{1,9},{9,1},{17,25},{25,17},{2,10},{10... | collective-permute-start | bytes 2506760 | tf_op jit(solution)/shard_map/ppermute | solution.py:32
  252.9 43.0 %collective-permute-start.38 = (bf16[2,256,768]{2,1,0:T(8,128)(2,1)}, bf16[2,256,768]{2,1,0:T(8,128)(2,1)}, u32[]{:S(2)}, u32[]{:S(2)}) collective-permute-start(bf16[2,256,768]{2,1,0:T(8,128)(2,1)} %slice_bitcast_fusion.5), channel_id=1, source_target_pairs={{0,8},{8,0},{16,24},{24,16},{1,9},{9,1},{17,25},{25,17},{2,10},{10... | collective-permute-start | bytes 2359304 | tf_op jit(solution)/shard_map/ppermute | solution.py:32
  253.2 157.4 %collective-permute-start.51 = (bf16[272,768]{1,0:T(8,128)(2,1)}, bf16[272,768]{1,0:T(8,128)(2,1)}, u32[]{:S(2)}, u32[]{:S(2)}) collective-permute-start(bf16[272,768]{1,0:T(8,128)(2,1)} %fusion.60), channel_id=1, source_target_pairs={{0,1},{1,0},{2,3},{3,2},{4,5},{5,4},{6,7},{7,6},{8,9},{9,8},{10,11... | collective-permute-start | bytes 1253384 | tf_op jit(solution)/shard_map/ppermute | solution.py:44
  271.6 89.8 %collective-permute-start.58 = (bf16[2,272,768]{2,1,0:T(8,128)(2,1)}, bf16[2,272,768]{2,1,0:T(8,128)(2,1)}, u32[]{:S(2)}, u32[]{:S(2)}) collective-permute-start(bf16[2,272,768]{2,1,0:T(8,128)(2,1)} %slice_bitcast_fusion), channel_id=1, source_target_pairs={{0,8},{8,0},{16,24},{24,16},{1,9},{9,1},{17,25},{25,17},{2,10},{10... | collective-permute-start | bytes 2506760 | tf_op jit(solution)/shard_map/ppermute | solution.py:32
  316.4 41.9 %collective-permute-start.46 = (bf16[2,256,768]{2,1,0:T(8,128)(2,1)S(1)}, bf16[2,256,768]{2,1,0:T(8,128)(2,1)S(1)}, u32[]{:S(2)}, u32[]{:S(2)}) collective-permute-start(bf16[2,256,768]{2,1,0:T(8,128)(2,1)S(1)} %copy-done.59), channel_id=1, source_target_pairs={{0,8},{8,0},{16,24},{24,16},{1,9},{9,1},{17,25},{25,17},{2,10},{10... | collective-permute-start | bytes 2359304 | tf_op jit(solution)/shard_map/ppermute | solution.py:32
  316.5 25.0 %collective-permute-start.96 = (bf16[384,1024]{1,0:T(8,128)(2,1)S(1)}, bf16[384,1024]{1,0:T(8,128)(2,1)S(1)}, u32[]{:S(2)}, u32[]{:S(2)}) collective-permute-start(bf16[384,1024]{1,0:T(8,128)(2,1)S(1)} %convolution_convert_fusion.1), channel_id=1, source_target_pairs={{0,16},{8,24},{16,0},{24,8},{1,17},{9,25},{17,1},{25,9},{2,18},{10... | collective-permute-start | bytes 2359304 | tf_op jit(solution)/shard_map/ppermute | solution.py:39
  324.6 31.3 %collective-permute-start.101 = (bf16[384,1024]{1,0:T(8,128)(2,1)S(1)}, bf16[384,1024]{1,0:T(8,128)(2,1)S(1)}, u32[]{:S(2)}, u32[]{:S(2)}) collective-permute-start(bf16[384,1024]{1,0:T(8,128)(2,1)S(1)} %convolution_convert_fusion), channel_id=1, source_target_pairs={{0,16},{8,24},{16,0},{24,8},{1,17},{9,25},{17,1},{25,9},{2,18},{10... | collective-permute-start | bytes 2359304 | tf_op jit(solution)/shard_map/ppermute | solution.py:39
  358.2 53.6 %collective-permute-start.54 = (bf16[272,768]{1,0:T(8,128)(2,1)S(1)}, bf16[272,768]{1,0:T(8,128)(2,1)S(1)}, u32[]{:S(2)}, u32[]{:S(2)}) collective-permute-start(bf16[272,768]{1,0:T(8,128)(2,1)S(1)} %fusion.16), channel_id=1, source_target_pairs={{0,6},{2,0},{4,2},{6,4},{1,7},{3,1},{5,3},{7,5},{8,14},{10,8},{12,... | collective-permute-start | bytes 1253384 | tf_op jit(solution)/shard_map/ppermute | solution.py:49
  361.4 26.6 %collective-permute-start.47 = (bf16[256,768]{1,0:T(8,128)(2,1)S(1)}, bf16[256,768]{1,0:T(8,128)(2,1)S(1)}, u32[]{:S(2)}, u32[]{:S(2)}) collective-permute-start(bf16[256,768]{1,0:T(8,128)(2,1)S(1)} %fusion.68), channel_id=1, source_target_pairs={{0,1},{1,0},{2,3},{3,2},{4,5},{5,4},{6,7},{7,6},{8,9},{9,8},{10,11... | collective-permute-start | bytes 1179656 | tf_op jit(solution)/shard_map/ppermute | solution.py:44
  383.2 58.3 %collective-permute-start.57 = (bf16[272,768]{1,0:T(8,128)(2,1)S(1)}, bf16[272,768]{1,0:T(8,128)(2,1)S(1)}, u32[]{:S(2)}, u32[]{:S(2)}) collective-permute-start(bf16[272,768]{1,0:T(8,128)(2,1)S(1)} %fusion.15), channel_id=1, source_target_pairs={{0,4},{2,6},{4,0},{6,2},{1,5},{3,7},{5,1},{7,3},{8,12},{10,14},{12... | collective-permute-start | bytes 1253384 | tf_op jit(solution)/shard_map/ppermute | solution.py:49
  389.2 52.5 %collective-permute-start.60 = (bf16[272,768]{1,0:T(8,128)(2,1)S(1)}, bf16[272,768]{1,0:T(8,128)(2,1)S(1)}, u32[]{:S(2)}, u32[]{:S(2)}) collective-permute-start(bf16[272,768]{1,0:T(8,128)(2,1)S(1)} %fusion.14), channel_id=1, source_target_pairs={{0,2},{2,4},{4,6},{6,0},{1,3},{3,5},{5,7},{7,1},{8,10},{10,12},{12... | collective-permute-start | bytes 1253384 | tf_op jit(solution)/shard_map/ppermute | solution.py:49
  401.8 39.7 %collective-permute-start.89 = (bf16[192,768]{1,0:T(8,128)(2,1)S(1)}, bf16[192,768]{1,0:T(8,128)(2,1)S(1)}, u32[]{:S(2)}, u32[]{:S(2)}) collective-permute-start(bf16[192,768]{1,0:T(8,128)(2,1)S(1)} %collective-permute-done.88), channel_id=1, source_target_pairs={{0,2},{2,4},{4,6},{6,0},{1,3},{3,5},{5,7},{7,1},{8,10},{10,12},{12... | collective-permute-start | bytes 884744 | tf_op jit(solution)/shard_map/ppermute | solution.py:49
  410.6 199.3 %collective-permute-start.21 = (bf16[256,768]{1,0:T(8,128)(2,1)}, bf16[256,768]{1,0:T(8,128)(2,1)}, u32[]{:S(2)}, u32[]{:S(2)}) collective-permute-start(bf16[256,768]{1,0:T(8,128)(2,1)} %fusion.65), channel_id=1, source_target_pairs={{0,1},{1,0},{2,3},{3,2},{4,5},{5,4},{6,7},{7,6},{8,9},{9,8},{10,11... | collective-permute-start | bytes 1179656 | tf_op jit(solution)/shard_map/ppermute | solution.py:44
  411.8 89.2 %collective-permute-start.93 = (bf16[2,192,1024]{2,1,0:T(8,128)(2,1)}, bf16[2,192,1024]{2,1,0:T(8,128)(2,1)}, u32[]{:S(2)}, u32[]{:S(2)}) collective-permute-start(bf16[2,192,1024]{2,1,0:T(8,128)(2,1)} %maximum_select_fusion.23), channel_id=1, source_target_pairs={{0,2},{2,4},{4,6},{6,0},{1,3},{3,5},{5,7},{7,1},{8,10},{10,12},{12... | collective-permute-start | bytes 2359304 | tf_op jit(solution)/shard_map/ppermute | solution.py:49
  441.5 59.5 %collective-permute-start.98 = (bf16[2,192,1024]{2,1,0:T(8,128)(2,1)}, bf16[2,192,1024]{2,1,0:T(8,128)(2,1)}, u32[]{:S(2)}, u32[]{:S(2)}) collective-permute-start(bf16[2,192,1024]{2,1,0:T(8,128)(2,1)} %maximum_select_fusion.25), channel_id=1, source_target_pairs={{0,2},{2,4},{4,6},{6,0},{1,3},{3,5},{5,7},{7,1},{8,10},{10,12},{12... | collective-permute-start | bytes 2359304 | tf_op jit(solution)/shard_map/ppermute | solution.py:49
  441.5 28.7 %collective-permute-start.90 = (bf16[192,768]{1,0:T(8,128)(2,1)S(1)}, bf16[192,768]{1,0:T(8,128)(2,1)S(1)}, u32[]{:S(2)}, u32[]{:S(2)}) collective-permute-start(bf16[192,768]{1,0:T(8,128)(2,1)S(1)} %collective-permute-done.89), channel_id=1, source_target_pairs={{0,2},{2,4},{4,6},{6,0},{1,3},{3,5},{5,7},{7,1},{8,10},{10,12},{12... | collective-permute-start | bytes 884744 | tf_op jit(solution)/shard_map/ppermute | solution.py:49
  453.7 55.3 %collective-permute-start.103 = (bf16[2,192,1024]{2,1,0:T(8,128)(2,1)}, bf16[2,192,1024]{2,1,0:T(8,128)(2,1)}, u32[]{:S(2)}, u32[]{:S(2)}) collective-permute-start(bf16[2,192,1024]{2,1,0:T(8,128)(2,1)} %maximum_select_fusion.27), channel_id=1, source_target_pairs={{0,2},{2,4},{4,6},{6,0},{1,3},{3,5},{5,7},{7,1},{8,10},{10,12},{12... | collective-permute-start | bytes 2359304 | tf_op jit(solution)/shard_map/ppermute | solution.py:49
  501.0 67.2 %collective-permute-start.94 = (bf16[2,192,1024]{2,1,0:T(8,128)(2,1)}, bf16[2,192,1024]{2,1,0:T(8,128)(2,1)}, u32[]{:S(2)}, u32[]{:S(2)}) collective-permute-start(bf16[2,192,1024]{2,1,0:T(8,128)(2,1)} %collective-permute-done.93), channel_id=1, source_target_pairs={{0,2},{2,4},{4,6},{6,0},{1,3},{3,5},{5,7},{7,1},{8,10},{10,12},{12... | collective-permute-start | bytes 2359304 | tf_op jit(solution)/shard_map/ppermute | solution.py:49
  501.0 94.5 %collective-permute-start.99 = (bf16[2,192,1024]{2,1,0:T(8,128)(2,1)}, bf16[2,192,1024]{2,1,0:T(8,128)(2,1)}, u32[]{:S(2)}, u32[]{:S(2)}) collective-permute-start(bf16[2,192,1024]{2,1,0:T(8,128)(2,1)} %collective-permute-done.98), channel_id=1, source_target_pairs={{0,2},{2,4},{4,6},{6,0},{1,3},{3,5},{5,7},{7,1},{8,10},{10,12},{12... | collective-permute-start | bytes 2359304 | tf_op jit(solution)/shard_map/ppermute | solution.py:49
  565.1 29.9 %collective-permute-start.66 = (bf16[256,768]{1,0:T(8,128)(2,1)S(1)}, bf16[256,768]{1,0:T(8,128)(2,1)S(1)}, u32[]{:S(2)}, u32[]{:S(2)}) collective-permute-start(bf16[256,768]{1,0:T(8,128)(2,1)S(1)} %fusion.33), channel_id=1, source_target_pairs={{2,0},{4,2},{6,4},{3,1},{5,3},{7,5},{10,8},{12,10},{14,12},{11,9},... | collective-permute-start | bytes 1179656 | tf_op jit(solution)/shard_map/ppermute | solution.py:55
  568.3 30.4 %collective-permute-start.104 = (bf16[2,192,1024]{2,1,0:T(8,128)(2,1)}, bf16[2,192,1024]{2,1,0:T(8,128)(2,1)S(1)}, u32[]{:S(2)}, u32[]{:S(2)}) collective-permute-start(bf16[2,192,1024]{2,1,0:T(8,128)(2,1)} %collective-permute-done.103), channel_id=1, source_target_pairs={{0,2},{2,4},{4,6},{6,0},{1,3},{3,5},{5,7},{7,1},{8,10},{10,12},{12... | collective-permute-start | bytes 2359304 | tf_op jit(solution)/shard_map/ppermute | solution.py:49
  574.2 82.4 %collective-permute-start.32 = (bf16[256,768]{1,0:T(8,128)(2,1)S(1)}, bf16[256,768]{1,0:T(8,128)(2,1)S(1)}, u32[]{:S(2)}, u32[]{:S(2)}) collective-permute-start(bf16[256,768]{1,0:T(8,128)(2,1)S(1)} %copy-done.71), channel_id=1, source_target_pairs={{0,6},{2,0},{4,2},{6,4},{1,7},{3,1},{5,3},{7,5},{8,14},{10,8},{12,... | collective-permute-start | bytes 1179656 | tf_op jit(solution)/shard_map/ppermute | solution.py:49
  598.6 62.9 %collective-permute-start.40 = (bf16[256,768]{1,0:T(8,128)(2,1)S(1)}, bf16[256,768]{1,0:T(8,128)(2,1)S(1)}, u32[]{:S(2)}, u32[]{:S(2)}) collective-permute-start(bf16[256,768]{1,0:T(8,128)(2,1)S(1)} %copy-done.72), channel_id=1, source_target_pairs={{0,4},{2,6},{4,0},{6,2},{1,5},{3,7},{5,1},{7,3},{8,12},{10,14},{12... | collective-permute-start | bytes 1179656 | tf_op jit(solution)/shard_map/ppermute | solution.py:49
  602.6 60.4 %collective-permute-start.48 = (bf16[256,768]{1,0:T(8,128)(2,1)S(1)}, bf16[256,768]{1,0:T(8,128)(2,1)S(1)}, u32[]{:S(2)}, u32[]{:S(2)}) collective-permute-start(bf16[256,768]{1,0:T(8,128)(2,1)S(1)} %copy-done.73), channel_id=1, source_target_pairs={{0,2},{2,4},{4,6},{6,0},{1,3},{3,5},{5,7},{7,1},{8,10},{10,12},{12... | collective-permute-start | bytes 1179656 | tf_op jit(solution)/shard_map/ppermute | solution.py:49
  607.4 74.0 %collective-permute-start.95 = (bf16[2,192,1024]{2,1,0:T(8,128)(2,1)}, bf16[2,192,1024]{2,1,0:T(8,128)(2,1)S(1)}, u32[]{:S(2)}, u32[]{:S(2)}) collective-permute-start(bf16[2,192,1024]{2,1,0:T(8,128)(2,1)} %collective-permute-done.94), channel_id=1, source_target_pairs={{0,2},{2,4},{4,6},{6,0},{1,3},{3,5},{5,7},{7,1},{8,10},{10,12},{12... | collective-permute-start | bytes 2359304 | tf_op jit(solution)/shard_map/ppermute | solution.py:49
  609.9 46.7 %collective-permute-start.79 = (f32[8,768]{1,0:T(8,128)S(1)}, f32[8,768]{1,0:T(8,128)S(1)}, u32[]{:S(2)}, u32[]{:S(2)}) collective-permute-start(f32[8,768]{1,0:T(8,128)S(1)} %add.567), channel_id=1, source_target_pairs={{0,2},{2,0},{4,6},{6,4},{1,3},{3,1},{5,7},{7,5},{8,10},{10,8},{12,... | collective-permute-start | bytes 73736 | tf_op jit(solution)/shard_map/ppermute | solution.py:79
  656.6 27.2 %collective-permute-start.100 = (bf16[2,192,1024]{2,1,0:T(8,128)(2,1)}, bf16[2,192,1024]{2,1,0:T(8,128)(2,1)S(1)}, u32[]{:S(2)}, u32[]{:S(2)}) collective-permute-start(bf16[2,192,1024]{2,1,0:T(8,128)(2,1)} %collective-permute-done.99), channel_id=1, source_target_pairs={{0,2},{2,4},{4,6},{6,0},{1,3},{3,5},{5,7},{7,1},{8,10},{10,12},{12... | collective-permute-start | bytes 2359304 | tf_op jit(solution)/shard_map/ppermute | solution.py:49
  656.6 30.4 %collective-permute-start.105 = (bf16[2,192,1024]{2,1,0:T(8,128)(2,1)S(1)}, bf16[2,192,1024]{2,1,0:T(8,128)(2,1)S(1)}, u32[]{:S(2)}, u32[]{:S(2)}) collective-permute-start(bf16[2,192,1024]{2,1,0:T(8,128)(2,1)S(1)} %collective-permute-done.104), channel_id=1, source_target_pairs={{0,2},{2,4},{4,6},{6,0},{1,3},{3,5},{5,7},{7,1},{8,10},{10,12},{12... | collective-permute-start | bytes 2359304 | tf_op jit(solution)/shard_map/ppermute | solution.py:49
  661.4 23.7 %collective-permute-start.69 = (bf16[192,1536]{1,0:T(8,128)(2,1)S(1)}, bf16[192,1536]{1,0:T(8,128)(2,1)S(1)}, u32[]{:S(2)}, u32[]{:S(2)}) collective-permute-start(bf16[192,1536]{1,0:T(8,128)(2,1)S(1)} %fusion.43), channel_id=1, source_target_pairs={{0,16},{8,24},{16,0},{24,8},{1,17},{9,25},{17,1},{25,9},{2,18},{10... | collective-permute-start | bytes 1769480 | tf_op jit(solution)/shard_map/ppermute | solution.py:39
  (150 other events, 1461.7 us)

commit v2 on v1

v2 whole, which is shorter than its diff:
```python
import functools

import jax
import jax.numpy as jnp
from jax import lax
from jax.experimental import pallas as pl
from jax.experimental.pallas import tpu as pltpu
from jax.sharding import PartitionSpec as P

HD = 64
WINDOW = 1024
EPS = 1e-06
F32 = jnp.float32
BF16 = jnp.bfloat16
VMEM_BYTES = 56 * 1024 * 1024
COST_SCALE = 0.25


def dot(left, right):
    return lax.dot_general(left, right, (((1,), (0,)), ((), ())), preferred_element_type=F32)


def dot_nt(left, right):
    return lax.dot_general(left, right, (((1,), (1,)), ((), ())), preferred_element_type=F32)


def dot_tn(left, right):
    return lax.dot_general(left, right, (((0,), (0,)), ((), ())), preferred_element_type=F32)


def core_swap(block):
    size = lax.axis_size("fsdp")
    return lax.ppermute(block, "fsdp", [(i, i ^ 1) for i in range(size)])


def pair_shift(block, distance):
    size = lax.axis_size("fsdp")
    pairs = size // 2
    route = [(i, ((i // 2 + distance) % pairs) * 2 + i % 2) for i in range(size)]
    return lax.ppermute(block, "fsdp", route)


def tp_shift(block, distance):
    size = lax.axis_size("tp")
    return lax.ppermute(block, "tp", [(i, (i + distance) % size) for i in range(size)])


def ctx_shift(block, distance):
    size = lax.axis_size("ctx")
    return lax.ppermute(block, "ctx", [(i, (i + distance) % size) for i in range(size)])


def ctx_swap(block):
    size = lax.axis_size("ctx")
    return lax.ppermute(block, "ctx", [(i, i ^ 1) for i in range(size)])


def ctx_open(block, distance):
    size = lax.axis_size("ctx")
    route = [(i, i + distance) for i in range(size) if 0 <= i + distance < size]
    return lax.ppermute(block, "ctx", route)


def pick(stack, index):
    return lax.dynamic_index_in_dim(stack, index, 0, keepdims=False)


def place_rows(pieces, me):
    first, second = pieces
    return jnp.where(
        me == 0, jnp.stack([first, second], axis=1), jnp.stack([second, first], axis=1))


def place(pieces, me):
    count = len(pieces)
    if count == 1:
        return pieces[0][None]
    if count == 2:
        first, second = pieces
        return jnp.where(me == 0, jnp.stack([first, second]), jnp.stack([second, first]))
    result = jnp.zeros((count,) + pieces[0].shape, pieces[0].dtype)
    for d, piece in enumerate(pieces):
        result = lax.dynamic_update_index_in_dim(result, piece, (me - d) % count, 0)
    return result


def tie(values, *others):
    return lax.optimization_barrier((values, others))[0]


class Phases:
    def __init__(self):
        self.last = []

    def run(self, function, *values):
        given = function(*(tie(values, self.last) if self.last else values))
        self.last = jax.tree.leaves(given)
        return given


def all_sum(block, axis):
    size = lax.axis_size(axis)
    reach = 1
    while reach < size:
        other = lax.ppermute(block, axis, [(i, i ^ reach) for i in range(size)])
        block = block + other
        reach *= 2
    return block


def whole(shape):
    return pl.BlockSpec(shape, lambda *_: (0,) * len(shape))


def params():
    return pltpu.CompilerParams(vmem_limit_bytes=VMEM_BYTES)


def cost(microseconds):
    return pl.CostEstimate(flops=0, bytes_accessed=int(microseconds * COST_SCALE * 3.4e6), transcendentals=0)


def swap_halves(values):
    width = values.shape[-1]
    lane = lax.broadcasted_iota(jnp.int32, values.shape, 1)
    up = pltpu.roll(values, width - HD // 2, 1)
    down = pltpu.roll(values, HD // 2, 1)
    return jnp.where(lane % HD < HD // 2, up, down)


def widen(table, width):
    copies = -(-width // table.shape[1])
    return jnp.concatenate([table] * copies, axis=1)[:, :width]


def project_kernel(with_query, count, *refs):
    sources = refs[:count]
    gain_ref, w_ref, cos_ref, sin_ref = refs[count : count + 4]
    hid_ref, k_ref, v_ref = refs[len(refs) - 3 - with_query :][:3]
    width = k_ref.shape[1]
    cosine = widen(cos_ref[...], width)
    sine = widen(sin_ref[...], width)
    for i, tok_ref in enumerate(sources):

        @pl.when(pl.program_id(0) == i)
        def _():
            inputs = tok_ref[...].astype(F32)
            scale = lax.rsqrt(jnp.mean(inputs * inputs, axis=-1, keepdims=True) + EPS)
            hidden = (inputs * scale * gain_ref[...]).astype(BF16)
            hid_ref[...] = hidden
            keys = dot(hidden, w_ref[:, :width])
            k_ref[...] = (keys * cosine + swap_halves(keys) * sine).astype(BF16)
            v_ref[...] = dot(hidden, w_ref[:, width : 2 * width]).astype(BF16)
            if with_query and i == count - 1:
                query = dot(hidden, w_ref[:, 2 * width : 3 * width])
                turned = (query * cosine + swap_halves(query) * sine).astype(BF16)
                refs[-1][...] = turned * jnp.asarray(HD**-0.5, BF16)


def project(sources, gain, weights, cosine, sine, width, blocks, first, saved):
    rows, features = sources[0].shape
    count = len(sources)
    with_query = first + count == blocks
    shapes = [(blocks * rows, features), (blocks * rows, width), (blocks * rows, width)]
    outs = [jax.ShapeDtypeStruct(shape, BF16) for shape in shapes]
    specs = [pl.BlockSpec((rows, shape[1]), lambda i: (i + first, 0)) for shape in shapes]
    if with_query:
        outs.append(jax.ShapeDtypeStruct((rows, width), BF16))
        specs.append(whole((rows, width)))
    table = pl.BlockSpec((rows, cosine.shape[1]), lambda i: (i + first, 0))
    return pl.pallas_call(
        functools.partial(project_kernel, with_query, count),
        grid=(count,),
        in_specs=[whole(source.shape) for source in sources]
        + [whole(gain.shape), whole(weights.shape), table, table]
        + [pl.BlockSpec(memory_space=pl.ANY)] * len(saved),
        out_specs=specs,
        out_shape=outs,
        input_output_aliases={count + 4 + i: i for i in range(len(saved))},
        compiler_params=params(),
        cost_estimate=cost(1 + 3 * count),
    )(*sources, gain, weights, cosine, sine, *saved)


def mask_bias(kseg, qseg, keys, queries):
    key = lax.broadcasted_iota(jnp.int32, (keys, queries), 0)
    query = lax.broadcasted_iota(jnp.int32, (keys, queries), 1)
    allowed = (key > query) & (key <= query + WINDOW) & (kseg == qseg)
    return jnp.where(allowed, 0.0, -1e30).astype(F32)


def head_only(values, head):
    lane = lax.broadcasted_iota(jnp.int32, values.shape, 1)
    return jnp.where(lane // HD == head, values, jnp.zeros_like(values))


def attend_kernel(tile, q_ref, k_ref, v_ref, kseg_ref, qseg_ref, out_ref, lse_ref, bias_ref):
    rows = q_ref.shape[0]
    span = WINDOW + tile
    tiles = rows // tile

    @pl.when(pl.program_id(0) == 0)
    def _():
        for j in range(tiles):
            bias_ref[j] = mask_bias(
                kseg_ref[pl.ds(j * tile, span), :], qseg_ref[:, pl.ds(j * tile, tile)], span, tile
            )

    keys = k_ref[...]
    values_t = v_ref[...].T
    for j in range(tiles):
        start = j * tile
        query = q_ref[pl.ds(start, tile), :]
        parts = []
        for head in range(2):
            scores = dot_nt(keys[start : start + span], head_only(query, head)) + bias_ref[j]
            top = jnp.max(scores, axis=0, keepdims=True)
            expo = jnp.exp(scores - top)
            total = jnp.sum(expo, axis=0, keepdims=True)
            part = dot(
                values_t[head * HD : (head + 1) * HD, start : start + span], expo.astype(BF16)
            )
            parts.append(part / total)
            lse_ref[0, pl.ds(head, 1), pl.ds(start, tile)] = top + jnp.log(total)
        out_ref[pl.ds(start, tile), :] = jnp.concatenate(parts, axis=0).T.astype(BF16)


def attend(query, keys, values, kseg, qseg):
    rows, width = query.shape
    span = keys.shape[0]
    tile = min(256, rows)
    pairs = -(-width // (2 * HD))
    columns = lambda count: pl.BlockSpec((count, 2 * HD), lambda i: (0, i))
    return pl.pallas_call(
        functools.partial(attend_kernel, tile),
        grid=(pairs,),
        in_specs=[columns(rows), columns(span), columns(span), whole((span, 1)), whole((1, rows))],
        out_specs=[columns(rows), pl.BlockSpec((1, 2, rows), lambda i: (i, 0, 0))],
        out_shape=[
            jax.ShapeDtypeStruct((rows, width), BF16),
            jax.ShapeDtypeStruct((pairs, 2, rows), F32),
        ],
        scratch_shapes=[pltpu.VMEM((rows // tile, WINDOW + tile, tile), F32)],
        compiler_params=params(),
        cost_estimate=cost(13),
    )(query, keys, values, kseg, qseg)


def attend_back_kernel(
    tile, q_ref, k_ref, v_ref, g_ref, lse_ref, kseg_ref, qseg_ref, cos_ref, sin_ref,
    dq_ref, dk_ref, dv_ref, bias_ref, dk_acc, dv_acc,
):
    rows = q_ref.shape[0]
    span = WINDOW + tile
    tiles = rows // tile
    total_keys = k_ref.shape[0]

    @pl.when(pl.program_id(0) == 0)
    def _():
        for j in range(tiles):
            bias_ref[j] = mask_bias(
                kseg_ref[pl.ds(j * tile, span), :], qseg_ref[:, pl.ds(j * tile, tile)], span, tile
            )

    keys = k_ref[...]
    values = v_ref[...]
    keys_t = keys.T
    dk_acc[...] = jnp.zeros_like(dk_acc)
    dv_acc[...] = jnp.zeros_like(dv_acc)
    cosine = cos_ref[...]
    sine = sin_ref[...]
    lead = total_keys - rows
    for j in range(tiles):
        start = j * tile
        query = q_ref[pl.ds(start, tile), :]
        grad = g_ref[pl.ds(start, tile), :]
        parts = []
        for head in range(2):
            query_one = head_only(query, head)
            grad_one = head_only(grad, head)
            scores = dot_nt(keys[start : start + span], query_one) + bias_ref[j]
            probs = jnp.exp(scores - lse_ref[0, pl.ds(head, 1), pl.ds(start, tile)])
            grad_probs = dot_nt(values[start : start + span], grad_one)
            delta = jnp.sum(probs * grad_probs, axis=0, keepdims=True)
            grad_scores = (probs * (grad_probs - delta)).astype(BF16)
            dv_acc[pl.ds(start, span), :] += dot(probs.astype(BF16), grad_one)
            dk_acc[pl.ds(start, span), :] += dot(grad_scores, query_one)
            parts.append(
                dot(keys_t[head * HD : (head + 1) * HD, start : start + span], grad_scores)
            )
        dq = jnp.concatenate(parts, axis=0).T * HD**-0.5
        places = pl.ds(lead + start, tile)
        dq_ref[pl.ds(start, tile), :] = (
            dq * cos_ref[places, :] - swap_halves(dq) * sin_ref[places, :]
        ).astype(BF16)
    dk = dk_acc[...]
    dk_ref[...] = (dk * cosine - swap_halves(dk) * sine).astype(BF16)
    dv_ref[...] = dv_acc[...].astype(BF16)


def attend_back(query, keys, values, grad, lse, kseg, qseg, cosine, sine):
    rows, width = query.shape
    span = keys.shape[0]
    tile = min(256, rows)
    pairs = -(-width // (2 * HD))
    columns = lambda count: pl.BlockSpec((count, 2 * HD), lambda i: (0, i))
    return pl.pallas_call(
        functools.partial(attend_back_kernel, tile),
        grid=(pairs,),
        in_specs=[
            columns(rows), columns(span), columns(span), columns(rows),
            pl.BlockSpec((1, 2, rows), lambda i: (i, 0, 0)),
            whole((span, 1)), whole((1, rows)), whole((span, 2 * HD)), whole((span, 2 * HD)),
        ],
        out_specs=[columns(rows), columns(span), columns(span)],
        out_shape=[
            jax.ShapeDtypeStruct((rows, width), BF16),
            jax.ShapeDtypeStruct((span, width), BF16),
            jax.ShapeDtypeStruct((span, width), BF16),
        ],
        scratch_shapes=[
            pltpu.VMEM((rows // tile, WINDOW + tile, tile), F32),
            pltpu.VMEM((span, 2 * HD), F32),
            pltpu.VMEM((span, 2 * HD), F32),
        ],
        compiler_params=params(),
        cost_estimate=cost(18),
    )(query, keys, values, grad, lse, kseg, qseg, cosine, sine)


def expert_kernel(capacity, parts, experts, full, steps, n_saved, meta_ref, *refs):
    if full:
        count = steps * parts
        x_refs, c_refs, refs = refs[:count], refs[count : 2 * count], refs[2 * count :]
        w_ref, rt_ref = refs[:2]
        refs = refs[2 + n_saved :]
        dx_ref, sx_ref, sr_ref, sh_ref, sa_ref, sb_ref = refs[:6]
        ssx_ref, ssc_ref, ssh_ref, ssa_ref, ssb_ref, out_ref, x_all, c_all, t_all = refs[6:]
        tok, width = x_all.shape[1:]
        lane = meta_ref[1 + steps]
        for j in range(parts):
            spot = lax.rem(lane + parts - j, parts)
            for i in range(steps):

                @pl.when(pl.program_id(0) == i)
                def _():
                    x_all[spot] = x_refs[i * parts + j][...]
                    c_all[spot] = c_refs[i * parts + j][:tok]
                    if j == 0:
                        t_all[...] = c_refs[i * parts][tok:]

        block = tok * parts
        inputs = x_all[...].reshape(block, width)
        cot = c_all[...].reshape(block, width)
        low_table = t_all[...]
        ssx_ref[0] = inputs
        ssc_ref[0, :block] = cot
        ssc_ref[0, block:] = low_table
    else:
        x_ref, c_ref, w_ref, rt_ref = refs[:4]
        sx_ref, sr_ref, sh_ref, sa_ref, sb_ref = refs[4 + n_saved :]
        block, width = x_ref.shape[1:]
        tok = block // parts
        inputs = x_ref[0]
        cot = c_ref[0, :block]
        low_table = c_ref[0, block:]
    hidden = w_ref.shape[3]
    owned = sx_ref.shape[1]
    table = low_table[:, :block].astype(F32)[:experts]

    def weights(which):
        return w_ref[:, which].reshape(width, hidden)

    logits = dot_nt(rt_ref[...], inputs)[:experts]
    named = table >= 0.0
    top = jnp.max(jnp.where(named, logits, -1e30), axis=0, keepdims=True)
    expo = jnp.where(named, jnp.exp(logits - top), 0.0)
    gates = expo / jnp.sum(expo, axis=0, keepdims=True)
    row = lax.broadcasted_iota(jnp.int32, (experts, block), 0)
    slot = lax.broadcasted_iota(jnp.int32, (capacity, block), 0).astype(F32)
    hits, spreads, gate_slots = [], [], []
    for j in range(owned):
        mine = row == meta_ref[0] + j
        gate = jnp.sum(jnp.where(mine, gates, 0.0), axis=0, keepdims=True)
        position = jnp.sum(jnp.where(mine, table, 0.0), axis=0, keepdims=True)
        hit = slot == position
        hits.append(hit)
        spreads.append(jnp.where(hit, 1.0, 0.0).astype(BF16))
        gate_slots.append(jnp.sum(jnp.where(hit, gate, 0.0), axis=1, keepdims=True))
    spread = jnp.concatenate(spreads, axis=0)
    routed = dot(spread, inputs).astype(BF16)
    cots = dot(spread, cot)
    gate_slots = jnp.concatenate(gate_slots, axis=0)
    grads = (gate_slots * cots).astype(BF16)

    def branch(left, right, gate_weights, up_weights, down_weights):
        gating = dot(left, gate_weights)
        linear = dot(left, up_weights)
        sigma = jax.nn.sigmoid(gating)
        silu = gating * sigma
        active = (silu * linear).astype(BF16)
        grad_active = dot(right, down_weights)
        slope = sigma * (1.0 + gating * (1.0 - sigma))
        grad_gating = (grad_active * linear * slope).astype(BF16)
        grad_linear = (grad_active * silu).astype(BF16)
        if not full:
            return active, grad_gating, grad_linear
        result = dot_nt(active, down_weights)
        grad_left = dot_nt(grad_gating, gate_weights) + dot_nt(grad_linear, up_weights)
        return active, grad_gating, grad_linear, result, grad_left

    weighted = []
    gate_lines = []
    for j in range(owned):
        rows = slice(j * capacity, (j + 1) * capacity)
        sx_ref[0, j] = routed[rows]
        sr_ref[0, j] = grads[rows]
        got = branch(
            routed[rows], grads[rows], weights(j), weights(owned + j), weights(2 * owned + j))
        sh_ref[0, j], sa_ref[0, j], sb_ref[0, j] = got[:3]
        if full:
            result, grad_left = got[3:]
            grad_gates = jnp.sum(result * cots[rows], axis=1, keepdims=True)
            gate_lines.append(jnp.sum(jnp.where(hits[j], grad_gates, 0.0), axis=0, keepdims=True))
            weighted.append(jnp.concatenate(
                [(gate_slots[rows] * result).astype(BF16), grad_left.astype(BF16)], axis=1))
    if not full:
        return
    back = dot_tn(spread, jnp.concatenate(weighted, axis=0))

    units = ssh_ref.shape[2]
    common = weights(3 * owned)
    active, grad_gating, grad_linear, result, grad_left = branch(
        inputs, cot, common[:, :units], common[:, units : 2 * units], common[:, 2 * units : 3 * units])
    ssh_ref[0] = active
    ssa_ref[0] = grad_gating
    ssb_ref[0] = grad_linear
    out = back[:, :width] + result
    dx = back[:, width:] + grad_left
    line = lax.broadcasted_iota(jnp.int32, (16, width), 0)
    for j in range(parts):
        piece = slice(j * tok, (j + 1) * tok)
        out_ref[0, j] = out[piece].astype(BF16)
        dx_ref[0, j, :tok] = dx[piece].astype(BF16)
        spare = jnp.zeros((1, width - tok), F32)
        extra = jnp.zeros((16, width), F32)
        for i in range(owned):
            padded = jnp.concatenate([gate_lines[i][:, piece], spare], axis=1)
            extra = jnp.where(line == meta_ref[0] + i, padded, extra)
        dx_ref[0, j, tok:] = extra.astype(BF16)


def expert_shapes(owned, capacity, width, hidden):
    return [(owned, capacity, width)] * 2 + [(owned, capacity, hidden)] * 3


def placed(shape, where):
    return pl.BlockSpec((1,) + shape, lambda i, meta: (where(i, meta),) + (0,) * len(shape))


def expert_blocks(first, blocks, capacity, experts, units, meta, x_pieces, c_pieces, weights, router_t, saved):
    steps, parts = len(x_pieces), len(x_pieces[0])
    tok, width = x_pieces[0][0].shape
    block = tok * parts
    hidden = weights.shape[3]
    owned = weights.shape[1] // 3
    shapes = expert_shapes(owned, capacity, width, hidden)
    shapes += [(block, width), (block + 16, width), (block, units), (block, units), (block, units), (parts, tok, width)]
    here = lambda i, meta: first + i
    at_place = lambda i, meta: meta[1 + i]
    dx_shape = (parts, tok + 16, width)
    outs = [jax.ShapeDtypeStruct((steps,) + dx_shape, BF16)]
    outs += [jax.ShapeDtypeStruct((blocks,) + shape, BF16) for shape in shapes]
    specs = [placed(dx_shape, lambda i, meta: i)] + [placed(shape, here) for shape in shapes[:-1]]
    specs.append(placed(shapes[-1], at_place))
    xs = [piece for pieces in x_pieces for piece in pieces]
    operands = xs + [piece for pieces in c_pieces for piece in pieces] + [weights, router_t]
    in_specs = [whole(one.shape) for one in operands]
    in_specs += [pl.BlockSpec(memory_space=pl.ANY)] * len(saved)
    return pl.pallas_call(
        functools.partial(expert_kernel, capacity, parts, experts, True, steps, len(saved)),
        grid_spec=pltpu.PrefetchScalarGridSpec(
            num_scalar_prefetch=1,
            grid=(steps,),
            in_specs=in_specs,
            out_specs=specs,
            scratch_shapes=[pltpu.VMEM((parts, tok, width), BF16)] * 2 + [pltpu.VMEM((16, width), BF16)],
        ),
        out_shape=outs,
        input_output_aliases={1 + len(operands) + i: 1 + i for i in range(len(saved))},
        compiler_params=params(),
        cost_estimate=cost(13 * steps),
    )(meta, *operands, *saved)


def expert_again(d, capacity, parts, experts, meta, inputs, cots, weights, router_t, saved):
    blocks, block, width = inputs.shape
    hidden = weights.shape[3]
    shapes = expert_shapes(weights.shape[1] // 3, capacity, width, hidden)
    here = lambda i, meta: d
    return pl.pallas_call(
        functools.partial(expert_kernel, capacity, parts, experts, False, 1, len(saved)),
        grid_spec=pltpu.PrefetchScalarGridSpec(
            num_scalar_prefetch=1,
            grid=(1,),
            in_specs=[placed(inputs.shape[1:], here), placed(cots.shape[1:], here)]
            + [whole(weights.shape), whole(router_t.shape)]
            + [pl.BlockSpec(memory_space=pl.ANY)] * len(saved),
            out_specs=[placed(shape, here) for shape in shapes],
        ),
        out_shape=[jax.ShapeDtypeStruct((blocks,) + shape, BF16) for shape in shapes],
        input_output_aliases={5 + i: i for i in range(len(saved))},
        compiler_params=params(),
        cost_estimate=cost(9),
    )(meta, inputs, cots, weights, router_t, *saved)


def split_rows(value, core, sent_ref, kept_ref, *at):
    pairs = sent_ref.shape[0]
    share = value.shape[0] // (2 * pairs)
    for q in range(pairs):
        first = value[2 * q * share : (2 * q + 1) * share].astype(BF16)
        second = value[(2 * q + 1) * share : (2 * q + 2) * share].astype(BF16)
        index = (q,) + at
        kept_ref[index] = jnp.where(core == 0, first, second)
        sent_ref[index] = jnp.where(core == 0, second, first)


def weight_kernel(core_ref, left_ref, right_ref, sent_ref, kept_ref):
    steps, _, slots, rows = left_ref.shape
    left = left_ref[...].reshape(steps * slots, rows)
    right = right_ref[...].reshape(steps * slots, right_ref.shape[3])
    split_rows(dot_tn(left, right), core_ref[0], sent_ref, kept_ref, 0)


def weight_grads(core, left, right, pairs):
    steps, owned, slots, width = left.shape
    columns = right.shape[3]
    share = width // (2 * pairs)
    parts = 2 if columns % 256 == 0 else 1
    wide = columns // parts
    shape = jax.ShapeDtypeStruct((pairs, owned, share, columns), BF16)
    spec = pl.BlockSpec((pairs, 1, share, wide), lambda j, i, core: (0, j, 0, i))
    return pl.pallas_call(
        weight_kernel,
        grid_spec=pltpu.PrefetchScalarGridSpec(
            num_scalar_prefetch=1,
            grid=(owned, parts),
            in_specs=[
                pl.BlockSpec((steps, 1, slots, width), lambda j, i, core: (0, j, 0, 0)),
                pl.BlockSpec((steps, 1, slots, wide), lambda j, i, core: (0, j, 0, i)),
            ],
            out_specs=[spec, spec],
        ),
        out_shape=[shape, shape],
        compiler_params=params(),
        cost_estimate=cost(6),
    )(core, left, right)


def shared_grad_kernel(core_ref, x_ref, c_ref, a_ref, b_ref, h_ref, sent_ref, kept_ref, total_ref):
    step = pl.program_id(0)
    block, units = a_ref.shape[1:]

    @pl.when(step == 0)
    def _():
        total_ref[...] = jnp.zeros_like(total_ref)

    total_ref[:, :units] += dot_tn(x_ref[0], a_ref[0])
    total_ref[:, units : 2 * units] += dot_tn(x_ref[0], b_ref[0])
    total_ref[:, 2 * units :] += dot_tn(c_ref[0, :block], h_ref[0])

    @pl.when(step == pl.num_programs(0) - 1)
    def _():
        split_rows(total_ref[...], core_ref[0], sent_ref, kept_ref)


def shared_grads(core, x, c, a, b, h, pairs):
    operands = (x, c, a, b, h)
    width, units = x.shape[2], a.shape[2]
    shape = jax.ShapeDtypeStruct((pairs, width // (2 * pairs), 3 * units), BF16)
    return pl.pallas_call(
        shared_grad_kernel,
        grid_spec=pltpu.PrefetchScalarGridSpec(
            num_scalar_prefetch=1,
            grid=(x.shape[0],),
            in_specs=[pl.BlockSpec((1,) + o.shape[1:], lambda i, core: (i, 0, 0)) for o in operands],
            out_specs=[whole(shape.shape), whole(shape.shape)],
            scratch_shapes=[pltpu.VMEM((width, 3 * units), F32)],
        ),
        out_shape=[shape, shape],
        compiler_params=params(),
        cost_estimate=cost(8),
    )(core, *operands)


def attn_grad_kernel(core_ref, hid_ref, dk_ref, dv_ref, dq_ref, gm_ref, at_ref, small_ref, sent_ref, kept_ref):
    lead = hid_ref.shape[0] - dq_ref.shape[0]
    value = jnp.concatenate(
        [
            dot_tn(hid_ref[...], dk_ref[...]),
            dot_tn(hid_ref[...], dv_ref[...]),
            dot_tn(hid_ref[lead:, :], dq_ref[...]),
            dot_tn(gm_ref[...], at_ref[...]),
            small_ref[...].T,
        ],
        axis=1,
    )
    split_rows(value, core_ref[0], sent_ref, kept_ref)


def attn_grads_of(core, hid, dk, dv, dq, grad_mixed_low, attended, small, pairs):
    width, cols = hid.shape[1], dk.shape[1]
    shape = jax.ShapeDtypeStruct((pairs, width // (2 * pairs), 4 * cols + small.shape[0]), BF16)
    operands = (hid, dk, dv, dq, grad_mixed_low, attended, small)
    return pl.pallas_call(
        attn_grad_kernel,
        grid_spec=pltpu.PrefetchScalarGridSpec(
            num_scalar_prefetch=1,
            grid=(1,),
            in_specs=[whole(o.shape) for o in operands],
            out_specs=[whole(shape.shape), whole(shape.shape)],
        ),
        out_shape=[shape, shape],
        compiler_params=params(),
        cost_estimate=cost(8),
    )(core, *operands)


def hidden_back_kernel(count, *refs):
    sources = refs[:count]
    dk_ref, dv_ref, dq_ref, w_ref, out_ref, gain_ref = refs[count:]
    cols = dk_ref.shape[1]
    step = pl.program_id(0)

    @pl.when(step == 0)
    def _():
        gain_ref[...] = jnp.zeros_like(gain_ref)

    for i, tok_ref in enumerate(sources):

        @pl.when(step == i)
        def _():
            grad = dot_nt(dk_ref[...], w_ref[:, :cols]) + dot_nt(dv_ref[...], w_ref[:, cols : 2 * cols])
            if i == count - 1:
                grad = grad + dot_nt(dq_ref[...], w_ref[:, 2 * cols : 3 * cols])
            out_ref[0] = grad.astype(BF16)
            inputs = tok_ref[...].astype(F32)
            scale = lax.rsqrt(jnp.mean(inputs * inputs, axis=-1, keepdims=True) + EPS)
            gain_ref[...] += jnp.sum(grad * (inputs * scale), axis=0, keepdims=True)


def hidden_back(sources, dk, dv, dq, weights):
    count = len(sources)
    rows, width = sources[0].shape
    cols = dk.shape[1]
    part = pl.BlockSpec((rows, cols), lambda i: (i, 0))
    return pl.pallas_call(
        functools.partial(hidden_back_kernel, count),
        grid=(count,),
        in_specs=[whole((rows, width))] * count
        + [part, part, whole((rows, cols)), whole(weights.shape)],
        out_specs=[pl.BlockSpec((1, rows, width), lambda i: (i, 0, 0)), whole((1, width))],
        out_shape=[
            jax.ShapeDtypeStruct((count, rows, width), BF16),
            jax.ShapeDtypeStruct((1, width), F32),
        ],
        compiler_params=params(),
        cost_estimate=cost(7),
    )(*sources, dk, dv, dq, weights)


def collect_kernel(turned, places_ref, first_ref, second_ref, out_ref):
    step = pl.program_id(0)
    for half, ref in enumerate((first_ref, second_ref)):

        @pl.when(step // (pl.num_programs(0) // 2) == half)
        def _():
            piece = ref[0, 0].astype(F32)
            out_ref[0] = piece.T if turned else piece


def collect(places, first, second, skip, owned, turned):
    rows, columns = first.shape[2:]
    count = 4 * owned
    half = 2 * owned
    block = (1, columns, rows) if turned else (1, rows, columns)

    def part(start, low):
        def index(i, places):
            local = jnp.clip(i - start, 0, half - 1)
            return (local // owned, low + local % owned, 0, 0)

        return pl.BlockSpec((1, 1, rows, columns), index)

    return pl.pallas_call(
        functools.partial(collect_kernel, turned),
        grid_spec=pltpu.PrefetchScalarGridSpec(
            num_scalar_prefetch=1,
            grid=(count,),
            in_specs=[part(0, skip[0]), part(half, skip[1])],
            out_specs=pl.BlockSpec(block, lambda i, places: (places[i // half] * half + i % half, 0, 0)),
        ),
        out_shape=jax.ShapeDtypeStruct((count,) + block[1:], F32),
        compiler_params=params(),
        cost_estimate=cost(5),
    )(places, first, second)


def norm_back(grad, values, scale, gain):
    grad_gain = jnp.sum(grad * values * scale, axis=0)
    scaled = grad * gain
    grad_values = scale * scaled - values * scale * scale * scale * jnp.mean(
        scaled * values, axis=-1, keepdims=True
    )
    return grad_values, grad_gain


def local(
    tokens,
    segments,
    routes,
    query_weight,
    key_weight,
    value_weight,
    out_weight,
    attn_gain,
    ffn_gain,
    router_weight,
    shared_gate,
    shared_up,
    shared_down,
    expert_gate,
    expert_up,
    expert_down,
    cotangent,
):
    fsdp, ctx, tp = (lax.axis_size(a) for a in ("fsdp", "ctx", "tp"))
    pairs = fsdp // 2
    me = lax.axis_index("fsdp")
    pair, core = me // 2, me % 2
    plane = lax.axis_index("ctx")
    lane = lax.axis_index("tp")
    tokens, cotangent, routes = tokens[0], cotangent[0], routes[0]
    block, width = tokens.shape
    share, cols = query_weight.shape
    experts = expert_gate.shape[0]
    hidden_units = expert_gate.shape[2]
    units = shared_gate.shape[1] // ctx
    owned = experts // ctx
    top_count = routes.shape[1]
    capacity = 3 * top_count * block // (2 * experts)
    tok = block // tp
    core_index = core.astype(jnp.int32)[None]

    phases = Phases()

    def to_pairs(piece):
        return [pair_shift(piece, d) for d in range(1, pairs)]

    def to_tp(piece):
        return [tp_shift(piece, j) for j in range(1, tp)]

    def joined(*pieces):
        return place(pieces, lane).reshape(block, width)

    def start(*_):
        small = jnp.concatenate(
            [router_weight, attn_gain[:, None], ffn_gain[:, None],
             jnp.zeros((share, 128 - experts - 2), BF16)], axis=1)
        attn_mine = jnp.concatenate(
            [key_weight, value_weight, query_weight, out_weight.T, small], axis=1)
        return attn_mine, lax.dynamic_slice_in_dim(tokens, lane * tok, tok, 0)

    attn_mine, tokens_mine = phases.run(start)

    def cot_rows(cotangent, plane):
        chosen = routes.T
        hits = jnp.zeros((experts, block), jnp.bool_)
        for j in range(top_count):
            hits = hits | (chosen[j : j + 1] == jnp.arange(experts, dtype=jnp.int32)[:, None])
        spot = jnp.arange(block, dtype=jnp.int32)
        before = (spot[:, None] < spot[None, :]).astype(BF16)
        rank = dot(hits.astype(BF16), before)
        table = jnp.pad(jnp.where(hits, rank, -1.0).astype(BF16), ((0, 16 - experts), (0, width - block)))
        pieces = [
            lax.dynamic_slice_in_dim(cotangent, (lane - j) % tp * tok, tok, 0) for j in range(tp)]
        return [jnp.concatenate([pieces[0], table], axis=0)] + pieces[1:], hits

    def of_plane(stack, index):
        return lax.dynamic_slice_in_dim(stack, owned * index, owned, 0)

    def experts_of(index, expert_gate, expert_up, expert_down):
        return [
            of_plane(expert_gate, index),
            of_plane(expert_up, index),
            jnp.swapaxes(of_plane(expert_down, index), 1, 2),
        ]

    at = plane * units
    other_plane = plane ^ 2

    def weight_rows(expert_gate, expert_up, expert_down):
        shared_mine = jnp.concatenate(
            [
                lax.dynamic_slice_in_dim(shared_gate, at, units, 1),
                lax.dynamic_slice_in_dim(shared_up, at, units, 1),
                lax.dynamic_slice_in_dim(shared_down, at, units, 0).T,
                jnp.zeros((share, hidden_units - 3 * units), BF16),
            ],
            axis=1,
        )
        return jnp.concatenate(experts_of(plane, expert_gate, expert_up, expert_down) + [shared_mine[None]], axis=0)

    def tables(plane):
        positions = (plane - 2) * block + jnp.arange(3 * block, dtype=jnp.int32)
        index = jnp.arange(2 * HD, dtype=jnp.int32)
        rates = 10000.0 ** (-2.0 * (index % (HD // 2)).astype(F32) / HD)
        angles = positions.astype(F32)[:, None] * rates[None, :]
        sign = jnp.where(index % HD < HD // 2, -1.0, 1.0)
        segment_pad = jnp.concatenate([jnp.full((2 * block,), -1, jnp.int32), segments[0]])
        kseg = lax.dynamic_slice_in_dim(segment_pad, plane * block, 3 * block, 0)
        return jnp.cos(angles), sign * jnp.sin(angles), kseg[:, None], kseg[2 * block :][None, :]

    def phase_first(attn_mine, tokens_mine, plane, cotangent, expert_gate, expert_up, expert_down):
        return (
            to_pairs(attn_mine), core_swap(attn_mine), ctx_open(tokens_mine, 1), tables(plane),
            cot_rows(cotangent, plane), weight_rows(expert_gate, expert_up, expert_down))

    attn_far, attn_core, prev_one_mine, attn_tables, (cot_own, hits), weights_mine = phases.run(
        phase_first, attn_mine, tokens_mine, plane, cotangent, expert_gate, expert_up, expert_down)
    cosine, sine, kseg, qseg = attn_tables
    weights = lax.all_gather(weights_mine, "fsdp", axis=0)
    cot_mine = [cot_own[0]]
    attn_far_core, prev_one_other, prev_two_mine, got = phases.run(
        lambda attn_far, prev_one_mine, cot: (
            [core_swap(one) for one in attn_far], to_tp(prev_one_mine), ctx_open(prev_one_mine, 1),
            ctx_shift(cot, -1)),
        attn_far, prev_one_mine, cot_mine[-1])
    cot_mine.append(got)

    def all_rows(mine, far, across, far_across, columns):
        same = place([mine[:, columns]] + [one[:, columns] for one in far], pair)
        other = place([across[:, columns]] + [one[:, columns] for one in far_across], pair)
        return place_rows([same, other], core).reshape(width, same.shape[2])

    def project_near(tokens, prev_one_mine, prev_one_other, prev_two_mine, cot, *attn):
        sent = to_tp(prev_two_mine), ctx_shift(cot, -1)
        qkv_full = all_rows(*attn, slice(0, 3 * cols))
        small_t = all_rows(*attn, slice(4 * cols, 4 * cols + 128))[:, :16].T
        attn_scale = small_t[experts : experts + 1].astype(F32)
        prev_one = joined(prev_one_mine, *prev_one_other)
        first = project([prev_one, tokens], attn_scale, qkv_full, cosine, sine, cols, 3, 1, [])
        return qkv_full, small_t, attn_scale, prev_one, first, sent

    qkv_full, small_t, attn_scale, prev_one, first, (prev_two_other, got) = phases.run(
        project_near, tokens, prev_one_mine, prev_one_other, prev_two_mine, cot_mine[-1],
        attn_mine, attn_far, attn_core, attn_far_core)
    cot_mine.append(got)
    query = first[3]
    half = ctx // 2
    here = [(plane + d) % ctx for d in range(ctx)]

    def attention(prev_two_mine, prev_two_other, cots, *attn):
        cot_sent = ctx_shift(cots[-1], -1), to_tp(cots[1]), to_tp(cots[2])
        prev_two = joined(prev_two_mine, *prev_two_other)
        hid, keys, values = project(
            [prev_two], attn_scale, qkv_full, cosine, sine, cols, 3, 0, first[:3])
        attended, lse = attend(query, keys, values, kseg, qseg)
        out_full = all_rows(*attn, slice(3 * cols, 4 * cols))
        router_full = all_rows(*attn, slice(4 * cols, 4 * cols + 128))[:, :experts]
        partial = dot_nt(attended, out_full).astype(BF16).reshape(tp, tok, width)
        return cot_sent, prev_two, hid, keys, values, attended, lse, out_full, router_full, partial

    cot_sent, prev_two, hid, keys, values, attended, lse, out_full, router_full, partial = phases.run(
        attention, prev_two_mine, prev_two_other, cot_mine, attn_mine, attn_far, attn_core, attn_far_core)
    cot_mine.append(cot_sent[0])
    cot_other = [cot_own[1:], cot_sent[1], cot_sent[2]]

    def sent_tp(total):
        return [tp_shift(pick(total, (lane + j) % tp), j) for j in range(1, tp)]

    def sum_tp(total, got):
        result = pick(total, lane).astype(F32)
        for one in got:
            result = result + one.astype(F32)
        return result

    partial_other = phases.run(sent_tp, partial)
    router_t = jnp.concatenate([small_t[:experts], jnp.zeros((16 - experts, width), BF16)], axis=0)
    ffn_scale = small_t[experts + 1 : experts + 2].astype(F32)
    inputs_mine = tokens_mine.astype(F32)

    def normalize(partial, got):
        mixed = inputs_mine + sum_tp(partial, got)
        scale_ffn = lax.rsqrt(jnp.mean(mixed * mixed, axis=-1, keepdims=True) + EPS)
        return (mixed * scale_ffn * ffn_scale).astype(BF16), mixed, scale_ffn

    normed_low, mixed, scale_ffn = phases.run(normalize, partial, partial_other)

    mine, other = [normed_low], []
    for d in range(1, ctx):
        got, moved = phases.run(lambda one: (to_tp(one), ctx_shift(one, -1)), mine[-1])
        other.append(got)
        mine.append(moved)

    near, far = list(range(0, ctx, 2)), list(range(1, ctx, 2))

    def meta_of(blocks):
        return jnp.stack([owned * plane] + [here[d] for d in blocks] + [lane]).astype(jnp.int32)

    def pieces_of(mine, other, blocks):
        return [[mine[d]] + list(other[d]) for d in blocks]

    def near_blocks(last, last_cot, weights, mine, cot_mine, expert_gate, expert_up, expert_down):
        later = to_tp(last), to_tp(last_cot)
        got = expert_blocks(
            0, ctx, capacity, experts, units, meta_of(near), pieces_of(mine, other, near),
            pieces_of(cot_mine, cot_other, near), weights, router_t, [])
        again_mine = jnp.concatenate(experts_of(other_plane, expert_gate, expert_up, expert_down), axis=0)
        return later, got, again_mine

    later, got, again_mine = phases.run(
        near_blocks, mine[-1], cot_mine[-1], weights, mine[:-1], cot_mine[:-1], expert_gate, expert_up, expert_down)
    other_weights = lax.all_gather(again_mine, "fsdp", axis=0)
    other.append(later[0])
    cot_other.append(later[1])
    near_dx = [got[0][i] for i in range(half)]

    def far_blocks(dx, mine, other, cot_mine, cot_other, saved):
        sent = [sent_tp(one) for one in dx]
        got = expert_blocks(
            half, ctx, capacity, experts, units, meta_of(far), pieces_of(mine, other, far),
            pieces_of(cot_mine, cot_other, far), weights, router_t, saved)
        return sent, got

    near_sent, got = phases.run(far_blocks, near_dx, mine, other, cot_mine, cot_other, got[1:])
    far_dx = [got[0][i] for i in range(half)]
    sx, sr, sh, sa, sb, ssx, ssc, ssh, ssa, ssb, out_parts = got[1:]

    def sent_pairs(kept, got):
        return [
            pair_shift(
                (pick(kept, (pair + j) % pairs).astype(F32) + pick(got, (pair + j) % pairs).astype(F32)
                 ).astype(BF16), j)
            for j in range(1, pairs)
        ]

    def add_pairs(kept, got, far):
        result = pick(kept, pair).astype(F32) + pick(got, pair).astype(F32)
        for one in far:
            result = result + one.astype(F32)
        return result.astype(BF16)

    def weight_step(left, right):
        return weight_grads(core_index, left, right, pairs)

    def again(d, ssx, saved):
        meta = jnp.stack([owned * other_plane, plane]).astype(jnp.int32)
        return expert_again(
            d, capacity, tp, experts, meta, ssx, ssc, other_weights, router_t, saved)

    def back_through_norm(dx_sum):
        grad_normed = dx_sum[:tok]
        grad_gates = dx_sum[tok : tok + experts, :tok].T
        named = lax.dynamic_slice_in_dim(hits, lane * tok, tok, 1).T
        logits = jnp.where(named, dot(normed_low, router_full), -1e30)
        expo = jnp.where(named, jnp.exp(logits - jnp.max(logits, axis=-1, keepdims=True)), 0.0)
        gates = expo / jnp.sum(expo, axis=-1, keepdims=True)
        grad_logits = (
            gates * (grad_gates - jnp.sum(gates * grad_gates, axis=-1, keepdims=True))
        ).astype(BF16)
        grad_normed = grad_normed + dot_nt(grad_logits, router_full)
        grad_mixed_norm, grad_ffn_gain = norm_back(grad_normed, mixed, scale_ffn, ffn_scale)
        grad_out = lax.dynamic_slice_in_dim(cotangent, lane * tok, tok, 0).astype(F32)
        grad_mixed = grad_out + grad_mixed_norm
        return grad_mixed.astype(BF16), grad_mixed, grad_ffn_gain, dot_tn(grad_logits, normed_low)

    def out_sent(out_parts, d):
        return [
            tp_shift(lax.dynamic_index_in_dim(out_parts[d], (lane + j) % tp, 0, keepdims=False), j)
            for j in range(1, tp)
        ]

    def phase_one(near_dx, near_sent, far_dx, sr, sx):
        sent = [sent_tp(one) for one in far_dx]
        sums = [sum_tp(one, got) for one, got in zip(near_dx, near_sent)]
        home = [sums[0]] + [ctx_shift(one.astype(BF16), d) for d, one in zip(near[1:], sums[1:])]
        return sent, home, weight_step(sr, sh), weight_step(sx, sa)

    far_sent, home, down, gate = phases.run(phase_one, near_dx, near_sent, far_dx, sr, sx)

    def phase_two(far_dx, far_sent, down_sent, gate_sent, sx, ssx, out_parts):
        sums = [sum_tp(one, got) for one, got in zip(far_dx, far_sent)]
        more = [ctx_shift(one.astype(BF16), d) for d, one in zip(far, sums)]
        return (
            more, core_swap(down_sent), core_swap(gate_sent), out_sent(out_parts, 0),
            weight_step(sx, sb), again(0, ssx, []))

    more, down_got, gate_got, out_zero, up, other_saved = phases.run(
        phase_two, far_dx, far_sent, down[0], gate[0], sx, ssx, out_parts)

    def phase_three(home, down_kept, down_got, up_sent, ssx, saved, out_parts):
        sent = sent_pairs(down_kept, down_got), core_swap(up_sent), out_sent(out_parts, 1), out_sent(out_parts, 2)
        back = back_through_norm(sum(one.astype(F32) for one in home))
        return sent, back, again(1, ssx, saved)

    (down_far, up_got, out_one, out_two), back, other_saved = phases.run(
        phase_three, home + more, down[1], down_got, up[0], ssx, other_saved, out_parts)
    grad_mixed_low, grad_mixed, grad_ffn_gain, grad_router = back

    def phase_four(gate_kept, gate_got, grad_mixed_low, ssx, saved, out_parts):
        sent = sent_pairs(gate_kept, gate_got), to_tp(grad_mixed_low), out_sent(out_parts, 3)
        return sent, again(3, ssx, again(2, ssx, saved))

    (gate_far, grad_mixed_other, out_three), other_saved = phases.run(
        phase_four, gate[1], gate_got, grad_mixed_low, ssx, other_saved, out_parts)
    ox, orr, oh, oa, ob = other_saved

    def phase_five(up_kept, up_got, down, grad_mixed_low, grad_mixed_other, out_parts, out_far):
        sent = sent_pairs(up_kept, up_got)
        rows = joined(grad_mixed_low, *grad_mixed_other)
        grad_attended = dot(rows, out_full).astype(BF16)
        grads = attend_back(query, keys, values, grad_attended, lse, kseg, qseg, cosine, sine)
        total = lax.dynamic_index_in_dim(out_parts, lane, 1, keepdims=False).astype(F32)
        for j in range(tp - 1):
            total = total + jnp.stack([one[j] for one in out_far]).astype(F32)
        return sent, rows, grads, add_pairs(*down), total.astype(BF16)

    up_far, grad_mixed_rows, (dq, dk, dv), own_down, out_total = phases.run(
        phase_five, up[1], up_got, (down[1], down_got, down_far), grad_mixed_low, grad_mixed_other, out_parts,
        [out_zero, out_one, out_two, out_three])
    out_sum = lax.psum_scatter(out_total, "ctx", scatter_dimension=0, tiled=False)

    def phase_six(gate, up, dq, dk, dv, orr, ssx):
        back, gain_row = hidden_back([prev_two, prev_one, tokens], dk, dv, dq, qkv_full)
        return back, gain_row, add_pairs(*gate), add_pairs(*up), weight_step(orr, oh), shared_grads(
            core_index, ssx, ssc, ssa, ssb, ssh, pairs)

    back, gain_row, own_gate, own_up, other_down, shared = phases.run(
        phase_six, (gate[1], gate_got, gate_far), (up[1], up_got, up_far), dq, dk, dv, orr, ssx)
    groups = [[2 * i, 2 * i + 1] for i in range(ctx // 2)]
    own_all = lax.all_gather(
        jnp.concatenate([own_down, own_gate, own_up], axis=0), "ctx", axis=0, axis_index_groups=groups)
    small_rows = jnp.concatenate(
        [grad_router, grad_ffn_gain[None], gain_row, jnp.zeros((16 - experts - 2, width), F32)], axis=0)
    hidden_parts = [back[j].reshape(tp, tok, width) for j in range(3)]

    def phase_seven(hidden_parts, small_rows, down_sent, shared_sent, ox):
        sent = [sent_tp(hidden_parts[0]), sent_tp(hidden_parts[1]), all_sum(small_rows, "tp")]
        return sent, core_swap(down_sent), core_swap(shared_sent), weight_step(ox, oa), weight_step(ox, ob)

    hidden_sent, down_got, shared_got, other_gate, other_up = phases.run(
        phase_seven, hidden_parts, small_rows, other_down[0], shared[0], ox)
    small_rows = jnp.pad(hidden_sent[2], ((0, 112), (0, 0)))

    def phase_eight(hidden_parts, got, hid, down, gate_sent, up_sent):
        far_two = sum_tp(hidden_parts[0], got[0]).astype(BF16)
        sent = [
            sent_pairs(*down), ctx_open(far_two, -1), sent_tp(hidden_parts[2]), core_swap(gate_sent), core_swap(up_sent)]
        attn = attn_grads_of(
            core_index, hid, dk, dv, dq, grad_mixed_rows, attended, small_rows, pairs)
        return sent, attn

    (down_far, carried, hidden_mine_sent, gate_got, up_got), attn = phases.run(
        phase_eight, hidden_parts, hidden_sent, hid, (other_down[1], down_got), other_gate[0], other_up[0])

    def phase_nine(hidden_parts, got, carried, attn_sent, gate, down, shared):
        sent = sent_pairs(*gate)
        far_one = (sum_tp(hidden_parts[1], got[1]) + carried.astype(F32)).astype(BF16)
        return sent, ctx_open(far_one, -1), core_swap(attn_sent), add_pairs(*down), sent_pairs(*shared)

    gate_far, carried, attn_got, other_down, shared_far = phases.run(
        phase_nine, hidden_parts, hidden_sent, carried, attn[0], (other_gate[1], gate_got),
        (other_down[1], down_got, down_far), (shared[1], shared_got))

    def input_back(total, got, carried):
        grad_hidden = sum_tp(total, got) + carried.astype(F32)
        scale_attn = lax.rsqrt(jnp.mean(inputs_mine * inputs_mine, axis=-1, keepdims=True) + EPS)
        scaled = grad_hidden * attn_scale
        grad_norm = scale_attn * scaled - inputs_mine * scale_attn * scale_attn * scale_attn * jnp.mean(
            scaled * inputs_mine, axis=-1, keepdims=True)
        return (grad_mixed + grad_norm).astype(BF16)

    def phase_ten(hidden_parts, got, carried, attn, up, gate, shared, other_down):
        return (
            input_back(hidden_parts[2], got, carried), sent_pairs(*attn), sent_pairs(*up), add_pairs(*gate),
            add_pairs(*shared), ctx_swap(other_down))

    input_mine, attn_far, up_far, other_gate, own_shared, far_other_down = phases.run(
        phase_ten, hidden_parts, hidden_mine_sent, carried, (attn[1], attn_got), (other_up[1], up_got),
        (other_gate[1], gate_got, gate_far), (shared[1], shared_got, shared_far), other_down)
    all_shared = lax.all_gather(own_shared, "ctx", axis=0)
    odd = plane % 2

    def paired(one, got):
        return jnp.where(odd == 0, jnp.stack([one, got]), jnp.stack([got, one]))

    places = jnp.stack([plane // 2, 1 - plane // 2]).astype(jnp.int32)

    def phase_eleven(input_mine, attn, up, other_gate, other_down, far_other_down, own_all, out_sum):
        output_mine = (mixed + out_sum.astype(F32)).astype(BF16)
        return (
            to_tp(input_mine), add_pairs(*attn), add_pairs(*up), ctx_swap(other_gate),
            collect(places, own_all, paired(other_down, far_other_down), (0, 0), owned, True), output_mine)

    input_other, attn_rows, other_up, far_other_gate, grad_expert_down, output_mine = phases.run(
        phase_eleven, input_mine, (attn[1], attn_got, attn_far), (other_up[1], up_got, up_far), other_gate,
        other_down, far_other_down, own_all, out_sum)
    attn_rows = lax.psum(attn_rows, "ctx")

    def phase_twelve(other_up, other_gate, far_other_gate, input_mine, input_other, output_mine):
        return (
            ctx_swap(other_up), to_tp(output_mine), joined(input_mine, *input_other),
            collect(places, own_all, paired(other_gate, far_other_gate), (owned, 0), owned, False))

    far_other_up, output_other, input_grad, grad_expert_gate = phases.run(
        phase_twelve, other_up, other_gate, far_other_gate, input_mine, input_other, output_mine)
    grad_expert_up = collect(places, own_all, paired(other_up, far_other_up), (2 * owned, 0), owned, False)
    output = joined(output_mine, *output_other)
    attn_rows = attn_rows.astype(F32)
    grad_key_weight = attn_rows[:, :cols]
    grad_value_weight = attn_rows[:, cols : 2 * cols]
    grad_query_weight = attn_rows[:, 2 * cols : 3 * cols]
    grad_out_rows = attn_rows[:, 3 * cols : 4 * cols].T
    small_out = attn_rows[:, 4 * cols :]
    result = all_shared.astype(F32)
    result = result.reshape(ctx, share, 3, units).transpose(2, 1, 0, 3).reshape(3, share, ctx * units)
    grad_shared_gate, grad_shared_up, grad_shared_down = result[0], result[1], result[2].T
    return (
        output[None],
        input_grad[None],
        grad_query_weight,
        grad_key_weight,
        grad_value_weight,
        grad_out_rows,
        small_out[:, experts + 1],
        small_out[:, experts],
        small_out[:, :experts],
        grad_shared_gate,
        grad_shared_up,
        grad_shared_down,
        grad_expert_gate,
        grad_expert_up,
        grad_expert_down,
    )


def solution(mesh):
    in_specs = (
        P("fsdp", "ctx", None),
        P("fsdp", None),
        P("fsdp", "ctx", None),
        P("fsdp", "tp"),
        P("fsdp", "tp"),
        P("fsdp", "tp"),
        P("tp", "fsdp"),
        P("fsdp"),
        P("fsdp"),
        P("fsdp", None),
        P("fsdp", "tp"),
        P("fsdp", "tp"),
        P("tp", "fsdp"),
        P(None, "fsdp", "tp"),
        P(None, "fsdp", "tp"),
        P(None, "tp", "fsdp"),
        P("fsdp", "ctx", None),
    )
    out_specs = (
        P("fsdp", "ctx", None),
        P("fsdp", "ctx", None),
        P("fsdp", "tp"),
        P("fsdp", "tp"),
        P("fsdp", "tp"),
        P("tp", "fsdp"),
        P("fsdp"),
        P("fsdp"),
        P("fsdp", None),
        P("fsdp", "tp"),
        P("fsdp", "tp"),
        P("tp", "fsdp"),
        P(None, "fsdp", "tp"),
        P(None, "fsdp", "tp"),
        P(None, "tp", "fsdp"),
    )
    return jax.shard_map(local, mesh=mesh, in_specs=in_specs, out_specs=out_specs, check_vma=False)
```

time: 724 us -> 618 us (0.85)
  waiting for transfers between devices: 312 us -> 138 us
  Pallas kernels: 94 us -> 221 us
  starting transfers between devices: 98.9 us -> 66 us
  local copies, waits for them, and re-layouts: 102 us -> 74.2 us
  matrix products: 27.5 us -> 6.14 us
  between operations: 2.96 us -> 15.6 us
  other arithmetic: 78 us -> 87.7 us
    pallas_call x7 -> x20, Pallas kernels: 63.1 us -> 190 us  [the longest x2 53.7 us: expert_blocks(): pl.pallas_call(functools.partial(expert_kernel, capacity, parts, experts,...]
    ppermute x10 -> x1, waiting for transfers between devices: 79.5 us -> 2.14 us  [all_sum(): other = lax.ppermute(block, axis, [(i, i ^ reach) for i in range(size)])]
    ppermute x33 -> x9, waiting for transfers between devices: 97.3 us -> 20.4 us  [ctx_shift(): lax.ppermute(block, 'ctx', [(i, (i + distance) % size) for i in range(siz...]
    convert_element_type x15 -> x30, other arithmetic: 10.4 us -> 45.8 us  [the longest x8 17.8 us: add_pairs(): return result.astype(BF16)]
    psum x0 -> x1, waiting for transfers between devices: none -> 26.1 us  [local(): attn_rows = lax.psum(attn_rows, 'ctx')]
    ppermute x22 -> x24, waiting for transfers between devices: 47.5 us -> 21.8 us  [tp_shift(): lax.ppermute(block, 'tp', [(i, (i + distance) % size) for i in range(size)])]
    dynamic_update_slice x17 -> x0, other arithmetic: 25.2 us -> none  [the longest x12 21.7 us: expert_grad(): lax.dynamic_update_index_in_dim(result, one.astype(F32), (plane - d) % ct...]
    ppermute x33 -> x9, starting transfers between devices: 39.6 us -> 16 us  [ctx_shift(): lax.ppermute(block, 'ctx', [(i, (i + distance) % size) for i in range(siz...]
  transfers between devices with their start and end apart: 106 -> 66, of which waited for: 39 -> 19; matrix products, arithmetic and copies ran while one was open for 26% -> 21% of each run, Pallas kernels for 13% -> 35%
where the time goes in v2:
time: 618 us; the launch traced here: 609 us
  Pallas kernels  221 us (36%)
  waiting for transfers between devices  138 us (22%)
  other arithmetic  87.7 us (14%)
  local copies, waits for them, and re-layouts  74.2 us (12%)
  starting transfers between devices  66 us (11%)
  between operations  15.6 us (3%)
    pallas_call x2, Pallas kernels, expert_blocks(): pl.pallas_call(functools.partial(expert_kernel, capacity, parts, experts,...  53.7 us
    ppermute x9, waiting for transfers between devices, pair_shift(): return lax.ppermute(block, 'fsdp', route)  42.8 us
    pallas_call x6, Pallas kernels, weight_grads(): pl.pallas_call(weight_kernel, grid_spec=pltpu.PrefetchScalarGridSpec(num_...  41.8 us
    pallas_call x4, Pallas kernels, expert_again(): pl.pallas_call(functools.partial(expert_kernel, capacity, parts, experts,...  37.5 us
    psum x1, waiting for transfers between devices, local(): attn_rows = lax.psum(attn_rows, 'ctx')  26.1 us
    pallas_call x3, Pallas kernels, collect(): pl.pallas_call(functools.partial(collect_kernel, turned), grid_spec=pltpu...  24.2 us
    ppermute x24, starting transfers between devices, tp_shift(): lax.ppermute(block, 'tp', [(i, (i + distance) % size) for i in range(size)])  23.6 us
    unnamed x139, local copies, waits for them, and re-layouts  23.2 us
  transfers between devices with their start and end apart: 66, of which 19 were waited for; matrix products, arithmetic and copies ran while one was open for 21% of the time, Pallas kernels for 35%

profile of v2, /device:TPU:0, one launch (start us, length us, event | category | flops | bytes accessed | tf_op | source)
XLA Modules:
  0.0 609.3 jit_solution(1312672851177906521)
XLA Ops:
  19.1 2.8 pad_maximum_fusion
  22.0 3.0 collective-permute-start.1
  25.1 3.5 collective-permute-start
  32.9 4.3 fusion.13
  37.9 6.1 %collective-permute-done.1 = bf16[192,1664]{1,0:T(8,128)(2,1)} collective-permute-done((bf16[192,1664]{1,0:T(8,128)(2,1)}, bf16[192,1664]{1,0:T(8,128)(2,1)}, u32[]{:S(2)}, u32[]{:S(2)}) %collective-permute-start.1) | collective-permute-done | bytes 639008 | tf_op jit(solution)/shard_map/ppermute | solution.py:40
  44.0 3.6 collective-permute-start.5
  53.1 5.9 collective-permute-done.3
  59.0 6.9 %collective-permute-done.4 = bf16[256,768]{1,0:T(8,128)(2,1)} collective-permute-done((bf16[256,768]{1,0:T(8,128)(2,1)S(1)}, bf16[256,768]{1,0:T(8,128)(2,1)}, u32[]{:S(2)}, u32[]{:S(2)}) %collective-permute-start.4) | collective-permute-done | bytes 393248 | tf_op jit(solution)/shard_map/ppermute | solution.py:61
  69.3 4.4 collective-permute-start.8
  84.2 6.7 %shard_map.280 = (bf16[1536,768]{1,0:T(8,128)(2,1)}, bf16[1536,384]{1,0:T(8,128)(2,1)}, bf16[1536,384]{1,0:T(8,128)(2,1)}, bf16[512,384]{1,0:T(8,128)(2,1)}) custom-call(bf16[512,768]{1,0:T(8,128)(2,1)} %bitcast.279, bf16[512,768]{1,0:T(8,128)(2,1)} %bitcast.276, f32[1,768]{1,0:T(1,128)} %slice_convert_fusion.1.refs_2_.refs_1_, bf16[768,1152]{1,0:T(8,128)(2,1)} %bitcast.273, ...), custom_call_target="tpu_custom_call" | custom-call | bytes 5950000 | tf_op jit(solution)/shard_map/pallas_call | solution.py:171
  99.5 3.8 shard_map.281
  103.3 13.4 %shard_map.282 = (bf16[512,384]{1,0:T(8,128)(2,1)}, f32[3,2,512]{2,1,0:T(2,128)}) custom-call(bf16[512,384]{1,0:T(8,128)(2,1)} %get-tuple-element.291.q_ref, bf16[1536,384]{1,0:T(8,128)(2,1)} %get-tuple-element.299.k_ref, bf16[1536,384]{1,0:T(8,128)(2,1)} %get-tuple-element.300.v_ref, s32[1536,1]{1,0:T(8,128)} %copy.94.kseg_ref, s32[1,512]{1,0:T(1,128)} %bitcast.321), custom_call_target="tpu_custom_call" | custom-call | bytes 11050000 | tf_op jit(solution)/shard_map/pallas_call | solution.py:234
  124.5 7.9 %collective-permute-done.12 = bf16[256,768]{1,0:T(8,128)(2,1)S(1)} collective-permute-done((bf16[256,768]{1,0:T(8,128)(2,1)}, bf16[256,768]{1,0:T(8,128)(2,1)S(1)}, u32[]{:S(2)}, u32[]{:S(2)}) %collective-permute-start.12) | collective-permute-done | bytes 393248 | tf_op jit(solution)/shard_map/ppermute | solution.py:45
  135.8 7.9 %collective-permute-done.13.refs_0_ = bf16[256,768]{1,0:T(8,128)(2,1)S(1)} collective-permute-done((bf16[256,768]{1,0:T(8,128)(2,1)S(1)}, bf16[256,768]{1,0:T(8,128)(2,1)S(1)}, u32[]{:S(2)}, u32[]{:S(2)}) %collective-permute-start.13) | collective-permute-done | bytes 393248 | tf_op jit(solution)/shard_map/ppermute | solution.py:50
  147.0 5.4 collective-permute-done.15.refs_2_
  158.2 5.2 collective-permute-done.17.refs_2_
  175.0 27.9 %shard_map.283 = (bf16[2,2,272,768]{3,2,1,0:T(8,128)(2,1)}, bf16[4,2,192,768]{3,2,1,0:T(8,128)(2,1)}, bf16[4,2,192,768]{3,2,1,0:T(8,128)(2,1)}, bf16[4,2,192,102...) custom-call(s32[4]{0:T(128)} %add_add_fusion.meta_ref, ...), custom_call_target="tpu_custom_call" | custom-call | bytes 22100000 | tf_op jit(solution)/shard_map/pallas_call | solution.py:480
  207.5 25.8 %shard_map.284 = (bf16[2,2,272,768]{3,2,1,0:T(8,128)(2,1)}, bf16[4,2,192,768]{3,2,1,0:T(8,128)(2,1)}, bf16[4,2,192,768]{3,2,1,0:T(8,128)(2,1)}, bf16[4,2,192,102...) custom-call(s32[4]{0:T(128)} %add_add_fusion.1.meta_ref, ...), custom_call_target="tpu_custom_call", output_to_operand_aliasing={{1}: (11, {}), {2}: (12, {}), {3}: (13, {}), {4}: (14, {}),... | custom-call | bytes 22100000 | tf_op jit(solution)/shard_map/pallas_call | solution.py:480
  238.1 6.7 %shard_map.286 = (bf16[2,2,192,1024]{3,2,1,0:T(8,128)(2,1)}, bf16[2,2,192,1024]{3,2,1,0:T(8,128)(2,1)}) custom-call(s32[1]{0:T(128)} %bitcast.63.core_ref, bf16[4,2,192,768]{3,2,1,0:T(8,128)(2,1)} %get-tuple-element.388.left_ref, bf16[4,2,192,1024]{3,2,1,0:T(8,128)(2,1)} %get-tuple-element.363.right_ref), custom_call_target="tpu_custom_call" | custom-call | bytes 5100000 | tf_op jit(solution)/shard_map/pallas_call | solution.py:544
  244.8 6.9 %shard_map.285 = (bf16[2,2,192,1024]{3,2,1,0:T(8,128)(2,1)}, bf16[2,2,192,1024]{3,2,1,0:T(8,128)(2,1)}) custom-call(s32[1]{0:T(128)} %bitcast.63.core_ref, bf16[4,2,192,768]{3,2,1,0:T(8,128)(2,1)} %get-tuple-element.377.left_ref, bf16[4,2,192,1024]{3,2,1,0:T(8,128)(2,1)} %get-tuple-element.362.right_ref), custom_call_target="tpu_custom_call" | custom-call | bytes 5100000 | tf_op jit(solution)/shard_map/pallas_call | solution.py:544
  261.9 6.9 %shard_map.287 = (bf16[2,2,192,1024]{3,2,1,0:T(8,128)(2,1)}, bf16[2,2,192,1024]{3,2,1,0:T(8,128)(2,1)}) custom-call(s32[1]{0:T(128)} %bitcast.63.core_ref, bf16[4,2,192,768]{3,2,1,0:T(8,128)(2,1)} %get-tuple-element.388.left_ref, bf16[4,2,192,1024]{3,2,1,0:T(8,128)(2,1)} %get-tuple-element.364.right_ref), custom_call_target="tpu_custom_call" | custom-call | bytes 5100000 | tf_op jit(solution)/shard_map/pallas_call | solution.py:544
  268.9 9.3 %shard_map.288 = (bf16[4,2,192,768]{3,2,1,0:T(8,128)(2,1)}, bf16[4,2,192,768]{3,2,1,0:T(8,128)(2,1)}, bf16[4,2,192,1024]{3,2,1,0:T(8,128)(2,1)}, bf16[4,2,192,10...) custom-call(s32[2]{0:T(128)} %pad_add_fusion.meta_ref, bf16[4,512,768]{2,1,0:T(8,128)(2,1)} %get-tuple-element.460.refs_0_.x_ref, ...), custom_call_target="tpu_custom_call" | custom-call | bytes 7650000 | tf_op jit(solution)/shard_map/pallas_call | solution.py:501
  291.5 9.3 %shard_map.289 = (bf16[4,2,192,768]{3,2,1,0:T(8,128)(2,1)}, bf16[4,2,192,768]{3,2,1,0:T(8,128)(2,1)}, bf16[4,2,192,1024]{3,2,1,0:T(8,128)(2,1)}, bf16[4,2,192,10...) custom-call(s32[2]{0:T(128)} %pad_add_fusion.meta_ref, ...), custom_call_target="tpu_custom_call", output_to_operand_aliasing={{0}: (5, {}), {1}: (6, {}), {2}: (7, {}), {3}: (8, {}), {4}... | custom-call | bytes 7650000 | tf_op jit(solution)/shard_map/pallas_call | solution.py:501
  302.1 3.5 collective-permute-done.34
  309.3 9.2 %shard_map.290 = (bf16[4,2,192,768]{3,2,1,0:T(8,128)(2,1)}, bf16[4,2,192,768]{3,2,1,0:T(8,128)(2,1)}, bf16[4,2,192,1024]{3,2,1,0:T(8,128)(2,1)}, bf16[4,2,192,10...) custom-call(s32[2]{0:T(128)} %pad_add_fusion.meta_ref, ...), custom_call_target="tpu_custom_call", output_to_operand_aliasing={{0}: (5, {}), {1}: (6, {}), {2}: (7, {}), {3}: (8, {}), {4}... | custom-call | bytes 7650000 | tf_op jit(solution)/shard_map/pallas_call | solution.py:501
  318.4 9.6 %shard_map.291 = (bf16[4,2,192,768]{3,2,1,0:T(8,128)(2,1)}, bf16[4,2,192,768]{3,2,1,0:T(8,128)(2,1)}, bf16[4,2,192,1024]{3,2,1,0:T(8,128)(2,1)}, bf16[4,2,192,10...) custom-call(s32[2]{0:T(128)} %pad_add_fusion.meta_ref, ...), custom_call_target="tpu_custom_call", output_to_operand_aliasing={{0}: (5, {}), {1}: (6, {}), {2}: (7, {}), {3}: (8, {}), {4}... | custom-call | bytes 7650000 | tf_op jit(solution)/shard_map/pallas_call | solution.py:501
  329.1 2.8 fusion
  340.4 17.6 %shard_map.292 = (bf16[512,384]{1,0:T(8,128)(2,1)}, bf16[1536,384]{1,0:T(8,128)(2,1)}, bf16[1536,384]{1,0:T(8,128)(2,1)}) custom-call(bf16[512,384]{1,0:T(8,128)(2,1)} %get-tuple-element.291.q_ref, bf16[1536,384]{1,0:T(8,128)(2,1)} %get-tuple-element.299.k_ref, bf16[1536,384]{1,0:T(8,128)(2,1)} %get-tuple-element.300.v_ref, ...), custom_call_target="tpu_custom_call" | custom-call | bytes 15300000 | tf_op jit(solution)/shard_map/pallas_call | solution.py:307
  359.8 7.3 %shard_map.295 = (bf16[2,192,768]{2,1,0:T(8,128)(2,1)}, bf16[2,192,768]{2,1,0:T(8,128)(2,1)}) custom-call(s32[1]{0:T(128)} %bitcast.63.core_ref, bf16[4,512,768]{2,1,0:T(8,128)(2,1)} %get-tuple-element.460.refs_0_.x_ref, bf16[4,528,768]{2,1,0:T(8,128)(2,1)} %get-tuple-element.366.refs_1_.c_ref, bf16[4,512,256]{2,1,0:T(8,128)(2,1)} %get-tuple-element.368.a_ref, ...), custom_call_target="tpu_custom_call" | custom-call | bytes 6800000 | tf_op jit(solution)/shard_map/pallas_call | solution.py:582
  367.1 6.8 %shard_map.294 = (bf16[2,2,192,1024]{3,2,1,0:T(8,128)(2,1)}, bf16[2,2,192,1024]{3,2,1,0:T(8,128)(2,1)}) custom-call(s32[1]{0:T(128)} %bitcast.63.core_ref, bf16[4,2,192,768]{3,2,1,0:T(8,128)(2,1)} %get-tuple-element.458.left_ref, bf16[4,2,192,1024]{3,2,1,0:T(8,128)(2,1)} %get-tuple-element.435.right_ref), custom_call_target="tpu_custom_call" | custom-call | bytes 5100000 | tf_op jit(solution)/shard_map/pallas_call | solution.py:544
  373.9 7.5 %shard_map.293 = (bf16[3,512,768]{2,1,0:T(8,128)(2,1)}, f32[1,768]{1,0:T(1,128)}) custom-call(bf16[512,768]{1,0:T(8,128)(2,1)} %bitcast.282, bf16[512,768]{1,0:T(8,128)(2,1)} %bitcast.280, bf16[512,768]{1,0:T(8,128)(2,1)} %bitcast.277, bf16[1536,384]{1,0:T(8,128)(2,1)} %get-tuple-element.453.refs_3_.dk_ref, ...), custom_call_target="tpu_custom_call" | custom-call | bytes 5950000 | tf_op jit(solution)/shard_map/pallas_call | solution.py:658
  392.6 7.6 %shard_map.297 = (bf16[2,2,192,1024]{3,2,1,0:T(8,128)(2,1)}, bf16[2,2,192,1024]{3,2,1,0:T(8,128)(2,1)}) custom-call(s32[1]{0:T(128)} %bitcast.63.core_ref, bf16[4,2,192,768]{3,2,1,0:T(8,128)(2,1)} %get-tuple-element.474.left_ref, bf16[4,2,192,1024]{3,2,1,0:T(8,128)(2,1)} %get-tuple-element.437.right_ref), custom_call_target="tpu_custom_call" | custom-call | bytes 5100000 | tf_op jit(solution)/shard_map/pallas_call | solution.py:544
  400.3 6.9 %shard_map.296 = (bf16[2,2,192,1024]{3,2,1,0:T(8,128)(2,1)}, bf16[2,2,192,1024]{3,2,1,0:T(8,128)(2,1)}) custom-call(s32[1]{0:T(128)} %bitcast.63.core_ref, bf16[4,2,192,768]{3,2,1,0:T(8,128)(2,1)} %get-tuple-element.474.left_ref, bf16[4,2,192,1024]{3,2,1,0:T(8,128)(2,1)} %get-tuple-element.436.right_ref), custom_call_target="tpu_custom_call" | custom-call | bytes 5100000 | tf_op jit(solution)/shard_map/pallas_call | solution.py:544
  416.1 7.9 %shard_map.298 = (bf16[2,192,1664]{2,1,0:T(8,128)(2,1)}, bf16[2,192,1664]{2,1,0:T(8,128)(2,1)}) custom-call(s32[1]{0:T(128)} %bitcast.63.core_ref, bf16[1536,768]{1,0:T(8,128)(2,1)} %get-tuple-element.483.hid_ref, bf16[1536,384]{1,0:T(8,128)(2,1)} %get-tuple-element.453.refs_3_.dk_ref, bf16[1536,384]{1,0:T(8,128)(2,1)} %get-tuple-element.454.refs_4_.dv_ref, ...), custom_call_target="tpu_custom_call" | custom-call | bytes 6800000 | tf_op jit(solution)/shard_map/pallas_call | solution.py:616
  424.0 10.1 %collective-permute-done.45 = bf16[256,768]{1,0:T(8,128)(2,1)S(1)} collective-permute-done((bf16[256,768]{1,0:T(8,128)(2,1)S(1)}, bf16[256,768]{1,0:T(8,128)(2,1)S(1)}, u32[]{:S(2)}, u32[]{:S(2)}) %collective-permute-start.45) | collective-permute-done | bytes 393248 | tf_op jit(solution)/shard_map/ppermute | solution.py:61
  445.9 16.4 %collective-permute-done.52 = bf16[192,768]{1,0:T(8,128)(2,1)} collective-permute-done((bf16[192,768]{1,0:T(8,128)(2,1)}, bf16[192,768]{1,0:T(8,128)(2,1)}, u32[]{:S(2)}, u32[]{:S(2)}) %collective-permute-start.52) | collective-permute-done | bytes 294944 | tf_op jit(solution)/shard_map/ppermute | solution.py:40
  470.6 3.0 fusion.2
  477.2 20.3 %collective-permute-done.53 = bf16[192,1664]{1,0:T(8,128)(2,1)} collective-permute-done((bf16[192,1664]{1,0:T(8,128)(2,1)}, bf16[192,1664]{1,0:T(8,128)(2,1)}, u32[]{:S(2)}, u32[]{:S(2)}) %collective-permute-start.53) | collective-permute-done | bytes 639008 | tf_op jit(solution)/shard_map/ppermute | solution.py:40
  497.5 7.3 %collective-permute-done.55 = bf16[2,192,1024]{2,1,0:T(8,128)(2,1)} collective-permute-done((bf16[2,192,1024]{2,1,0:T(8,128)(2,1)S(1)}, bf16[2,192,1024]{2,1,0:T(8,128)(2,1)}, u32[]{:S(2)}, u32[]{:S(2)}) %collective-permute-start.55) | collective-permute-done | bytes 786464 | tf_op jit(solution)/shard_map/ppermute | solution.py:55
  507.0 2.9 fusion.1
  512.7 8.7 %shard_map.299 = f32[8,1024,192]{2,1,0:T(8,128)} custom-call(s32[2]{0:T(128)} %pad_add_fusion.1.places_ref, bf16[2,6,192,1024]{3,2,1,0:T(8,128)(2,1)} %bitcast.270, bf16[2,2,192,1024]{3,2,1,0:T(8,128)(2,1)} %maximum_select_fusion.1.second_ref), custom_call_target="tpu_custom_call" | custom-call | bytes 4250000 | tf_op jit(solution)/shard_map/pallas_call | solution.py:696
  521.3 8.5 %copy.101 = f32[8,1024,192]{1,2,0:T(8,128)} copy(f32[8,1024,192]{2,1,0:T(8,128)} %shard_map.299) | data formatting | bytes 12582912
  535.7 2.9 maximum_select_fusion.2.second_ref
  538.6 7.7 %shard_map.300 = f32[8,192,1024]{2,1,0:T(8,128)} custom-call(s32[2]{0:T(128)} %pad_add_fusion.1.places_ref, bf16[2,6,192,1024]{3,2,1,0:T(8,128)(2,1)} %bitcast.271, bf16[2,2,192,1024]{3,2,1,0:T(8,128)(2,1)} %maximum_select_fusion.2.second_ref), custom_call_target="tpu_custom_call" | custom-call | bytes 4250000 | tf_op jit(solution)/shard_map/pallas_call | solution.py:696
  548.5 2.9 reshape.763
  559.8 26.1 %all-reduce.5.cloned.1.call-done = bf16[192,1664]{1,0:T(8,128)(2,1)} async-done(((bf16[192,1664]{1,0:T(8,128)(2,1)}), bf16[192,1664]{1,0:T(8,128)(2,1)}) %all-reduce.5.cloned.1.call-update) | async-done | bytes 638992 | tf_op jit(solution)/shard_map/psum | solution.py:1110
  591.1 3.3 maximum_select_fusion.3.second_ref
  594.4 7.8 %shard_map.301 = f32[8,192,1024]{2,1,0:T(8,128)} custom-call(s32[2]{0:T(128)} %pad_add_fusion.1.places_ref, bf16[2,6,192,1024]{3,2,1,0:T(8,128)(2,1)} %bitcast.272, bf16[2,2,192,1024]{3,2,1,0:T(8,128)(2,1)} %maximum_select_fusion.3.second_ref), custom_call_target="tpu_custom_call" | custom-call | bytes 4250000 | tf_op jit(solution)/shard_map/pallas_call | solution.py:696
  (399 shorter events, 195.3 us)
Async XLA Ops:
  7.2 158.8 %all-gather.9.cloned.1.call-start = ((), (), s32[]{:S(2)}) async-start(), calls=%async_computation.3 | async-start | bytes 13762560 | tf_op jit(solution)/shard_map/all_gather | solution.py:833
  22.0 246.9 %all-gather.11.cloned.1.call-start = ((), (), s32[]{:S(2)}) async-start(), calls=%async_computation.4 | async-start | bytes 11796480 | tf_op jit(solution)/shard_map/all_gather | solution.py:925
  22.0 22.0 %collective-permute-start.1 = (bf16[192,1664]{1,0:T(8,128)(2,1)}, bf16[192,1664]{1,0:T(8,128)(2,1)}, u32[]{:S(2)}, u32[]{:S(2)}) collective-permute-start(bf16[192,1664]{1,0:T(8,128)(2,1)} %concatenate.139), channel_id=1, source_target_pairs={{0,16},{8,24},{16,0},{24,8},{1,17},{9,25},{17,1},{25,9},{2,18},{10... | collective-permute-start | bytes 1916936 | tf_op jit(solution)/shard_map/ppermute | solution.py:40
  25.1 18.9 %collective-permute-start.2 = (bf16[192,1664]{1,0:T(8,128)(2,1)}, bf16[192,1664]{1,0:T(8,128)(2,1)}, u32[]{:S(2)}, u32[]{:S(2)}) collective-permute-start(bf16[192,1664]{1,0:T(8,128)(2,1)} %concatenate.139), channel_id=1, source_target_pairs={{0,8},{8,0},{16,24},{24,16},{1,9},{9,1},{17,25},{25,17},{2,10},{10... | collective-permute-start | bytes 1916936 | tf_op jit(solution)/shard_map/ppermute | solution.py:33
  44.0 21.9 %collective-permute-start.6 = (bf16[192,1664]{1,0:T(8,128)(2,1)}, bf16[192,1664]{1,0:T(8,128)(2,1)}, u32[]{:S(2)}, u32[]{:S(2)}) collective-permute-start(bf16[192,1664]{1,0:T(8,128)(2,1)} %collective-permute-done.1), channel_id=1, source_target_pairs={{0,8},{8,0},{16,24},{24,16},{1,9},{9,1},{17,25},{25,17},{2,10},{10... | collective-permute-start | bytes 1916936 | tf_op jit(solution)/shard_map/ppermute | solution.py:33
  44.0 21.9 %collective-permute-start.5 = (bf16[272,768]{1,0:T(8,128)(2,1)}, bf16[272,768]{1,0:T(8,128)(2,1)}, u32[]{:S(2)}, u32[]{:S(2)}) collective-permute-start(bf16[272,768]{1,0:T(8,128)(2,1)} %fusion.35.refs_4_), channel_id=1, source_target_pairs={{0,6},{2,0},{4,2},{6,4},{1,7},{3,1},{5,3},{7,5},{8,14},{10,8},{12,... | collective-permute-start | bytes 1253384 | tf_op jit(solution)/shard_map/ppermute | solution.py:50
  69.3 21.6 %collective-permute-start.8 = (bf16[272,768]{1,0:T(8,128)(2,1)}, bf16[272,768]{1,0:T(8,128)(2,1)S(1)}, u32[]{:S(2)}, u32[]{:S(2)}) collective-permute-start(bf16[272,768]{1,0:T(8,128)(2,1)} %collective-permute-done.5.refs_4_), channel_id=1, source_target_pairs={{0,6},{2,0},{4,2},{6,4},{1,7},{3,1},{5,3},{7,5},{8,14},{10,8},{12,... | collective-permute-start | bytes 1253384 | tf_op jit(solution)/shard_map/ppermute | solution.py:50
  90.9 29.2 %collective-permute-start.11 = (bf16[272,768]{1,0:T(8,128)(2,1)S(1)}, bf16[272,768]{1,0:T(8,128)(2,1)S(1)}, u32[]{:S(2)}, u32[]{:S(2)}) collective-permute-start(bf16[272,768]{1,0:T(8,128)(2,1)S(1)} %collective-permute-done.8.refs_6_), channel_id=1, source_target_pairs={{0,1},{1,0},{2,3},{3,2},{4,5},{5,4},{6,7},{7,6},{8,9},{9,8},{10,11... | collective-permute-start | bytes 1253384 | tf_op jit(solution)/shard_map/ppermute | solution.py:45
  91.3 28.8 %collective-permute-start.9 = (bf16[272,768]{1,0:T(8,128)(2,1)S(1)}, bf16[272,768]{1,0:T(8,128)(2,1)}, u32[]{:S(2)}, u32[]{:S(2)}) collective-permute-start(bf16[272,768]{1,0:T(8,128)(2,1)S(1)} %collective-permute-done.8.refs_6_), channel_id=1, source_target_pairs={{0,6},{2,0},{4,2},{6,4},{1,7},{3,1},{5,3},{7,5},{8,14},{10,8},{12,... | collective-permute-start | bytes 1253384 | tf_op jit(solution)/shard_map/ppermute | solution.py:50
  92.0 28.1 %collective-permute-start.10 = (bf16[272,768]{1,0:T(8,128)(2,1)}, bf16[272,768]{1,0:T(8,128)(2,1)}, u32[]{:S(2)}, u32[]{:S(2)}) collective-permute-start(bf16[272,768]{1,0:T(8,128)(2,1)} %collective-permute-done.5.refs_4_), channel_id=1, source_target_pairs={{0,1},{1,0},{2,3},{3,2},{4,5},{5,4},{6,7},{7,6},{8,9},{9,8},{10,11... | collective-permute-start | bytes 1253384 | tf_op jit(solution)/shard_map/ppermute | solution.py:45
  170.1 307.1 %reduce-scatter.2.cloned.1.call-start = ((), (), s32[]{:S(2)}) async-start(), calls=%async_computation.1 | async-start | bytes 1966080 | tf_op jit(solution)/shard_map/reduce_scatter | solution.py:1033
  172.3 32.1 %collective-permute-start.20 = (bf16[272,768]{1,0:T(8,128)(2,1)}, bf16[272,768]{1,0:T(8,128)(2,1)S(1)}, u32[]{:S(2)}, u32[]{:S(2)}) collective-permute-start(bf16[272,768]{1,0:T(8,128)(2,1)} %collective-permute-done.9.refs_6_), channel_id=1, source_target_pairs={{0,1},{1,0},{2,3},{3,2},{4,5},{5,4},{6,7},{7,6},{8,9},{9,8},{10,11... | collective-permute-start | bytes 1253384 | tf_op jit(solution)/shard_map/ppermute | solution.py:45
  172.7 31.7 %collective-permute-start.19 = (bf16[256,768]{1,0:T(8,128)(2,1)}, bf16[256,768]{1,0:T(8,128)(2,1)S(1)}, u32[]{:S(2)}, u32[]{:S(2)}) collective-permute-start(bf16[256,768]{1,0:T(8,128)(2,1)} %collective-permute-done.17.refs_2_), channel_id=1, source_target_pairs={{0,1},{1,0},{2,3},{3,2},{4,5},{5,4},{6,7},{7,6},{8,9},{9,8},{10,11... | collective-permute-start | bytes 1179656 | tf_op jit(solution)/shard_map/ppermute | solution.py:45
  204.5 30.3 %collective-permute-start.22 = (bf16[272,768]{1,0:T(8,128)(2,1)S(1)}, bf16[272,768]{1,0:T(8,128)(2,1)S(1)}, u32[]{:S(2)}, u32[]{:S(2)}) collective-permute-start(bf16[272,768]{1,0:T(8,128)(2,1)S(1)} %dynamic-slice_bitcast_fusion.4), channel_id=1, source_target_pairs={{0,1},{1,0},{2,3},{3,2},{4,5},{5,4},{6,7},{7,6},{8,9},{9,8},{10,11... | collective-permute-start | bytes 1253384 | tf_op jit(solution)/shard_map/ppermute | solution.py:45
  204.6 30.2 %collective-permute-start.21 = (bf16[272,768]{1,0:T(8,128)(2,1)S(1)}, bf16[272,768]{1,0:T(8,128)(2,1)S(1)}, u32[]{:S(2)}, u32[]{:S(2)}) collective-permute-start(bf16[272,768]{1,0:T(8,128)(2,1)S(1)} %dynamic-slice_bitcast_fusion.5), channel_id=1, source_target_pairs={{0,1},{1,0},{2,3},{3,2},{4,5},{5,4},{6,7},{7,6},{8,9},{9,8},{10,11... | collective-permute-start | bytes 1253384 | tf_op jit(solution)/shard_map/ppermute | solution.py:45
  252.8 27.2 %collective-permute-start.28 = (bf16[2,2,192,1024]{3,2,1,0:T(8,128)(2,1)}, bf16[2,2,192,1024]{3,2,1,0:T(8,128)(2,1)}, u32[]{:S(2)}, u32[]{:S(2)}) collective-permute-start(bf16[2,2,192,1024]{3,2,1,0:T(8,128)(2,1)} %get-tuple-element.387), channel_id=1, source_target_pairs={{0,8},{8,0},{16,24},{24,16},{1,9},{9,1},{17,25},{25,17},{2,10},{10... | collective-permute-start | bytes 4718600 | tf_op jit(solution)/shard_map/ppermute | solution.py:33
  252.9 27.1 %collective-permute-start.29 = (bf16[2,2,192,1024]{3,2,1,0:T(8,128)(2,1)}, bf16[2,2,192,1024]{3,2,1,0:T(8,128)(2,1)}, u32[]{:S(2)}, u32[]{:S(2)}) collective-permute-start(bf16[2,2,192,1024]{3,2,1,0:T(8,128)(2,1)} %get-tuple-element.396), channel_id=1, source_target_pairs={{0,8},{8,0},{16,24},{24,16},{1,9},{9,1},{17,25},{25,17},{2,10},{10... | collective-permute-start | bytes 4718600 | tf_op jit(solution)/shard_map/ppermute | solution.py:33
  255.9 22.3 %collective-permute-start.30 = (bf16[256,768]{1,0:T(8,128)(2,1)}, bf16[256,768]{1,0:T(8,128)(2,1)}, u32[]{:S(2)}, u32[]{:S(2)}) collective-permute-start(bf16[256,768]{1,0:T(8,128)(2,1)} %dynamic-slice_bitcast_fusion.12), channel_id=1, source_target_pairs={{0,1},{1,0},{2,3},{3,2},{4,5},{5,4},{6,7},{7,6},{8,9},{9,8},{10,11... | collective-permute-start | bytes 1179656 | tf_op jit(solution)/shard_map/ppermute | solution.py:45
  256.9 21.3 %collective-permute-start.27 = (bf16[272,768]{1,0:T(8,128)(2,1)}, bf16[272,768]{1,0:T(8,128)(2,1)}, u32[]{:S(2)}, u32[]{:S(2)}) collective-permute-start(bf16[272,768]{1,0:T(8,128)(2,1)} %fusion.9), channel_id=1, source_target_pairs={{0,6},{2,0},{4,2},{6,4},{1,7},{3,1},{5,3},{7,5},{8,14},{10,8},{12,... | collective-permute-start | bytes 1253384 | tf_op jit(solution)/shard_map/ppermute | solution.py:50
  258.8 21.2 %collective-permute-start.26 = (bf16[272,768]{1,0:T(8,128)(2,1)}, bf16[272,768]{1,0:T(8,128)(2,1)}, u32[]{:S(2)}, u32[]{:S(2)}) collective-permute-start(bf16[272,768]{1,0:T(8,128)(2,1)} %fusion.10), channel_id=1, source_target_pairs={{0,2},{2,4},{4,6},{6,0},{1,3},{3,5},{5,7},{7,1},{8,10},{10,12},{12... | collective-permute-start | bytes 1253384 | tf_op jit(solution)/shard_map/ppermute | solution.py:50
  281.5 24.1 %collective-permute-start.31 = (bf16[2,192,1024]{2,1,0:T(8,128)(2,1)S(1)}, bf16[2,192,1024]{2,1,0:T(8,128)(2,1)}, u32[]{:S(2)}, u32[]{:S(2)}) collective-permute-start(bf16[2,192,1024]{2,1,0:T(8,128)(2,1)S(1)} %fusion.22), channel_id=1, source_target_pairs={{0,16},{8,24},{16,0},{24,8},{1,17},{9,25},{17,1},{25,9},{2,18},{10... | collective-permute-start | bytes 2359304 | tf_op jit(solution)/shard_map/ppermute | solution.py:40
  284.4 21.2 %collective-permute-start.32 = (bf16[2,2,192,1024]{3,2,1,0:T(8,128)(2,1)}, bf16[2,2,192,1024]{3,2,1,0:T(8,128)(2,1)}, u32[]{:S(2)}, u32[]{:S(2)}) collective-permute-start(bf16[2,2,192,1024]{3,2,1,0:T(8,128)(2,1)} %get-tuple-element.416), channel_id=1, source_target_pairs={{0,8},{8,0},{16,24},{24,16},{1,9},{9,1},{17,25},{25,17},{2,10},{10... | collective-permute-start | bytes 4718600 | tf_op jit(solution)/shard_map/ppermute | solution.py:33
  307.0 21.1 %collective-permute-start.35 = (bf16[2,192,1024]{2,1,0:T(8,128)(2,1)S(1)}, bf16[2,192,1024]{2,1,0:T(8,128)(2,1)S(1)}, u32[]{:S(2)}, u32[]{:S(2)}) collective-permute-start(bf16[2,192,1024]{2,1,0:T(8,128)(2,1)S(1)} %fusion.23), channel_id=1, source_target_pairs={{0,16},{8,24},{16,0},{24,8},{1,17},{9,25},{17,1},{25,9},{2,18},{10... | collective-permute-start | bytes 2359304 | tf_op jit(solution)/shard_map/ppermute | solution.py:40
  307.2 20.9 %collective-permute-start.37 = (bf16[256,768]{1,0:T(8,128)(2,1)S(1)}, bf16[256,768]{1,0:T(8,128)(2,1)S(1)}, u32[]{:S(2)}, u32[]{:S(2)}) collective-permute-start(bf16[256,768]{1,0:T(8,128)(2,1)S(1)} %dynamic-slice_bitcast_fusion.9), channel_id=1, source_target_pairs={{0,1},{1,0},{2,3},{3,2},{4,5},{5,4},{6,7},{7,6},{8,9},{9,8},{10,11... | collective-permute-start | bytes 1179656 | tf_op jit(solution)/shard_map/ppermute | solution.py:45
  309.0 19.1 %collective-permute-start.36 = (bf16[256,768]{1,0:T(8,128)(2,1)S(1)}, bf16[256,768]{1,0:T(8,128)(2,1)S(1)}, u32[]{:S(2)}, u32[]{:S(2)}) collective-permute-start(bf16[256,768]{1,0:T(8,128)(2,1)S(1)} %get-tuple-element.440), channel_id=1, source_target_pairs={{0,1},{1,0},{2,3},{3,2},{4,5},{5,4},{6,7},{7,6},{8,9},{9,8},{10,11... | collective-permute-start | bytes 1179656 | tf_op jit(solution)/shard_map/ppermute | solution.py:45
  332.0 145.3 %all-gather.13.cloned.1.call-start = ((), (), s32[]{:S(2)}) async-start(), calls=%async_computation.5 | async-start | bytes 7077888 | tf_op jit(solution)/shard_map/all_gather | solution.py:1043
  335.7 24.2 %collective-permute-start.38 = (bf16[2,192,1024]{2,1,0:T(8,128)(2,1)}, bf16[2,192,1024]{2,1,0:T(8,128)(2,1)}, u32[]{:S(2)}, u32[]{:S(2)}) collective-permute-start(bf16[2,192,1024]{2,1,0:T(8,128)(2,1)} %fusion.24), channel_id=1, source_target_pairs={{0,16},{8,24},{16,0},{24,8},{1,17},{9,25},{17,1},{25,9},{2,18},{10... | collective-permute-start | bytes 2359304 | tf_op jit(solution)/shard_map/ppermute | solution.py:40
  386.3 23.1 %collective-permute-start.42 = (bf16[2,2,192,1024]{3,2,1,0:T(8,128)(2,1)}, bf16[2,2,192,1024]{3,2,1,0:T(8,128)(2,1)}, u32[]{:S(2)}, u32[]{:S(2)}) collective-permute-start(bf16[2,2,192,1024]{3,2,1,0:T(8,128)(2,1)} %get-tuple-element.473), channel_id=1, source_target_pairs={{0,8},{8,0},{16,24},{24,16},{1,9},{9,1},{17,25},{25,17},{2,10},{10... | collective-permute-start | bytes 4718600 | tf_op jit(solution)/shard_map/ppermute | solution.py:33
  388.0 160.4 %all-gather.15.cloned.1.call-start = ((), (), s32[]{:S(2)}) async-start(), calls=%async_computation.6 | async-start | bytes 1474560 | tf_op jit(solution)/shard_map/all_gather | solution.py:1093
  388.1 21.2 %collective-permute-start.43 = (bf16[2,192,768]{2,1,0:T(8,128)(2,1)}, bf16[2,192,768]{2,1,0:T(8,128)(2,1)S(1)}, u32[]{:S(2)}, u32[]{:S(2)}) collective-permute-start(bf16[2,192,768]{2,1,0:T(8,128)(2,1)} %get-tuple-element.477), channel_id=1, source_target_pairs={{0,8},{8,0},{16,24},{24,16},{1,9},{9,1},{17,25},{25,17},{2,10},{10... | collective-permute-start | bytes 1769480 | tf_op jit(solution)/shard_map/ppermute | solution.py:33
  388.7 20.6 %collective-permute-start.40 = (bf16[256,768]{1,0:T(8,128)(2,1)S(1)}, bf16[256,768]{1,0:T(8,128)(2,1)S(1)}, u32[]{:S(2)}, u32[]{:S(2)}) collective-permute-start(bf16[256,768]{1,0:T(8,128)(2,1)S(1)} %dynamic-slice_bitcast_fusion.7), channel_id=1, source_target_pairs={{0,1},{1,0},{2,3},{3,2},{4,5},{5,4},{6,7},{7,6},{8,9},{9,8},{10,11... | collective-permute-start | bytes 1179656 | tf_op jit(solution)/shard_map/ppermute | solution.py:45
  390.6 18.8 %collective-permute-start.39 = (bf16[256,768]{1,0:T(8,128)(2,1)S(1)}, bf16[256,768]{1,0:T(8,128)(2,1)S(1)}, u32[]{:S(2)}, u32[]{:S(2)}) collective-permute-start(bf16[256,768]{1,0:T(8,128)(2,1)S(1)} %dynamic-slice_bitcast_fusion.8), channel_id=1, source_target_pairs={{0,1},{1,0},{2,3},{3,2},{4,5},{5,4},{6,7},{7,6},{8,9},{9,8},{10,11... | collective-permute-start | bytes 1179656 | tf_op jit(solution)/shard_map/ppermute | solution.py:45
  410.0 24.1 %collective-permute-start.46 = (bf16[2,2,192,1024]{3,2,1,0:T(8,128)(2,1)}, bf16[2,2,192,1024]{3,2,1,0:T(8,128)(2,1)S(1)}, u32[]{:S(2)}, u32[]{:S(2)}) collective-permute-start(bf16[2,2,192,1024]{3,2,1,0:T(8,128)(2,1)} %get-tuple-element.485), channel_id=1, source_target_pairs={{0,8},{8,0},{16,24},{24,16},{1,9},{9,1},{17,25},{25,17},{2,10},{10... | collective-permute-start | bytes 4718600 | tf_op jit(solution)/shard_map/ppermute | solution.py:33
  410.0 24.2 %collective-permute-start.48 = (bf16[2,2,192,1024]{3,2,1,0:T(8,128)(2,1)}, bf16[2,2,192,1024]{3,2,1,0:T(8,128)(2,1)}, u32[]{:S(2)}, u32[]{:S(2)}) collective-permute-start(bf16[2,2,192,1024]{3,2,1,0:T(8,128)(2,1)} %get-tuple-element.488), channel_id=1, source_target_pairs={{0,8},{8,0},{16,24},{24,16},{1,9},{9,1},{17,25},{25,17},{2,10},{10... | collective-permute-start | bytes 4718600 | tf_op jit(solution)/shard_map/ppermute | solution.py:33
  412.0 22.2 %collective-permute-start.47 = (bf16[2,192,1024]{2,1,0:T(8,128)(2,1)S(1)}, bf16[2,192,1024]{2,1,0:T(8,128)(2,1)S(1)}, u32[]{:S(2)}, u32[]{:S(2)}) collective-permute-start(bf16[2,192,1024]{2,1,0:T(8,128)(2,1)S(1)} %fusion.25), channel_id=1, source_target_pairs={{0,16},{8,24},{16,0},{24,8},{1,17},{9,25},{17,1},{25,9},{2,18},{10... | collective-permute-start | bytes 2359304 | tf_op jit(solution)/shard_map/ppermute | solution.py:40
  412.2 21.9 %collective-permute-start.45 = (bf16[256,768]{1,0:T(8,128)(2,1)S(1)}, bf16[256,768]{1,0:T(8,128)(2,1)S(1)}, u32[]{:S(2)}, u32[]{:S(2)}) collective-permute-start(bf16[256,768]{1,0:T(8,128)(2,1)S(1)} %fusion.32), channel_id=1, source_target_pairs={{2,0},{4,2},{6,4},{3,1},{5,3},{7,5},{10,8},{12,10},{14,12},{11,9},... | collective-permute-start | bytes 1179656 | tf_op jit(solution)/shard_map/ppermute | solution.py:61
  413.5 20.6 %collective-permute-start.44 = (bf16[256,768]{1,0:T(8,128)(2,1)S(1)}, bf16[256,768]{1,0:T(8,128)(2,1)S(1)}, u32[]{:S(2)}, u32[]{:S(2)}) collective-permute-start(bf16[256,768]{1,0:T(8,128)(2,1)S(1)} %dynamic-slice_bitcast_fusion.6), channel_id=1, source_target_pairs={{0,1},{1,0},{2,3},{3,2},{4,5},{5,4},{6,7},{7,6},{8,9},{9,8},{10,11... | collective-permute-start | bytes 1179656 | tf_op jit(solution)/shard_map/ppermute | solution.py:45
  434.2 28.1 %collective-permute-start.50 = (bf16[2,192,1664]{2,1,0:T(8,128)(2,1)}, bf16[2,192,1664]{2,1,0:T(8,128)(2,1)}, u32[]{:S(2)}, u32[]{:S(2)}) collective-permute-start(bf16[2,192,1664]{2,1,0:T(8,128)(2,1)} %get-tuple-element.493), channel_id=1, source_target_pairs={{0,8},{8,0},{16,24},{24,16},{1,9},{9,1},{17,25},{25,17},{2,10},{10... | collective-permute-start | bytes 3833864 | tf_op jit(solution)/shard_map/ppermute | solution.py:33
  435.9 26.4 %collective-permute-start.51 = (bf16[2,192,1024]{2,1,0:T(8,128)(2,1)}, bf16[2,192,1024]{2,1,0:T(8,128)(2,1)}, u32[]{:S(2)}, u32[]{:S(2)}) collective-permute-start(bf16[2,192,1024]{2,1,0:T(8,128)(2,1)} %fusion.26), channel_id=1, source_target_pairs={{0,16},{8,24},{16,0},{24,8},{1,17},{9,25},{17,1},{25,9},{2,18},{10... | collective-permute-start | bytes 2359304 | tf_op jit(solution)/shard_map/ppermute | solution.py:40
  439.9 22.4 %collective-permute-start.49 = (bf16[256,768]{1,0:T(8,128)(2,1)}, bf16[256,768]{1,0:T(8,128)(2,1)}, u32[]{:S(2)}, u32[]{:S(2)}) collective-permute-start(bf16[256,768]{1,0:T(8,128)(2,1)} %fusion.31), channel_id=1, source_target_pairs={{2,0},{4,2},{6,4},{3,1},{5,3},{7,5},{10,8},{12,10},{14,12},{11,9},... | collective-permute-start | bytes 1179656 | tf_op jit(solution)/shard_map/ppermute | solution.py:61
  443.0 19.3 %collective-permute-start.52 = (bf16[192,768]{1,0:T(8,128)(2,1)}, bf16[192,768]{1,0:T(8,128)(2,1)}, u32[]{:S(2)}, u32[]{:S(2)}) collective-permute-start(bf16[192,768]{1,0:T(8,128)(2,1)} %fusion.36), channel_id=1, source_target_pairs={{0,16},{8,24},{16,0},{24,8},{1,17},{9,25},{17,1},{25,9},{2,18},{10... | collective-permute-start | bytes 884744 | tf_op jit(solution)/shard_map/ppermute | solution.py:40
  464.7 32.9 %collective-permute-start.54 = (bf16[2,192,1024]{2,1,0:T(8,128)(2,1)}, bf16[2,192,1024]{2,1,0:T(8,128)(2,1)}, u32[]{:S(2)}, u32[]{:S(2)}) collective-permute-start(bf16[2,192,1024]{2,1,0:T(8,128)(2,1)} %fusion.27), channel_id=1, source_target_pairs={{0,16},{8,24},{16,0},{24,8},{1,17},{9,25},{17,1},{25,9},{2,18},{10... | collective-permute-start | bytes 2359304 | tf_op jit(solution)/shard_map/ppermute | solution.py:40
  468.5 29.1 %collective-permute-start.53 = (bf16[192,1664]{1,0:T(8,128)(2,1)}, bf16[192,1664]{1,0:T(8,128)(2,1)}, u32[]{:S(2)}, u32[]{:S(2)}) collective-permute-start(bf16[192,1664]{1,0:T(8,128)(2,1)} %fusion.33), channel_id=1, source_target_pairs={{0,16},{8,24},{16,0},{24,8},{1,17},{9,25},{17,1},{25,9},{2,18},{10... | collective-permute-start | bytes 1916936 | tf_op jit(solution)/shard_map/ppermute | solution.py:40
  468.7 36.1 %collective-permute-start.55 = (bf16[2,192,1024]{2,1,0:T(8,128)(2,1)S(1)}, bf16[2,192,1024]{2,1,0:T(8,128)(2,1)}, u32[]{:S(2)}, u32[]{:S(2)}) collective-permute-start(bf16[2,192,1024]{2,1,0:T(8,128)(2,1)S(1)} %fusion.3), channel_id=1, source_target_pairs={{0,2},{2,0},{4,6},{6,4},{1,3},{3,1},{5,7},{7,5},{8,10},{10,8},{12,... | collective-permute-start | bytes 2359304 | tf_op jit(solution)/shard_map/ppermute | solution.py:55
  470.6 115.3 %all-reduce.5.cloned.1.call-start = ((), (), s32[]{:S(2)}) async-start(), calls=%async_computation.2 | async-start | bytes 1277952 | tf_op jit(solution)/shard_map/psum | solution.py:1110
  504.8 28.8 %collective-permute-start.56 = (bf16[2,192,1024]{2,1,0:T(8,128)(2,1)}, bf16[2,192,1024]{2,1,0:T(8,128)(2,1)}, u32[]{:S(2)}, u32[]{:S(2)}) collective-permute-start(bf16[2,192,1024]{2,1,0:T(8,128)(2,1)} %fusion.2), channel_id=1, source_target_pairs={{0,2},{2,0},{4,6},{6,4},{1,3},{3,1},{5,7},{7,5},{8,10},{10,8},{12,... | collective-permute-start | bytes 2359304 | tf_op jit(solution)/shard_map/ppermute | solution.py:55
  504.9 28.8 %collective-permute-start.57 = (bf16[256,768]{1,0:T(8,128)(2,1)}, bf16[256,768]{1,0:T(8,128)(2,1)}, u32[]{:S(2)}, u32[]{:S(2)}) collective-permute-start(bf16[256,768]{1,0:T(8,128)(2,1)} %fusion.20), channel_id=1, source_target_pairs={{0,1},{1,0},{2,3},{3,2},{4,5},{5,4},{6,7},{7,6},{8,9},{9,8},{10,11... | collective-permute-start | bytes 1179656 | tf_op jit(solution)/shard_map/ppermute | solution.py:45
  533.7 57.4 %collective-permute-start.59 = (bf16[2,192,1024]{2,1,0:T(8,128)(2,1)}, bf16[2,192,1024]{2,1,0:T(8,128)(2,1)}, u32[]{:S(2)}, u32[]{:S(2)}) collective-permute-start(bf16[2,192,1024]{2,1,0:T(8,128)(2,1)} %fusion.1), channel_id=1, source_target_pairs={{0,2},{2,0},{4,6},{6,4},{1,3},{3,1},{5,7},{7,5},{8,10},{10,8},{12,... | collective-permute-start | bytes 2359304 | tf_op jit(solution)/shard_map/ppermute | solution.py:55
  (84 other events, 703.3 us)
Sparse Core Ops, SparseCore 0:
  22.1 78.3 all-gather.8
  170.2 63.8 all-gather.10
  332.1 35.2 reduce-scatter.1
  388.2 78.1 all-gather.12
  470.7 37.6 all-gather.14
  546.4 39.4 all-reduce.4

commit v3 on v2

--- a/solution.py
+++ b/solution.py
@@ -13,7 +13,7 @@
 F32 = jnp.float32
 BF16 = jnp.bfloat16
 VMEM_BYTES = 56 * 1024 * 1024
-COST_SCALE = 0.25
+COST_SCALE = 0.1
 
 
 def dot(left, right):
@@ -38,6 +38,11 @@
     pairs = size // 2
     route = [(i, ((i // 2 + distance) % pairs) * 2 + i % 2) for i in range(size)]
     return lax.ppermute(block, "fsdp", route)
+
+
+def pair_swap(block, reach):
+    size = lax.axis_size("fsdp")
+    return lax.ppermute(block, "fsdp", [(i, i ^ (2 * reach)) for i in range(size)])
 
 
 def tp_shift(block, distance):
@@ -133,53 +138,277 @@
     return jnp.concatenate([table] * copies, axis=1)[:, :width]
 
 
-def project_kernel(with_query, count, *refs):
-    sources = refs[:count]
-    gain_ref, w_ref, cos_ref, sin_ref = refs[count : count + 4]
-    hid_ref, k_ref, v_ref = refs[len(refs) - 3 - with_query :][:3]
+def rotated(values, cosine, sine):
+    return (values * cosine + swap_halves(values) * sine).astype(BF16)
+
+
+def project_rows(inputs, gain, weights, cos_ref, sin_ref, hid_ref, k_ref, v_ref):
+    scale = lax.rsqrt(jnp.mean(inputs * inputs, axis=-1, keepdims=True) + EPS)
+    hidden = (inputs * scale * gain).astype(BF16)
+    hid_ref[...] = hidden
     width = k_ref.shape[1]
-    cosine = widen(cos_ref[...], width)
-    sine = widen(sin_ref[...], width)
-    for i, tok_ref in enumerate(sources):
-
-        @pl.when(pl.program_id(0) == i)
-        def _():
-            inputs = tok_ref[...].astype(F32)
-            scale = lax.rsqrt(jnp.mean(inputs * inputs, axis=-1, keepdims=True) + EPS)
-            hidden = (inputs * scale * gain_ref[...]).astype(BF16)
-            hid_ref[...] = hidden
-            keys = dot(hidden, w_ref[:, :width])
-            k_ref[...] = (keys * cosine + swap_halves(keys) * sine).astype(BF16)
-            v_ref[...] = dot(hidden, w_ref[:, width : 2 * width]).astype(BF16)
-            if with_query and i == count - 1:
-                query = dot(hidden, w_ref[:, 2 * width : 3 * width])
-                turned = (query * cosine + swap_halves(query) * sine).astype(BF16)
-                refs[-1][...] = turned * jnp.asarray(HD**-0.5, BF16)
-
-
-def project(sources, gain, weights, cosine, sine, width, blocks, first, saved):
-    rows, features = sources[0].shape
-    count = len(sources)
-    with_query = first + count == blocks
-    shapes = [(blocks * rows, features), (blocks * rows, width), (blocks * rows, width)]
-    outs = [jax.ShapeDtypeStruct(shape, BF16) for shape in shapes]
-    specs = [pl.BlockSpec((rows, shape[1]), lambda i: (i + first, 0)) for shape in shapes]
-    if with_query:
-        outs.append(jax.ShapeDtypeStruct((rows, width), BF16))
-        specs.append(whole((rows, width)))
-    table = pl.BlockSpec((rows, cosine.shape[1]), lambda i: (i + first, 0))
-    return pl.pallas_call(
-        functools.partial(project_kernel, with_query, count),
-        grid=(count,),
-        in_specs=[whole(source.shape) for source in sources]
-        + [whole(gain.shape), whole(weights.shape), table, table]
-        + [pl.BlockSpec(memory_space=pl.ANY)] * len(saved),
-        out_specs=specs,
-        out_shape=outs,
-        input_output_aliases={count + 4 + i: i for i in range(len(saved))},
-        compiler_params=params(),
-        cost_estimate=cost(1 + 3 * count),
-    )(*sources, gain, weights, cosine, sine, *saved)
+    k_ref[...] = rotated(
+        dot(hidden, weights[:, :width]), widen(cos_ref[...], width), widen(sin_ref[...], width))
+    v_ref[...] = dot(hidden, weights[:, width : 2 * width]).astype(BF16)
+    return hidden
+
+
+def project_near_kernel(parts, pairs, meta_ref, tok_ref, *refs):
+    prev_refs, refs = refs[:parts], refs[parts:]
+    same_refs, cross_refs, refs = refs[:pairs], refs[pairs : 2 * pairs], refs[2 * pairs :]
+    gain_ref, cos_ref, sin_ref, hid_ref, k_ref, v_ref, q_ref, w_ref, prev_ref, w_all, x_all = refs
+    tok, features = x_all.shape[1:]
+    share, columns = w_all.shape[1:]
+
+    @pl.when(pl.program_id(0) == 0)
+    def _():
+        for d in range(pairs):
+            row = 2 * lax.rem(meta_ref[1] + pairs - d, pairs)
+            w_all[row + meta_ref[2]] = same_refs[d][...]
+            w_all[row + 1 - meta_ref[2]] = cross_refs[d][...]
+        for j in range(parts):
+            x_all[lax.rem(meta_ref[0] + parts - j, parts)] = prev_refs[j][...]
+        weights = w_all[...].reshape(2 * pairs * share, columns)
+        w_ref[...] = weights
+        inputs = x_all[...].reshape(parts * tok, features)
+        prev_ref[...] = inputs
+        project_rows(inputs.astype(F32), gain_ref[...], weights, cos_ref, sin_ref, hid_ref, k_ref, v_ref)
+
+    @pl.when(pl.program_id(0) == 1)
+    def _():
+        weights = w_all[...].reshape(2 * pairs * share, columns)
+        hidden = project_rows(
+            tok_ref[...].astype(F32), gain_ref[...], weights, cos_ref, sin_ref, hid_ref, k_ref, v_ref)
+        width = k_ref.shape[1]
+        query = dot(hidden, weights[:, 2 * width :])
+        q_ref[...] = rotated(
+            query, widen(cos_ref[...], width), widen(sin_ref[...], width)) * jnp.asarray(HD**-0.5, BF16)
+
+
+def project_near(meta, tokens, prev_pieces, same, cross, gain, cosine, sine):
+    rows, features = tokens.shape
+    share, columns = same[0].shape
+    width = columns // 3
+    tok = prev_pieces[0].shape[0]
+    count = 2 * len(same) * share
+    shapes = [(3 * rows, features), (3 * rows, width), (3 * rows, width)]
+    block = lambda i, meta: (i + 1, 0)
+    others = [(rows, width), (count, columns), (rows, features)]
+    operands = [tokens, *prev_pieces, *same, *cross, gain]
+    table = pl.BlockSpec((rows, cosine.shape[1]), block)
+    return pl.pallas_call(
+        functools.partial(project_near_kernel, len(prev_pieces), len(same)),
+        grid_spec=pltpu.PrefetchScalarGridSpec(
+            num_scalar_prefetch=1,
+            grid=(2,),
+            in_specs=[whole(o.shape) for o in operands] + [table, table],
+            out_specs=[pl.BlockSpec((rows, shape[1]), block) for shape in shapes]
+            + [whole(shape) for shape in others],
+            scratch_shapes=[
+                pltpu.VMEM((2 * len(same), share, columns), BF16),
+                pltpu.VMEM((len(prev_pieces), tok, features), BF16),
+            ],
+        ),
+        out_shape=[jax.ShapeDtypeStruct(shape, BF16) for shape in shapes + others],
+        compiler_params=params(),
+        cost_estimate=cost(7),
+    )(meta, *operands, cosine, sine)
+
+
+def project_far_kernel(parts, meta_ref, *refs):
+    prev_refs, refs = refs[:parts], refs[parts:]
+    w_ref, gain_ref, cos_ref, sin_ref, _, _, _, hid_ref, k_ref, v_ref, prev_ref, x_all = refs
+    tok, features = x_all.shape[1:]
+    for j in range(parts):
+        x_all[lax.rem(meta_ref[0] + parts - j, parts)] = prev_refs[j][...]
+    inputs = x_all[...].reshape(parts * tok, features)
+    prev_ref[...] = inputs
+    project_rows(inputs.astype(F32), gain_ref[...], w_ref[...], cos_ref, sin_ref, hid_ref, k_ref, v_ref)
+
+
+def project_far(meta, prev_pieces, weights, gain, cosine, sine, saved):
+    tok, features = prev_pieces[0].shape
+    rows = tok * len(prev_pieces)
+    width = weights.shape[1] // 3
+    first = lambda i, meta: (0, 0)
+    operands = [*prev_pieces, weights, gain]
+    table = pl.BlockSpec((rows, cosine.shape[1]), first)
+    return pl.pallas_call(
+        functools.partial(project_far_kernel, len(prev_pieces)),
+        grid_spec=pltpu.PrefetchScalarGridSpec(
+            num_scalar_prefetch=1,
+            grid=(1,),
+            in_specs=[whole(o.shape) for o in operands] + [table, table]
+            + [pl.BlockSpec(memory_space=pl.ANY)] * 3,
+            out_specs=[pl.BlockSpec((rows, one.shape[1]), first) for one in saved]
+            + [whole((rows, features))],
+            scratch_shapes=[pltpu.VMEM((len(prev_pieces), tok, features), BF16)],
+        ),
+        out_shape=[jax.ShapeDtypeStruct(one.shape, BF16) for one in saved]
+        + [jax.ShapeDtypeStruct((rows, features), BF16)],
+        input_output_aliases={1 + len(operands) + 2 + i: i for i in range(3)},
+        compiler_params=params(),
+        cost_estimate=cost(4),
+    )(meta, *operands, cosine, sine, *saved)
+
+
+def prepare_kernel(parts, meta_ref, routes_ref, cot_ref, rates_ref, seg_ref, *refs):
+    cos_ref, sin_ref, kseg_ref, qseg_ref, hits_ref = refs[:5]
+    mine_ref, other_refs, seg_all = refs[5], refs[6:-1], refs[-1]
+    block, width = cot_ref.shape
+    tok = block // parts
+    experts = hits_ref.shape[0]
+    rows, lanes = cos_ref.shape
+    short = 64
+    origin = (meta_ref[1] - 2) * block
+    far = (lax.broadcasted_iota(jnp.int32, (rows // short, lanes), 0) * short + origin).astype(F32) * rates_ref[...]
+    near = lax.broadcasted_iota(jnp.int32, (short, lanes), 0).astype(F32) * rates_ref[...]
+    far_cos, far_sin, near_cos, near_sin = jnp.cos(far), jnp.sin(far), jnp.cos(near), jnp.sin(near)
+    sign = jnp.where(lax.broadcasted_iota(jnp.int32, (short, lanes), 1) % HD < HD // 2, -1.0, 1.0)
+    signed_sin, signed_cos = sign * near_sin, sign * near_cos
+    for h in range(rows // short):
+        part = slice(h * short, (h + 1) * short)
+        one_cos, one_sin = far_cos[h : h + 1], far_sin[h : h + 1]
+        cos_ref[part] = one_cos * near_cos - one_sin * near_sin
+        sin_ref[part] = one_sin * signed_cos + one_cos * signed_sin
+    seg_all[:, : 2 * block] = jnp.full((1, 2 * block), -1, jnp.int32)
+    seg_all[:, 2 * block :] = seg_ref[...]
+    kseg = seg_all[:, pl.ds(pl.multiple_of(meta_ref[1] * block, block), rows)]
+    qseg_ref[...] = kseg[:, rows - block :]
+    kseg_ref[...] = jnp.broadcast_to(kseg, (8, rows)).T[:, :1]
+    row = lax.broadcasted_iota(jnp.int32, (experts, block), 0)
+    named = row == routes_ref[0:1, :]
+    for j in range(1, routes_ref.shape[0]):
+        named = named | (row == routes_ref[j : j + 1, :])
+    hits = jnp.where(named, 1.0, 0.0).astype(F32)
+    before = lax.broadcasted_iota(jnp.int32, (block, block), 0) < lax.broadcasted_iota(jnp.int32, (block, block), 1)
+    rank = dot(hits.astype(BF16), jnp.where(before, 1.0, 0.0).astype(BF16))
+    hits_ref[...] = hits
+    table = jnp.concatenate([jnp.where(named, rank, -1.0), jnp.zeros((16 - experts, block), F32)], axis=0)
+    mine_ref[tok:, :] = jnp.concatenate([table, jnp.zeros((16, width - block), F32)], axis=1).astype(BF16)
+    for j, ref in enumerate((mine_ref,) + other_refs):
+        start = lax.rem(meta_ref[0] + parts - j, parts) * tok
+        ref[:tok, :] = cot_ref[pl.ds(pl.multiple_of(start, tok), tok), :]
+
+
+def prepare(meta, parts, experts, routes_t, cotangent, segments):
+    block, width = cotangent.shape
+    tok = block // parts
+    index = jnp.arange(2 * HD, dtype=jnp.int32)
+    rates = (10000.0 ** (-2.0 * (index % (HD // 2)).astype(F32) / HD))[None, :]
+    shapes = [
+        ((3 * block, 2 * HD), F32), ((3 * block, 2 * HD), F32), ((3 * block, 1), jnp.int32), ((1, block), jnp.int32),
+        ((experts, block), F32), ((tok + 16, width), BF16),
+    ] + [((tok, width), BF16)] * (parts - 1)
+    operands = (routes_t, cotangent, rates, segments)
+    return pl.pallas_call(
+        functools.partial(prepare_kernel, parts),
+        grid_spec=pltpu.PrefetchScalarGridSpec(
+            num_scalar_prefetch=1,
+            grid=(1,),
+            in_specs=[whole(o.shape) for o in operands],
+            out_specs=[whole(shape) for shape, _ in shapes],
+            scratch_shapes=[pltpu.VMEM((1, segments.shape[1] + 2 * block), jnp.int32)],
+        ),
+        out_shape=[jax.ShapeDtypeStruct(shape, kind) for shape, kind in shapes],
+        compiler_params=params(),
+        cost_estimate=cost(3),
+    )(meta, *operands)
+
+
+def bundle_kernel(plane_ref, *refs):
+    stacks, shared, out_ref = refs[:3], refs[3:-1], refs[-1]
+    owned = stacks[0].shape[0]
+    for i, ref in enumerate(stacks):
+        out_ref[i * owned : (i + 1) * owned] = ref[...]
+    if shared:
+        units = shared[0].shape[1]
+        out_ref[3 * owned] = jnp.zeros(out_ref.shape[1:], BF16)
+        for i, ref in enumerate(shared):
+            out_ref[3 * owned, :, i * units : (i + 1) * units] = ref[...]
+
+
+def bundle(plane, owned, units, stacks, shared):
+    _, share, hidden = stacks[0].shape
+    count = 3 * owned + bool(shared)
+    return pl.pallas_call(
+        bundle_kernel,
+        grid_spec=pltpu.PrefetchScalarGridSpec(
+            num_scalar_prefetch=1,
+            grid=(1,),
+            in_specs=[pl.BlockSpec((owned, share, hidden), lambda i, plane: (plane[0], 0, 0))] * 3
+            + [pl.BlockSpec((share, units), lambda i, plane: (0, plane[0]))] * len(shared),
+            out_specs=whole((count, share, hidden)),
+        ),
+        out_shape=jax.ShapeDtypeStruct((count, share, hidden), BF16),
+        compiler_params=params(),
+        cost_estimate=cost(3),
+    )(plane.astype(jnp.int32)[None], *stacks, *shared)
+
+
+def finish_kernel(meta_ref, mine_ref, *refs):
+    count = len(refs) - 6
+    pieces = (mine_ref,) + refs[:count]
+    k_ref, v_ref, q_ref, o_ref, small_ref, all_ref = refs[count:]
+    total = len(pieces)
+    rows = mine_ref.shape[0]
+    for d, ref in enumerate(pieces):
+        all_ref[lax.rem(meta_ref[0] + total - d, total)] = ref[...].astype(F32)
+    whole_rows = all_ref[...].reshape(total * rows, mine_ref.shape[1])
+    share, cols = k_ref.shape
+    for i, ref in enumerate((k_ref, v_ref, q_ref, o_ref)):
+        ref[...] = whole_rows[:share, i * cols : (i + 1) * cols]
+    small_ref[...] = whole_rows[share : share + 16, : small_ref.shape[1]]
+
+
+def finish(meta, pieces, share, cols):
+    rows, columns = pieces[0].shape
+    shapes = [(share, cols)] * 4 + [(16, columns)]
+    return pl.pallas_call(
+        finish_kernel,
+        grid_spec=pltpu.PrefetchScalarGridSpec(
+            num_scalar_prefetch=1,
+            grid=(1,),
+            in_specs=[whole(piece.shape) for piece in pieces],
+            out_specs=[whole(shape) for shape in shapes],
+            scratch_shapes=[pltpu.VMEM((len(pieces), rows, columns), F32)],
+        ),
+        out_shape=[jax.ShapeDtypeStruct(shape, F32) for shape in shapes],
+        compiler_params=params(),
+        cost_estimate=cost(2),
+    )(meta, *pieces)
+
+
+def pack_kernel(lane_ref, k_ref, v_ref, q_ref, router_ref, gains_ref, tok_ref, qkv_ref, small_ref, mine_ref):
+    width = k_ref.shape[1]
+    for i, ref in enumerate((k_ref, v_ref, q_ref)):
+        qkv_ref[:, i * width : (i + 1) * width] = ref[...]
+    experts, share = router_ref.shape
+    small_ref[...] = jnp.concatenate(
+        [router_ref[...].astype(F32), gains_ref[...].astype(F32),
+         jnp.zeros((small_ref.shape[0] - experts - 2, share), F32)], axis=0).astype(BF16)
+    mine_ref[...] = tok_ref[...]
+
+
+def pack(lane, parts, key_weight, value_weight, query_weight, router_t, gains, tokens):
+    rows, width = tokens.shape
+    share, cols = key_weight.shape
+    part = (rows // parts, width)
+    shapes = [(share, 3 * cols), (16, share), part]
+    operands = (key_weight, value_weight, query_weight, router_t, gains)
+    return pl.pallas_call(
+        pack_kernel,
+        grid_spec=pltpu.PrefetchScalarGridSpec(
+            num_scalar_prefetch=1,
+            grid=(1,),
+            in_specs=[whole(o.shape) for o in operands]
+            + [pl.BlockSpec(part, lambda i, lane: (lane[0], 0))],
+            out_specs=[whole(shape) for shape in shapes],
+        ),
+        out_shape=[jax.ShapeDtypeStruct(shape, BF16) for shape in shapes],
+        compiler_params=params(),
+        cost_estimate=cost(2),
+    )(lane.astype(jnp.int32)[None], *operands, tokens)
 
 
 def mask_bias(kseg, qseg, keys, queries):
@@ -493,16 +722,16 @@
     )(meta, *operands, *saved)
 
 
-def expert_again(d, capacity, parts, experts, meta, inputs, cots, weights, router_t, saved):
+def expert_again(first, steps, capacity, parts, experts, meta, inputs, cots, weights, router_t, saved):
     blocks, block, width = inputs.shape
     hidden = weights.shape[3]
     shapes = expert_shapes(weights.shape[1] // 3, capacity, width, hidden)
-    here = lambda i, meta: d
-    return pl.pallas_call(
-        functools.partial(expert_kernel, capacity, parts, experts, False, 1, len(saved)),
+    here = lambda i, meta: first + i
+    return pl.pallas_call(
+        functools.partial(expert_kernel, capacity, parts, experts, False, steps, len(saved)),
         grid_spec=pltpu.PrefetchScalarGridSpec(
             num_scalar_prefetch=1,
-            grid=(1,),
+            grid=(steps,),
             in_specs=[placed(inputs.shape[1:], here), placed(cots.shape[1:], here)]
             + [whole(weights.shape), whole(router_t.shape)]
             + [pl.BlockSpec(memory_space=pl.ANY)] * len(saved),
@@ -511,8 +740,36 @@
         out_shape=[jax.ShapeDtypeStruct((blocks,) + shape, BF16) for shape in shapes],
         input_output_aliases={5 + i: i for i in range(len(saved))},
         compiler_params=params(),
-        cost_estimate=cost(9),
+        cost_estimate=cost(6 * steps),
     )(meta, inputs, cots, weights, router_t, *saved)
+
+
+def pair_sum_kernel(index_ref, kept_ref, got_ref, *refs):
+    total = kept_ref[0].astype(F32) + got_ref[0].astype(F32)
+    for ref in refs[:-1]:
+        total = total + ref[...].astype(F32)
+    refs[-1][...] = total.astype(BF16)
+
+
+def pair_sum(index, kept, got, far):
+    shape = kept.shape[1:]
+    steps = shape[0] if len(shape) == 3 else 1
+    part = (shape[0] // steps,) + shape[1:]
+    rest = (0,) * (len(shape) - 1)
+    picked = pl.BlockSpec((1,) + part, lambda i, index: (index[0], i) + rest)
+    plain = pl.BlockSpec(part, lambda i, index: (i,) + rest)
+    return pl.pallas_call(
+        pair_sum_kernel,
+        grid_spec=pltpu.PrefetchScalarGridSpec(
+            num_scalar_prefetch=1,
+            grid=(steps,),
+            in_specs=[picked, picked] + [plain] * len(far),
+            out_specs=plain,
+        ),
+        out_shape=jax.ShapeDtypeStruct(shape, BF16),
+        compiler_params=params(),
+        cost_estimate=cost(2),
+    )(index.astype(jnp.int32)[None], kept, got, *far)
 
 
 def split_rows(value, core, sent_ref, kept_ref, *at):
@@ -537,8 +794,7 @@
     steps, owned, slots, width = left.shape
     columns = right.shape[3]
     share = width // (2 * pairs)
-    parts = 2 if columns % 256 == 0 else 1
-    wide = columns // parts
+    parts, wide = 1, columns
     shape = jax.ShapeDtypeStruct((pairs, owned, share, columns), BF16)
     spec = pl.BlockSpec((pairs, 1, share, wide), lambda j, i, core: (0, j, 0, i))
     return pl.pallas_call(
@@ -594,7 +850,7 @@
     )(core, *operands)
 
 
-def attn_grad_kernel(core_ref, hid_ref, dk_ref, dv_ref, dq_ref, gm_ref, at_ref, small_ref, sent_ref, kept_ref):
+def attn_grad_kernel(core_ref, hid_ref, dk_ref, dv_ref, dq_ref, gm_ref, at_ref, sent_ref, kept_ref):
     lead = hid_ref.shape[0] - dq_ref.shape[0]
     value = jnp.concatenate(
         [
@@ -602,17 +858,16 @@
             dot_tn(hid_ref[...], dv_ref[...]),
             dot_tn(hid_ref[lead:, :], dq_ref[...]),
             dot_tn(gm_ref[...], at_ref[...]),
-            small_ref[...].T,
         ],
         axis=1,
     )
     split_rows(value, core_ref[0], sent_ref, kept_ref)
 
 
-def attn_grads_of(core, hid, dk, dv, dq, grad_mixed_low, attended, small, pairs):
+def attn_grads_of(core, hid, dk, dv, dq, grad_mixed_low, attended, pairs):
     width, cols = hid.shape[1], dk.shape[1]
-    shape = jax.ShapeDtypeStruct((pairs, width // (2 * pairs), 4 * cols + small.shape[0]), BF16)
-    operands = (hid, dk, dv, dq, grad_mixed_low, attended, small)
+    shape = jax.ShapeDtypeStruct((pairs, width // (2 * pairs), 4 * cols), BF16)
+    operands = (hid, dk, dv, dq, grad_mixed_low, attended)
     return pl.pallas_call(
         attn_grad_kernel,
         grid_spec=pltpu.PrefetchScalarGridSpec(
@@ -670,41 +925,35 @@
     )(*sources, dk, dv, dq, weights)
 
 
-def collect_kernel(turned, places_ref, first_ref, second_ref, out_ref):
-    step = pl.program_id(0)
-    for half, ref in enumerate((first_ref, second_ref)):
-
-        @pl.when(step // (pl.num_programs(0) // 2) == half)
+def collect_kernel(places_ref, *refs):
+    group = pl.num_programs(0) // (len(refs) - 1)
+    for i, piece_ref in enumerate(refs[:-1]):
+
+        @pl.when(pl.program_id(0) // group == i)
         def _():
-            piece = ref[0, 0].astype(F32)
-            out_ref[0] = piece.T if turned else piece
-
-
-def collect(places, first, second, skip, owned, turned):
-    rows, columns = first.shape[2:]
-    count = 4 * owned
-    half = 2 * owned
-    block = (1, columns, rows) if turned else (1, rows, columns)
-
-    def part(start, low):
-        def index(i, places):
-            local = jnp.clip(i - start, 0, half - 1)
-            return (local // owned, low + local % owned, 0, 0)
-
-        return pl.BlockSpec((1, 1, rows, columns), index)
-
-    return pl.pallas_call(
-        functools.partial(collect_kernel, turned),
+            refs[-1][...] = piece_ref[...].astype(F32)
+
+
+def collect(places, pieces):
+    group, rows, columns = pieces[0].shape
+    block = (1, rows, columns)
+
+    def part(i):
+        return pl.BlockSpec(block, lambda step, places: (jnp.clip(step - i * group, 0, group - 1), 0, 0))
+
+    return pl.pallas_call(
+        collect_kernel,
         grid_spec=pltpu.PrefetchScalarGridSpec(
             num_scalar_prefetch=1,
-            grid=(count,),
-            in_specs=[part(0, skip[0]), part(half, skip[1])],
-            out_specs=pl.BlockSpec(block, lambda i, places: (places[i // half] * half + i % half, 0, 0)),
+            grid=(len(pieces) * group,),
+            in_specs=[part(i) for i in range(len(pieces))],
+            out_specs=pl.BlockSpec(
+                block, lambda step, places: (places[step // group] * group + step % group, 0, 0)),
         ),
-        out_shape=jax.ShapeDtypeStruct((count,) + block[1:], F32),
+        out_shape=jax.ShapeDtypeStruct((len(pieces) * group, rows, columns), F32),
         compiler_params=params(),
         cost_estimate=cost(5),
-    )(places, first, second)
+    )(places, *pieces)
 
 
 def norm_back(grad, values, scale, gain):
@@ -764,118 +1013,76 @@
     def joined(*pieces):
         return place(pieces, lane).reshape(block, width)
 
-    def start(*_):
-        small = jnp.concatenate(
-            [router_weight, attn_gain[:, None], ffn_gain[:, None],
-             jnp.zeros((share, 128 - experts - 2), BF16)], axis=1)
-        attn_mine = jnp.concatenate(
-            [key_weight, value_weight, query_weight, out_weight.T, small], axis=1)
-        return attn_mine, lax.dynamic_slice_in_dim(tokens, lane * tok, tok, 0)
-
-    attn_mine, tokens_mine = phases.run(start)
-
-    def cot_rows(cotangent, plane):
-        chosen = routes.T
-        hits = jnp.zeros((experts, block), jnp.bool_)
-        for j in range(top_count):
-            hits = hits | (chosen[j : j + 1] == jnp.arange(experts, dtype=jnp.int32)[:, None])
-        spot = jnp.arange(block, dtype=jnp.int32)
-        before = (spot[:, None] < spot[None, :]).astype(BF16)
-        rank = dot(hits.astype(BF16), before)
-        table = jnp.pad(jnp.where(hits, rank, -1.0).astype(BF16), ((0, 16 - experts), (0, width - block)))
-        pieces = [
-            lax.dynamic_slice_in_dim(cotangent, (lane - j) % tp * tok, tok, 0) for j in range(tp)]
-        return [jnp.concatenate([pieces[0], table], axis=0)] + pieces[1:], hits
-
-    def of_plane(stack, index):
-        return lax.dynamic_slice_in_dim(stack, owned * index, owned, 0)
-
-    def experts_of(index, expert_gate, expert_up, expert_down):
-        return [
-            of_plane(expert_gate, index),
-            of_plane(expert_up, index),
-            jnp.swapaxes(of_plane(expert_down, index), 1, 2),
-        ]
-
-    at = plane * units
     other_plane = plane ^ 2
 
-    def weight_rows(expert_gate, expert_up, expert_down):
-        shared_mine = jnp.concatenate(
-            [
-                lax.dynamic_slice_in_dim(shared_gate, at, units, 1),
-                lax.dynamic_slice_in_dim(shared_up, at, units, 1),
-                lax.dynamic_slice_in_dim(shared_down, at, units, 0).T,
-                jnp.zeros((share, hidden_units - 3 * units), BF16),
-            ],
-            axis=1,
-        )
-        return jnp.concatenate(experts_of(plane, expert_gate, expert_up, expert_down) + [shared_mine[None]], axis=0)
-
-    def tables(plane):
-        positions = (plane - 2) * block + jnp.arange(3 * block, dtype=jnp.int32)
-        index = jnp.arange(2 * HD, dtype=jnp.int32)
-        rates = 10000.0 ** (-2.0 * (index % (HD // 2)).astype(F32) / HD)
-        angles = positions.astype(F32)[:, None] * rates[None, :]
-        sign = jnp.where(index % HD < HD // 2, -1.0, 1.0)
-        segment_pad = jnp.concatenate([jnp.full((2 * block,), -1, jnp.int32), segments[0]])
-        kseg = lax.dynamic_slice_in_dim(segment_pad, plane * block, 3 * block, 0)
-        return jnp.cos(angles), sign * jnp.sin(angles), kseg[:, None], kseg[2 * block :][None, :]
-
-    def phase_first(attn_mine, tokens_mine, plane, cotangent, expert_gate, expert_up, expert_down):
+    gains = jnp.concatenate([attn_gain[None], ffn_gain[None]], axis=0)
+    qkv_mine, small_mine, tokens_mine = pack(
+        lane, tp, key_weight, value_weight, query_weight, router_weight.T, gains, tokens)
+    small_core = core_swap(small_mine)
+    qkv_mine, small_mine, tokens_mine, small_core = phases.run(
+        lambda *given: given, qkv_mine, small_mine, tokens_mine, small_core)
+
+    prepare_meta = jnp.stack([lane, plane]).astype(jnp.int32)
+
+    def send_first(qkv, small, small_core, tokens_mine, cotangent):
         return (
-            to_pairs(attn_mine), core_swap(attn_mine), ctx_open(tokens_mine, 1), tables(plane),
-            cot_rows(cotangent, plane), weight_rows(expert_gate, expert_up, expert_down))
-
-    attn_far, attn_core, prev_one_mine, attn_tables, (cot_own, hits), weights_mine = phases.run(
-        phase_first, attn_mine, tokens_mine, plane, cotangent, expert_gate, expert_up, expert_down)
-    cosine, sine, kseg, qseg = attn_tables
+            to_pairs(qkv), core_swap(qkv), to_pairs(jnp.concatenate([small, small_core], axis=0)),
+            ctx_open(tokens_mine, 1),
+            prepare(prepare_meta, tp, experts, routes.T, cotangent, segments))
+
+    qkv_far, qkv_core, small_far, prev_one_mine, prepared = phases.run(
+        send_first, qkv_mine, small_mine, small_core, tokens_mine, cotangent)
+    cosine, sine, kseg, qseg, hits = prepared[:5]
+    cot_own = prepared[5:]
+    gathered = small_mine, small_core, small_far
+
+    def all_small(small_mine, small_core, small_far):
+        rows = place([jnp.concatenate([small_mine, small_core], axis=0)] + small_far, pair)
+        rows = rows.reshape(pairs, 2, 16, share)
+        rows = jnp.where(core == 0, rows, rows[:, ::-1])
+        return rows.reshape(fsdp, 16, share).transpose(1, 0, 2).reshape(16, width)
+
+    def send_second(qkv_far, prev_one_mine, out_weight, gathered, *stacks):
+        return (
+            [core_swap(one) for one in qkv_far], to_tp(prev_one_mine), ctx_open(prev_one_mine, 1),
+            to_pairs(out_weight.T), all_small(*gathered), bundle(plane, owned, units, stacks[:3], stacks[3:]))
+
+    qkv_far_core, prev_one_other, prev_two_mine, out_far, small_all, weights_mine = phases.run(
+        send_second, qkv_far, prev_one_mine, out_weight, gathered, expert_gate, expert_up,
+        jnp.swapaxes(expert_down, 1, 2), shared_gate, shared_up, shared_down.T)
     weights = lax.all_gather(weights_mine, "fsdp", axis=0)
-    cot_mine = [cot_own[0]]
-    attn_far_core, prev_one_other, prev_two_mine, got = phases.run(
-        lambda attn_far, prev_one_mine, cot: (
-            [core_swap(one) for one in attn_far], to_tp(prev_one_mine), ctx_open(prev_one_mine, 1),
-            ctx_shift(cot, -1)),
-        attn_far, prev_one_mine, cot_mine[-1])
-    cot_mine.append(got)
-
-    def all_rows(mine, far, across, far_across, columns):
-        same = place([mine[:, columns]] + [one[:, columns] for one in far], pair)
-        other = place([across[:, columns]] + [one[:, columns] for one in far_across], pair)
-        return place_rows([same, other], core).reshape(width, same.shape[2])
-
-    def project_near(tokens, prev_one_mine, prev_one_other, prev_two_mine, cot, *attn):
-        sent = to_tp(prev_two_mine), ctx_shift(cot, -1)
-        qkv_full = all_rows(*attn, slice(0, 3 * cols))
-        small_t = all_rows(*attn, slice(4 * cols, 4 * cols + 128))[:, :16].T
-        attn_scale = small_t[experts : experts + 1].astype(F32)
-        prev_one = joined(prev_one_mine, *prev_one_other)
-        first = project([prev_one, tokens], attn_scale, qkv_full, cosine, sine, cols, 3, 1, [])
-        return qkv_full, small_t, attn_scale, prev_one, first, sent
-
-    qkv_full, small_t, attn_scale, prev_one, first, (prev_two_other, got) = phases.run(
-        project_near, tokens, prev_one_mine, prev_one_other, prev_two_mine, cot_mine[-1],
-        attn_mine, attn_far, attn_core, attn_far_core)
-    cot_mine.append(got)
-    query = first[3]
+    attn_scale = small_all[experts : experts + 1].astype(F32)
+    ffn_scale = small_all[experts + 1 : experts + 2].astype(F32)
+    router_t = jnp.concatenate([small_all[:experts], jnp.zeros((16 - experts, width), BF16)], axis=0)
+    router_full = small_all[:experts].T
+    here = [(plane + d) % ctx for d in range(ctx)]
     half = ctx // 2
-    here = [(plane + d) % ctx for d in range(ctx)]
-
-    def attention(prev_two_mine, prev_two_other, cots, *attn):
-        cot_sent = ctx_shift(cots[-1], -1), to_tp(cots[1]), to_tp(cots[2])
-        prev_two = joined(prev_two_mine, *prev_two_other)
-        hid, keys, values = project(
-            [prev_two], attn_scale, qkv_full, cosine, sine, cols, 3, 0, first[:3])
+    place_meta = jnp.stack([lane, pair, core]).astype(jnp.int32)
+
+    def near_projection(prev_one_mine, prev_one_other, prev_two_mine, cot, out_weight, out_far, same, cross, scale):
+        sent = (
+            to_tp(prev_two_mine), ctx_shift(cot, -1), [core_swap(one) for one in [out_weight.T] + out_far])
+        return sent, project_near(
+            place_meta, tokens, [prev_one_mine] + prev_one_other, same, cross, scale, cosine, sine)
+
+    (prev_two_other, cot_one, out_cross), first = phases.run(
+        near_projection, prev_one_mine, prev_one_other, prev_two_mine, cot_own[0], out_weight, out_far,
+        [qkv_mine] + qkv_far, [qkv_core] + qkv_far_core, attn_scale)
+    query, qkv_full, prev_one = first[3:]
+
+    def attention(prev_two_mine, prev_two_other, cot, cot_one, out_weight, out_far, out_cross):
+        sent = ctx_shift(cot, -2), to_tp(cot_one)
+        hid, keys, values, prev_two = project_far(
+            place_meta, [prev_two_mine] + prev_two_other, qkv_full, attn_scale, cosine, sine, first[:3])
         attended, lse = attend(query, keys, values, kseg, qseg)
-        out_full = all_rows(*attn, slice(3 * cols, 4 * cols))
-        router_full = all_rows(*attn, slice(4 * cols, 4 * cols + 128))[:, :experts]
+        same = place([out_weight.T] + out_far, pair)
+        cross = place(out_cross, pair)
+        out_full = place_rows([same, cross], core).reshape(width, cols)
         partial = dot_nt(attended, out_full).astype(BF16).reshape(tp, tok, width)
-        return cot_sent, prev_two, hid, keys, values, attended, lse, out_full, router_full, partial
-
-    cot_sent, prev_two, hid, keys, values, attended, lse, out_full, router_full, partial = phases.run(
-        attention, prev_two_mine, prev_two_other, cot_mine, attn_mine, attn_far, attn_core, attn_far_core)
-    cot_mine.append(cot_sent[0])
-    cot_other = [cot_own[1:], cot_sent[1], cot_sent[2]]
+        return sent, hid, keys, values, prev_two, attended, lse, out_full, partial
+
+    (cot_two, cot_one_other), hid, keys, values, prev_two, attended, lse, out_full, partial = phases.run(
+        attention, prev_two_mine, prev_two_other, cot_own[0], cot_one, out_weight, out_far, out_cross)
 
     def sent_tp(total):
         return [tp_shift(pick(total, (lane + j) % tp), j) for j in range(1, tp)]
@@ -886,9 +1093,13 @@
             result = result + one.astype(F32)
         return result
 
-    partial_other = phases.run(sent_tp, partial)
-    router_t = jnp.concatenate([small_t[:experts], jnp.zeros((16 - experts, width), BF16)], axis=0)
-    ffn_scale = small_t[experts + 1 : experts + 2].astype(F32)
+    def after_attention(partial, cot, gate, up, down):
+        return (
+            sent_tp(partial), ctx_shift(cot, -3),
+            bundle(other_plane, owned, units, [gate, up, down], []))
+
+    partial_other, cot_three, again_mine = phases.run(
+        after_attention, partial, cot_own[0], expert_gate, expert_up, jnp.swapaxes(expert_down, 1, 2))
     inputs_mine = tokens_mine.astype(F32)
 
     def normalize(partial, got):
@@ -904,66 +1115,61 @@
         other.append(got)
         mine.append(moved)
 
-    near, far = list(range(0, ctx, 2)), list(range(1, ctx, 2))
+    near, far = list(range(half)), list(range(half, ctx))
+    cot_mine = [cot_own[0], cot_one, cot_two, cot_three]
 
     def meta_of(blocks):
         return jnp.stack([owned * plane] + [here[d] for d in blocks] + [lane]).astype(jnp.int32)
 
-    def pieces_of(mine, other, blocks):
-        return [[mine[d]] + list(other[d]) for d in blocks]
-
-    def near_blocks(last, last_cot, weights, mine, cot_mine, expert_gate, expert_up, expert_down):
-        later = to_tp(last), to_tp(last_cot)
+    def pieces_of(mine, other):
+        return [[one] + list(two) for one, two in zip(mine, other)]
+
+    def near_blocks(last, cot_late, weights, x_mine, x_other, cot_mine, cot_other, again_mine):
+        later = to_tp(last), [to_tp(one) for one in cot_late]
         got = expert_blocks(
-            0, ctx, capacity, experts, units, meta_of(near), pieces_of(mine, other, near),
-            pieces_of(cot_mine, cot_other, near), weights, router_t, [])
-        again_mine = jnp.concatenate(experts_of(other_plane, expert_gate, expert_up, expert_down), axis=0)
+            0, ctx, capacity, experts, units, meta_of(near), pieces_of(x_mine, x_other),
+            pieces_of(cot_mine, cot_other), weights, router_t, [])
         return later, got, again_mine
 
     later, got, again_mine = phases.run(
-        near_blocks, mine[-1], cot_mine[-1], weights, mine[:-1], cot_mine[:-1], expert_gate, expert_up, expert_down)
+        near_blocks, mine[-1], cot_mine[half:], weights, mine[:half], other[:half], cot_mine[:half],
+        [cot_own[1:], cot_one_other], again_mine)
     other_weights = lax.all_gather(again_mine, "fsdp", axis=0)
     other.append(later[0])
-    cot_other.append(later[1])
     near_dx = [got[0][i] for i in range(half)]
 
-    def far_blocks(dx, mine, other, cot_mine, cot_other, saved):
+    def far_blocks(dx, x_mine, x_other, cot_mine, cot_other, saved):
         sent = [sent_tp(one) for one in dx]
         got = expert_blocks(
-            half, ctx, capacity, experts, units, meta_of(far), pieces_of(mine, other, far),
-            pieces_of(cot_mine, cot_other, far), weights, router_t, saved)
+            half, ctx, capacity, experts, units, meta_of(far), pieces_of(x_mine, x_other),
+            pieces_of(cot_mine, cot_other), weights, router_t, saved)
         return sent, got
 
-    near_sent, got = phases.run(far_blocks, near_dx, mine, other, cot_mine, cot_other, got[1:])
+    near_sent, got = phases.run(
+        far_blocks, near_dx, mine[half:], other[half:], cot_mine[half:], later[1], got[1:])
     far_dx = [got[0][i] for i in range(half)]
     sx, sr, sh, sa, sb, ssx, ssc, ssh, ssa, ssb, out_parts = got[1:]
 
-    def sent_pairs(kept, got):
-        return [
-            pair_shift(
-                (pick(kept, (pair + j) % pairs).astype(F32) + pick(got, (pair + j) % pairs).astype(F32)
-                 ).astype(BF16), j)
-            for j in range(1, pairs)
-        ]
+    def for_pairs(kept, got):
+        return [pair_sum((pair + j) % pairs, kept, got, []) for j in range(1, pairs)]
+
+    def sent_pairs(rows):
+        return [pair_shift(one, j + 1) for j, one in enumerate(rows)]
 
     def add_pairs(kept, got, far):
-        result = pick(kept, pair).astype(F32) + pick(got, pair).astype(F32)
-        for one in far:
-            result = result + one.astype(F32)
-        return result.astype(BF16)
+        return pair_sum(pair, kept, got, far)
 
     def weight_step(left, right):
         return weight_grads(core_index, left, right, pairs)
 
-    def again(d, ssx, saved):
+    def again(ssx):
         meta = jnp.stack([owned * other_plane, plane]).astype(jnp.int32)
-        return expert_again(
-            d, capacity, tp, experts, meta, ssx, ssc, other_weights, router_t, saved)
+        return expert_again(0, ctx, capacity, tp, experts, meta, ssx, ssc, other_weights, router_t, [])
 
     def back_through_norm(dx_sum):
         grad_normed = dx_sum[:tok]
         grad_gates = dx_sum[tok : tok + experts, :tok].T
-        named = lax.dynamic_slice_in_dim(hits, lane * tok, tok, 1).T
+        named = lax.dynamic_slice_in_dim(hits, lane * tok, tok, 1).T > 0.0
         logits = jnp.where(named, dot(normed_low, router_full), -1e30)
         expo = jnp.where(named, jnp.exp(logits - jnp.max(logits, axis=-1, keepdims=True)), 0.0)
         gates = expo / jnp.sum(expo, axis=-1, keepdims=True)
@@ -982,97 +1188,132 @@
             for j in range(1, tp)
         ]
 
-    def phase_one(near_dx, near_sent, far_dx, sr, sx):
-        sent = [sent_tp(one) for one in far_dx]
+    def phase_one(near_dx, near_sent, far_dx, sr, ssx):
+        sent = sent_tp(far_dx[0])
         sums = [sum_tp(one, got) for one, got in zip(near_dx, near_sent)]
         home = [sums[0]] + [ctx_shift(one.astype(BF16), d) for d, one in zip(near[1:], sums[1:])]
-        return sent, home, weight_step(sr, sh), weight_step(sx, sa)
-
-    far_sent, home, down, gate = phases.run(phase_one, near_dx, near_sent, far_dx, sr, sx)
-
-    def phase_two(far_dx, far_sent, down_sent, gate_sent, sx, ssx, out_parts):
-        sums = [sum_tp(one, got) for one, got in zip(far_dx, far_sent)]
-        more = [ctx_shift(one.astype(BF16), d) for d, one in zip(far, sums)]
-        return (
-            more, core_swap(down_sent), core_swap(gate_sent), out_sent(out_parts, 0),
-            weight_step(sx, sb), again(0, ssx, []))
-
-    more, down_got, gate_got, out_zero, up, other_saved = phases.run(
-        phase_two, far_dx, far_sent, down[0], gate[0], sx, ssx, out_parts)
-
-    def phase_three(home, down_kept, down_got, up_sent, ssx, saved, out_parts):
-        sent = sent_pairs(down_kept, down_got), core_swap(up_sent), out_sent(out_parts, 1), out_sent(out_parts, 2)
+        return sent, home, weight_step(sr, sh), shared_grads(core_index, ssx, ssc, ssa, ssb, ssh, pairs)
+
+    first_sent, home, down, shared = phases.run(phase_one, near_dx, near_sent, far_dx, sr, ssx)
+
+    def phase_one_more(far_dx, first_sent, down_sent, shared_sent, sx, out_parts):
+        sent = core_swap(down_sent), core_swap(shared_sent), sent_tp(far_dx[1]), out_sent(out_parts, 0)
+        more = ctx_shift(sum_tp(far_dx[0], first_sent).astype(BF16), far[0])
+        return sent, more, weight_step(sx, sa), weight_step(sx, sb)
+
+    (down_got, shared_got, second_sent, out_zero), more, gate, up = phases.run(
+        phase_one_more, far_dx, first_sent, down[0], shared[0], sx, out_parts)
+    home.append(more)
+
+    def phase_two(far_dx, second_sent, down, shared, gate_sent, ssx, out_parts):
+        sent = (
+            sent_pairs(for_pairs(*down)), sent_pairs(for_pairs(*shared)), core_swap(gate_sent),
+            [tp_shift(
+                lax.dynamic_index_in_dim(out_parts, (lane + j) % tp, 1, keepdims=False)[1:], j)
+             for j in range(1, tp)])
+        more = ctx_shift(sum_tp(far_dx[1], second_sent).astype(BF16), far[1])
+        return sent, more, again(ssx)
+
+    (down_far, shared_far, gate_got, out_rest), more, other_saved = phases.run(
+        phase_two, far_dx, second_sent, (down[1], down_got), (shared[1], shared_got), gate[0], ssx, out_parts)
+    home.append(more)
+    out_far = out_zero, out_rest
+    ox, orr, oh, oa, ob = other_saved
+
+    def out_sums(out_parts, out_far):
+        total = lax.dynamic_index_in_dim(out_parts, lane, 1, keepdims=False).astype(F32)
+        for one, rest in zip(*out_far):
+            total = total + jnp.concatenate([one[None], rest], axis=0).astype(F32)
+        return total.astype(BF16)
+
+    out_total = phases.run(out_sums, out_parts, out_far)
+    out_sum = lax.psum_scatter(out_total, "ctx", scatter_dimension=0, tiled=False)
+
+    def phase_three(gate, up_sent, down, shared, home, orr, ox):
+        sent = sent_pairs(for_pairs(*gate)), core_swap(up_sent)
         back = back_through_norm(sum(one.astype(F32) for one in home))
-        return sent, back, again(1, ssx, saved)
-
-    (down_far, up_got, out_one, out_two), back, other_saved = phases.run(
-        phase_three, home + more, down[1], down_got, up[0], ssx, other_saved, out_parts)
+        return sent, back, add_pairs(*down), add_pairs(*shared), weight_step(orr, oh), weight_step(ox, oa)
+
+    (gate_far, up_got), back, own_down, own_shared, other_down, other_gate = phases.run(
+        phase_three, (gate[1], gate_got), up[0], (down[1], down_got, down_far), (shared[1], shared_got, shared_far),
+        home, orr, ox)
     grad_mixed_low, grad_mixed, grad_ffn_gain, grad_router = back
-
-    def phase_four(gate_kept, gate_got, grad_mixed_low, ssx, saved, out_parts):
-        sent = sent_pairs(gate_kept, gate_got), to_tp(grad_mixed_low), out_sent(out_parts, 3)
-        return sent, again(3, ssx, again(2, ssx, saved))
-
-    (gate_far, grad_mixed_other, out_three), other_saved = phases.run(
-        phase_four, gate[1], gate_got, grad_mixed_low, ssx, other_saved, out_parts)
-    ox, orr, oh, oa, ob = other_saved
-
-    def phase_five(up_kept, up_got, down, grad_mixed_low, grad_mixed_other, out_parts, out_far):
-        sent = sent_pairs(up_kept, up_got)
+    all_shared = lax.all_gather(own_shared, "ctx", axis=0)
+
+    def phase_four(up, grad_mixed_low, own_down, down_sent, gate, ox, out_sum):
+        sent = sent_pairs(for_pairs(*up)), to_tp(grad_mixed_low), ctx_swap(own_down), core_swap(down_sent)
+        return sent, weight_step(ox, ob), add_pairs(*gate), out_sum
+
+    (up_far, grad_mixed_other, far_down, down_got), other_up, own_gate, out_sum = phases.run(
+        phase_four, (up[1], up_got), grad_mixed_low, own_down, other_down[0], (gate[1], gate_got, gate_far), ox,
+        out_sum)
+
+    def phase_five(down, gate_sent, up_sent, own_gate, up, grad_mixed_low, grad_mixed_other):
+        sent = sent_pairs(for_pairs(*down)), core_swap(gate_sent), core_swap(up_sent), ctx_swap(own_gate)
         rows = joined(grad_mixed_low, *grad_mixed_other)
         grad_attended = dot(rows, out_full).astype(BF16)
         grads = attend_back(query, keys, values, grad_attended, lse, kseg, qseg, cosine, sine)
-        total = lax.dynamic_index_in_dim(out_parts, lane, 1, keepdims=False).astype(F32)
-        for j in range(tp - 1):
-            total = total + jnp.stack([one[j] for one in out_far]).astype(F32)
-        return sent, rows, grads, add_pairs(*down), total.astype(BF16)
-
-    up_far, grad_mixed_rows, (dq, dk, dv), own_down, out_total = phases.run(
-        phase_five, up[1], up_got, (down[1], down_got, down_far), grad_mixed_low, grad_mixed_other, out_parts,
-        [out_zero, out_one, out_two, out_three])
-    out_sum = lax.psum_scatter(out_total, "ctx", scatter_dimension=0, tiled=False)
-
-    def phase_six(gate, up, dq, dk, dv, orr, ssx):
+        return sent, rows, grads, add_pairs(*up)
+
+    (down_far, gate_got, up_got, far_gate), grad_mixed_rows, (dq, dk, dv), own_up = phases.run(
+        phase_five, (other_down[1], down_got), other_gate[0], other_up[0], own_gate,
+        (up[1], up_got, up_far), grad_mixed_low, grad_mixed_other)
+
+    def phase_six(gate, own_up, dq, dk, dv, hid, down, all_shared):
+        sent = sent_pairs(for_pairs(*gate)), ctx_swap(own_up)
         back, gain_row = hidden_back([prev_two, prev_one, tokens], dk, dv, dq, qkv_full)
-        return back, gain_row, add_pairs(*gate), add_pairs(*up), weight_step(orr, oh), shared_grads(
-            core_index, ssx, ssc, ssa, ssb, ssh, pairs)
-
-    back, gain_row, own_gate, own_up, other_down, shared = phases.run(
-        phase_six, (gate[1], gate_got, gate_far), (up[1], up_got, up_far), dq, dk, dv, orr, ssx)
-    groups = [[2 * i, 2 * i + 1] for i in range(ctx // 2)]
-    own_all = lax.all_gather(
-        jnp.concatenate([own_down, own_gate, own_up], axis=0), "ctx", axis=0, axis_index_groups=groups)
+        attn = attn_grads_of(core_index, hid, dk, dv, dq, grad_mixed_rows, attended, pairs)
+        return sent, back, gain_row, attn, add_pairs(*down), all_shared
+
+    (gate_far, far_up), back, gain_row, attn, own_other_down, all_shared = phases.run(
+        phase_six, (other_gate[1], gate_got), own_up, dq, dk, dv, hid, (other_down[1], down_got, down_far),
+        all_shared)
     small_rows = jnp.concatenate(
         [grad_router, grad_ffn_gain[None], gain_row, jnp.zeros((16 - experts - 2, width), F32)], axis=0)
     hidden_parts = [back[j].reshape(tp, tok, width) for j in range(3)]
 
-    def phase_seven(hidden_parts, small_rows, down_sent, shared_sent, ox):
-        sent = [sent_tp(hidden_parts[0]), sent_tp(hidden_parts[1]), all_sum(small_rows, "tp")]
-        return sent, core_swap(down_sent), core_swap(shared_sent), weight_step(ox, oa), weight_step(ox, ob)
-
-    hidden_sent, down_got, shared_got, other_gate, other_up = phases.run(
-        phase_seven, hidden_parts, small_rows, other_down[0], shared[0], ox)
-    small_rows = jnp.pad(hidden_sent[2], ((0, 112), (0, 0)))
-
-    def phase_eight(hidden_parts, got, hid, down, gate_sent, up_sent):
-        far_two = sum_tp(hidden_parts[0], got[0]).astype(BF16)
-        sent = [
-            sent_pairs(*down), ctx_open(far_two, -1), sent_tp(hidden_parts[2]), core_swap(gate_sent), core_swap(up_sent)]
-        attn = attn_grads_of(
-            core_index, hid, dk, dv, dq, grad_mixed_rows, attended, small_rows, pairs)
-        return sent, attn
-
-    (down_far, carried, hidden_mine_sent, gate_got, up_got), attn = phases.run(
-        phase_eight, hidden_parts, hidden_sent, hid, (other_down[1], down_got), other_gate[0], other_up[0])
-
-    def phase_nine(hidden_parts, got, carried, attn_sent, gate, down, shared):
-        sent = sent_pairs(*gate)
-        far_one = (sum_tp(hidden_parts[1], got[1]) + carried.astype(F32)).astype(BF16)
-        return sent, ctx_open(far_one, -1), core_swap(attn_sent), add_pairs(*down), sent_pairs(*shared)
-
-    gate_far, carried, attn_got, other_down, shared_far = phases.run(
-        phase_nine, hidden_parts, hidden_sent, carried, attn[0], (other_gate[1], gate_got),
-        (other_down[1], down_got, down_far), (shared[1], shared_got))
+    def phase_seven(up, attn_sent, own_other_down, hidden_parts, small_rows, gate):
+        sent = (
+            sent_pairs(for_pairs(*up)), core_swap(attn_sent), ctx_swap(own_other_down), sent_tp(hidden_parts[0]),
+            all_sum(small_rows, "tp"))
+        return sent, add_pairs(*gate)
+
+    (up_far, attn_got, far_other_down, far_two, small_rows), own_other_gate = phases.run(
+        phase_seven, (other_up[1], up_got), attn[0], own_other_down, hidden_parts, small_rows,
+        (other_gate[1], gate_got, gate_far))
+
+    def shared_out(all_shared):
+        result = all_shared.astype(F32)
+        return result.reshape(ctx, share, 3, units).transpose(2, 1, 0, 3).reshape(3, share, ctx * units)
+
+    def phase_eight(attn, own_other_gate, hidden_parts, far_two, small_rows, up, all_shared):
+        carried = ctx_open(sum_tp(hidden_parts[0], far_two).astype(BF16), -1)
+        sent = (
+            carried, sent_pairs(for_pairs(*attn)), ctx_swap(own_other_gate), core_swap(small_rows),
+            sent_tp(hidden_parts[1]))
+        return sent, add_pairs(*up), shared_out(all_shared)
+
+    (carried, attn_far, far_other_gate, small_got, far_one), own_other_up, result = phases.run(
+        phase_eight, (attn[1], attn_got), own_other_gate, hidden_parts, far_two, small_rows,
+        (other_up[1], up_got, up_far), all_shared)
+    places = jnp.stack([plane, plane ^ 1, plane ^ 2, plane ^ 3]).astype(jnp.int32)
+
+    def phase_nine(hidden_parts, far_one, carried, own_other_up, attn, small_rows, small_got, out_sum, own_down):
+        carried = ctx_open(
+            (sum_tp(hidden_parts[1], far_one) + carried.astype(F32)).astype(BF16), -1)
+        output_mine = (mixed + out_sum.astype(F32)).astype(BF16)
+        sent = carried, sent_tp(hidden_parts[2]), ctx_swap(own_other_up), to_tp(output_mine)
+        small_rows = small_rows + small_got
+        reach = 1
+        while reach < pairs:
+            small_rows = small_rows + pair_swap(small_rows, reach)
+            reach *= 2
+        return sent, small_rows, add_pairs(*attn), output_mine, collect(
+            places, [own_down, far_down, own_other_down, far_other_down])
+
+    (carried, hidden_other, far_other_up, output_other), small_rows, attn_rows, output_mine, grad_expert_down = phases.run(
+        phase_nine, hidden_parts, far_one, carried, own_other_up, (attn[1], attn_got, attn_far), small_rows,
+        small_got, out_sum, own_down)
 
     def input_back(total, got, carried):
         grad_hidden = sum_tp(total, got) + carried.astype(F32)
@@ -1082,50 +1323,35 @@
             scaled * inputs_mine, axis=-1, keepdims=True)
         return (grad_mixed + grad_norm).astype(BF16)
 
-    def phase_ten(hidden_parts, got, carried, attn, up, gate, shared, other_down):
+    def phase_ten(attn_rows, hidden_parts, hidden_other, carried, small_rows, own_gate, output_mine, output_other):
+        input_mine = input_back(hidden_parts[2], hidden_other, carried)
+        small = lax.dynamic_slice_in_dim(small_rows, me * share, share, 1).astype(BF16)
+        small = jnp.pad(small, ((0, 16), (0, 4 * cols - share)))
+        pieces = jnp.concatenate([attn_rows, small], axis=0).reshape(ctx, (share + 32) // ctx, 4 * cols)
         return (
-            input_back(hidden_parts[2], got, carried), sent_pairs(*attn), sent_pairs(*up), add_pairs(*gate),
-            add_pairs(*shared), ctx_swap(other_down))
-
-    input_mine, attn_far, up_far, other_gate, own_shared, far_other_down = phases.run(
-        phase_ten, hidden_parts, hidden_mine_sent, carried, (attn[1], attn_got), (other_up[1], up_got),
-        (other_gate[1], gate_got, gate_far), (shared[1], shared_got, shared_far), other_down)
-    all_shared = lax.all_gather(own_shared, "ctx", axis=0)
-    odd = plane % 2
-
-    def paired(one, got):
-        return jnp.where(odd == 0, jnp.stack([one, got]), jnp.stack([got, one]))
-
-    places = jnp.stack([plane // 2, 1 - plane // 2]).astype(jnp.int32)
-
-    def phase_eleven(input_mine, attn, up, other_gate, other_down, far_other_down, own_all, out_sum):
-        output_mine = (mixed + out_sum.astype(F32)).astype(BF16)
+            to_tp(input_mine), [ctx_shift(pick(pieces, (plane + d) % ctx), d) for d in range(1, ctx)],
+            pick(pieces, plane), input_mine, joined(output_mine, *output_other),
+            collect(places, [own_gate, far_gate, own_other_gate, far_other_gate]))
+
+    input_other, attn_got, attn_piece, input_mine, output, grad_expert_gate = phases.run(
+        phase_ten, attn_rows, hidden_parts, hidden_other, carried, small_rows, own_gate, output_mine, output_other)
+
+    def phase_eleven(attn_piece, attn_got, own_up, input_mine, input_other):
+        total = attn_piece.astype(F32)
+        for one in attn_got:
+            total = total + one.astype(F32)
+        total = total.astype(BF16)
         return (
-            to_tp(input_mine), add_pairs(*attn), add_pairs(*up), ctx_swap(other_gate),
-            collect(places, own_all, paired(other_down, far_other_down), (0, 0), owned, True), output_mine)
-
-    input_other, attn_rows, other_up, far_other_gate, grad_expert_down, output_mine = phases.run(
-        phase_eleven, input_mine, (attn[1], attn_got, attn_far), (other_up[1], up_got, up_far), other_gate,
-        other_down, far_other_down, own_all, out_sum)
-    attn_rows = lax.psum(attn_rows, "ctx")
-
-    def phase_twelve(other_up, other_gate, far_other_gate, input_mine, input_other, output_mine):
-        return (
-            ctx_swap(other_up), to_tp(output_mine), joined(input_mine, *input_other),
-            collect(places, own_all, paired(other_gate, far_other_gate), (owned, 0), owned, False))
-
-    far_other_up, output_other, input_grad, grad_expert_gate = phases.run(
-        phase_twelve, other_up, other_gate, far_other_gate, input_mine, input_other, output_mine)
-    grad_expert_up = collect(places, own_all, paired(other_up, far_other_up), (2 * owned, 0), owned, False)
-    output = joined(output_mine, *output_other)
-    attn_rows = attn_rows.astype(F32)
-    grad_key_weight = attn_rows[:, :cols]
-    grad_value_weight = attn_rows[:, cols : 2 * cols]
-    grad_query_weight = attn_rows[:, 2 * cols : 3 * cols]
-    grad_out_rows = attn_rows[:, 3 * cols : 4 * cols].T
-    small_out = attn_rows[:, 4 * cols :]
-    result = all_shared.astype(F32)
-    result = result.reshape(ctx, share, 3, units).transpose(2, 1, 0, 3).reshape(3, share, ctx * units)
+            total, [ctx_shift(total, d) for d in range(1, ctx)],
+            collect(places, [own_up, far_up, own_other_up, far_other_up]), joined(input_mine, *input_other))
+
+    attn_piece, attn_got, grad_expert_up, input_grad = phases.run(
+        phase_eleven, attn_piece, attn_got, own_up, input_mine, input_other)
+    grad_key_weight, grad_value_weight, grad_query_weight, grad_out_rows, small_out = finish(
+        plane.astype(jnp.int32)[None], [attn_piece] + attn_got, share, cols)
+    grad_out_rows = grad_out_rows.T
+    grad_expert_down = jnp.swapaxes(grad_expert_down, 1, 2)
+    small_out = small_out[:, :share]
     grad_shared_gate, grad_shared_up, grad_shared_down = result[0], result[1], result[2].T
     return (
         output[None],
@@ -1134,9 +1360,9 @@
         grad_key_weight,
         grad_value_weight,
         grad_out_rows,
-        small_out[:, experts + 1],
-        small_out[:, experts],
-        small_out[:, :experts],
+        small_out[experts + 1],
+        small_out[experts],
+        small_out[:experts].T,
         grad_shared_gate,
         grad_shared_up,
         grad_shared_down,

time: 618 us -> 545 us (0.88)
  other arithmetic: 87.7 us -> 29.3 us
  local copies, waits for them, and re-layouts: 74.2 us -> 35.9 us
  Pallas kernels: 221 us -> 252 us
  waiting for transfers between devices: 138 us -> 115 us
  starting transfers between devices: 66 us -> 80.8 us
    pallas_call x5 -> x26, Pallas kernels: 34.6 us -> 90.5 us  [the longest x16 38.6 us: pair_sum(): pl.pallas_call(pair_sum_kernel, grid_spec=pltpu.PrefetchScalarGridSpec(nu...]
    convert_element_type x26 -> x8, other arithmetic: 42.2 us -> 6.43 us  [the longest x1 3.41 us: out_sums(): return total.astype(BF16)]
    psum x1 -> x0, waiting for transfers between devices: 26.1 us -> none  [local(): attn_rows = lax.psum(attn_rows, 'ctx')]
    ppermute x9 -> x11, waiting for transfers between devices: 42.8 us -> 19.9 us  [pair_shift(): return lax.ppermute(block, 'fsdp', route)]
    pallas_call x4 -> x1, Pallas kernels: 37.5 us -> 19.4 us  [expert_again(): pl.pallas_call(functools.partial(expert_kernel, capacity, parts, experts,...]
    another operation x16 -> x0, local copies, waits for them, and re-layouts: 14.4 us -> none  [place(): jnp.stack([first, second])]
    ppermute x3 -> x6, waiting for transfers between devices: 7.33 us -> 20.2 us  [ctx_swap(): return lax.ppermute(block, 'ctx', [(i, i ^ 1) for i in range(size)])]
    dynamic_slice x7 -> x0, local copies, waits for them, and re-layouts: 9.72 us -> none  [the longest x3 5 us: of_plane(): return lax.dynamic_slice_in_dim(stack, owned * index, owned, 0)]
  transfers between devices with their start and end apart: 66 -> 78, of which waited for: 19 -> 23; matrix products, arithmetic and copies ran while one was open for 21% -> 9% of each run, Pallas kernels for 35% -> 45%
where the time goes in v3:
time: 545 us; the launch traced here: 535 us
  Pallas kernels  252 us (46%)
  waiting for transfers between devices  115 us (21%)
  starting transfers between devices  80.8 us (15%)
  local copies, waits for them, and re-layouts  35.9 us (7%)
  other arithmetic  29.3 us (5%)
  between operations  15 us (3%)
  matrix products  7.05 us (1%)
    pallas_call x2, Pallas kernels, expert_blocks(): pl.pallas_call(functools.partial(expert_kernel, capacity, parts, experts,...  53.2 us
    pallas_call x16, Pallas kernels, pair_sum(): pl.pallas_call(pair_sum_kernel, grid_spec=pltpu.PrefetchScalarGridSpec(nu...  38.6 us
    pallas_call x6, Pallas kernels, weight_grads(): pl.pallas_call(weight_kernel, grid_spec=pltpu.PrefetchScalarGridSpec(num_...  34.9 us
    ppermute x22, starting transfers between devices, tp_shift(): lax.ppermute(block, 'tp', [(i, (i + distance) % size) for i in range(size)])  27.1 us
    ppermute x15, starting transfers between devices, ctx_shift(): lax.ppermute(block, 'ctx', [(i, (i + distance) % size) for i in range(siz...  24.9 us
    pallas_call x3, Pallas kernels, collect(): pl.pallas_call(collect_kernel, grid_spec=pltpu.PrefetchScalarGridSpec(num...  23.7 us
    ppermute x22, waiting for transfers between devices, tp_shift(): lax.ppermute(block, 'tp', [(i, (i + distance) % size) for i in range(size)])  22.7 us
    ppermute x4, waiting for transfers between devices, ctx_open(): return lax.ppermute(block, 'ctx', route)  21.6 us
  transfers between devices with their start and end apart: 78, of which 23 were waited for; matrix products, arithmetic and copies ran while one was open for 9% of the time, Pallas kernels for 45%

profile of v3, /device:TPU:0, one launch (start us, length us, event | category | flops | bytes accessed | tf_op | source)
XLA Modules:
  0.0 534.9 jit_solution(11120513053424596135)
XLA Ops:
  12.8 2.9 collective-permute-start.1
  15.7 3.5 collective-permute-start.2
  21.5 3.9 shard_map.281
  28.5 3.9 shard_map.282
  32.5 4.4 collective-permute-start.5
  39.8 5.1 collective-permute-done.7
  52.3 8.3 %shard_map.283 = (bf16[1536,768]{1,0:T(8,128)(2,1)}, bf16[1536,384]{1,0:T(8,128)(2,1)}, bf16[1536,384]{1,0:T(8,128)(2,1)}, bf16[512,384]{1,0:T(8,128)(2,1)}, bf1...) custom-call(s32[3]{0:T(128)} %pad_add_fusion.meta_ref, bf16[512,768]{1,0:T(8,128)(2,1)} %bitcast.172, ...), custom_call_target="tpu_custom_call" | custom-call | bytes 2380000 | tf_op jit(solution)/shard_map/pallas_call | solution.py:199
  62.2 4.5 shard_map.284
  66.7 13.4 %shard_map.285 = (bf16[512,384]{1,0:T(8,128)(2,1)}, f32[3,2,512]{2,1,0:T(2,128)}) custom-call(bf16[512,384]{1,0:T(8,128)(2,1)} %get-tuple-element.332.q_ref, bf16[1536,384]{1,0:T(8,128)(2,1)} %get-tuple-element.338.k_ref, bf16[1536,384]{1,0:T(8,128)(2,1)} %get-tuple-element.339.v_ref, s32[1536,1]{1,0:T(8,128)} %get-tuple-element.301.kseg_ref, ...), custom_call_target="tpu_custom_call" | custom-call | bytes 4420000 | tf_op jit(solution)/shard_map/pallas_call | solution.py:463
  85.9 3.2 shard_map.286
  89.1 5.4 %collective-permute-done.15 = bf16[256,768]{1,0:T(8,128)(2,1)S(1)} collective-permute-done((bf16[256,768]{1,0:T(8,128)(2,1)S(1)}, bf16[256,768]{1,0:T(8,128)(2,1)S(1)}, u32[]{:S(2)}, u32[]{:S(2)}) %collective-permute-start.15) | collective-permute-done | bytes 393248 | tf_op jit(solution)/shard_map/ppermute | solution.py:50
  100.8 6.1 %collective-permute-done.17.refs_2_ = bf16[256,768]{1,0:T(8,128)(2,1)S(1)} collective-permute-done((bf16[256,768]{1,0:T(8,128)(2,1)S(1)}, bf16[256,768]{1,0:T(8,128)(2,1)S(1)}, u32[]{:S(2)}, u32[]{:S(2)}) %collective-permute-start.17) | collective-permute-done | bytes 393248 | tf_op jit(solution)/shard_map/ppermute | solution.py:55
  111.9 4.7 collective-permute-done.19.refs_0_
  123.0 4.3 collective-permute-done.21.refs_2_
  127.3 3.7 collective-permute-done.22.refs_1_
  136.0 27.4 %shard_map.287 = (bf16[2,2,272,768]{3,2,1,0:T(8,128)(2,1)}, bf16[4,2,192,768]{3,2,1,0:T(8,128)(2,1)}, bf16[4,2,192,768]{3,2,1,0:T(8,128)(2,1)}, bf16[4,2,192,102...) custom-call(s32[4]{0:T(128)} %add_add_fusion.1.meta_ref, ...), custom_call_target="tpu_custom_call" | custom-call | bytes 8840000 | tf_op jit(solution)/shard_map/pallas_call | solution.py:709
  169.3 25.8 %shard_map.288 = (bf16[2,2,272,768]{3,2,1,0:T(8,128)(2,1)}, bf16[4,2,192,768]{3,2,1,0:T(8,128)(2,1)}, bf16[4,2,192,768]{3,2,1,0:T(8,128)(2,1)}, bf16[4,2,192,102...) custom-call(s32[4]{0:T(128)} %add_add_fusion.meta_ref, ...), custom_call_target="tpu_custom_call", output_to_operand_aliasing={{1}: (11, {}), {2}: (12, {}), {3}: (13, {}), {4}: (14, {}),... | custom-call | bytes 8840000 | tf_op jit(solution)/shard_map/pallas_call | solution.py:709
  199.4 7.4 %shard_map.290 = (bf16[2,192,768]{2,1,0:T(8,128)(2,1)}, bf16[2,192,768]{2,1,0:T(8,128)(2,1)}) custom-call(s32[1]{0:T(128)} %bitcast.2.core_ref, bf16[4,512,768]{2,1,0:T(8,128)(2,1)} %get-tuple-element.446.x_ref.refs_0_, bf16[4,528,768]{2,1,0:T(8,128)(2,1)} %get-tuple-element.412.c_ref.refs_1_, bf16[4,512,256]{2,1,0:T(8,128)(2,1)} %get-tuple-element.414.a_ref, ...), custom_call_target="tpu_custom_call" | custom-call | bytes 2720000 | tf_op jit(solution)/shard_map/pallas_call | solution.py:838
  206.8 5.8 %shard_map.289 = (bf16[2,2,192,1024]{3,2,1,0:T(8,128)(2,1)}, bf16[2,2,192,1024]{3,2,1,0:T(8,128)(2,1)}) custom-call(s32[1]{0:T(128)} %bitcast.2.core_ref, bf16[4,2,192,768]{3,2,1,0:T(8,128)(2,1)} %get-tuple-element.418.left_ref, bf16[4,2,192,1024]{3,2,1,0:T(8,128)(2,1)} %get-tuple-element.409.right_ref), custom_call_target="tpu_custom_call" | custom-call | bytes 2040000 | tf_op jit(solution)/shard_map/pallas_call | solution.py:800
  218.5 5.8 %shard_map.292 = (bf16[2,2,192,1024]{3,2,1,0:T(8,128)(2,1)}, bf16[2,2,192,1024]{3,2,1,0:T(8,128)(2,1)}) custom-call(s32[1]{0:T(128)} %bitcast.2.core_ref, bf16[4,2,192,768]{3,2,1,0:T(8,128)(2,1)} %get-tuple-element.428.left_ref, bf16[4,2,192,1024]{3,2,1,0:T(8,128)(2,1)} %get-tuple-element.411.right_ref), custom_call_target="tpu_custom_call" | custom-call | bytes 2040000 | tf_op jit(solution)/shard_map/pallas_call | solution.py:800
  224.3 5.8 %shard_map.291 = (bf16[2,2,192,1024]{3,2,1,0:T(8,128)(2,1)}, bf16[2,2,192,1024]{3,2,1,0:T(8,128)(2,1)}) custom-call(s32[1]{0:T(128)} %bitcast.2.core_ref, bf16[4,2,192,768]{3,2,1,0:T(8,128)(2,1)} %get-tuple-element.428.left_ref, bf16[4,2,192,1024]{3,2,1,0:T(8,128)(2,1)} %get-tuple-element.410.right_ref), custom_call_target="tpu_custom_call" | custom-call | bytes 2040000 | tf_op jit(solution)/shard_map/pallas_call | solution.py:800
  230.1 6.3 %collective-permute-done.33 = bf16[256,768]{1,0:T(8,128)(2,1)S(1)} collective-permute-done((bf16[256,768]{1,0:T(8,128)(2,1)S(1)}, bf16[256,768]{1,0:T(8,128)(2,1)S(1)}, u32[]{:S(2)}, u32[]{:S(2)}) %collective-permute-start.33) | collective-permute-done | bytes 393248 | tf_op jit(solution)/shard_map/ppermute | solution.py:50
  245.6 3.8 collective-permute-start.38
  252.9 19.4 %shard_map.295 = (bf16[4,2,192,768]{3,2,1,0:T(8,128)(2,1)}, bf16[4,2,192,768]{3,2,1,0:T(8,128)(2,1)}, bf16[4,2,192,1024]{3,2,1,0:T(8,128)(2,1)}, bf16[4,2,192,10...) custom-call(s32[2]{0:T(128)} %pad_add_fusion.2.meta_ref, bf16[4,512,768]{2,1,0:T(8,128)(2,1)} %get-tuple-element.446.x_ref.refs_0_, ...), custom_call_target="tpu_custom_call" | custom-call | bytes 8160000 | tf_op jit(solution)/shard_map/pallas_call | solution.py:730
  272.4 3.4 fusion
  283.7 5.8 %shard_map.297 = (bf16[2,2,192,1024]{3,2,1,0:T(8,128)(2,1)}, bf16[2,2,192,1024]{3,2,1,0:T(8,128)(2,1)}) custom-call(s32[1]{0:T(128)} %bitcast.2.core_ref, bf16[4,2,192,768]{3,2,1,0:T(8,128)(2,1)} %get-tuple-element.458.left_ref, bf16[4,2,192,1024]{3,2,1,0:T(8,128)(2,1)} %get-tuple-element.450.right_ref), custom_call_target="tpu_custom_call" | custom-call | bytes 2040000 | tf_op jit(solution)/shard_map/pallas_call | solution.py:800
  289.5 5.9 %shard_map.296 = (bf16[2,2,192,1024]{3,2,1,0:T(8,128)(2,1)}, bf16[2,2,192,1024]{3,2,1,0:T(8,128)(2,1)}) custom-call(s32[1]{0:T(128)} %bitcast.2.core_ref, bf16[4,2,192,768]{3,2,1,0:T(8,128)(2,1)} %get-tuple-element.476.left_ref, bf16[4,2,192,1024]{3,2,1,0:T(8,128)(2,1)} %get-tuple-element.451.right_ref), custom_call_target="tpu_custom_call" | custom-call | bytes 2040000 | tf_op jit(solution)/shard_map/pallas_call | solution.py:800
  297.3 2.6 shard_map.298.refs_0_
  302.7 6.7 %reduce-scatter.2.cloned.1.call-done = bf16[1,256,768]{2,1,0:T(8,128)(2,1)} async-done(((bf16[4,256,768]{2,1,0:T(8,128)(2,1)}), bf16[1,256,768]{2,1,0:T(8,128)(2,1)}) %reduce-scatter.2.cloned.1.call-update) | async-done | bytes 393232 | tf_op jit(solution)/shard_map/reduce_scatter | solution.py:1230
  315.0 5.8 %shard_map.301 = (bf16[2,2,192,1024]{3,2,1,0:T(8,128)(2,1)}, bf16[2,2,192,1024]{3,2,1,0:T(8,128)(2,1)}) custom-call(s32[1]{0:T(128)} %bitcast.2.core_ref, bf16[4,2,192,768]{3,2,1,0:T(8,128)(2,1)} %get-tuple-element.476.left_ref, bf16[4,2,192,1024]{3,2,1,0:T(8,128)(2,1)} %get-tuple-element.452.right_ref), custom_call_target="tpu_custom_call" | custom-call | bytes 2040000 | tf_op jit(solution)/shard_map/pallas_call | solution.py:800
  324.8 7.0 %collective-permute-done.43.refs_0_ = bf16[2,192,1024]{2,1,0:T(8,128)(2,1)S(1)} collective-permute-done((bf16[2,192,1024]{2,1,0:T(8,128)(2,1)}, bf16[2,192,1024]{2,1,0:T(8,128)(2,1)S(1)}, u32[]{:S(2)}, u32[]{:S(2)}) %collective-permute-start.43) | collective-permute-done | bytes 786464 | tf_op jit(solution)/shard_map/ppermute | solution.py:40
  331.8 20.2 %collective-permute-done.45.refs_1_ = bf16[2,192,1024]{2,1,0:T(8,128)(2,1)S(1)} collective-permute-done((bf16[2,192,1024]{2,1,0:T(8,128)(2,1)}, bf16[2,192,1024]{2,1,0:T(8,128)(2,1)S(1)}, u32[]{:S(2)}, u32[]{:S(2)}) %collective-permute-start.45) | collective-permute-done | bytes 786464 | tf_op jit(solution)/shard_map/ppermute | solution.py:60
  360.5 17.5 %shard_map.305 = (bf16[512,384]{1,0:T(8,128)(2,1)}, bf16[1536,384]{1,0:T(8,128)(2,1)}, bf16[1536,384]{1,0:T(8,128)(2,1)}) custom-call(bf16[512,384]{1,0:T(8,128)(2,1)} %get-tuple-element.332.q_ref, bf16[1536,384]{1,0:T(8,128)(2,1)} %get-tuple-element.338.k_ref, bf16[1536,384]{1,0:T(8,128)(2,1)} %get-tuple-element.339.v_ref, ...), custom_call_target="tpu_custom_call" | custom-call | bytes 6120000 | tf_op jit(solution)/shard_map/pallas_call | solution.py:536
  380.5 2.8 shard_map.310
  387.4 7.8 %shard_map.307 = (bf16[3,512,768]{2,1,0:T(8,128)(2,1)}, f32[1,768]{1,0:T(1,128)}) custom-call(bf16[512,768]{1,0:T(8,128)(2,1)} %get-tuple-element.337.refs_0_, bf16[512,768]{1,0:T(8,128)(2,1)} %get-tuple-element.334.refs_1_, bf16[512,768]{1,0:T(8,128)(2,1)} %bitcast.173, bf16[1536,384]{1,0:T(8,128)(2,1)} %get-tuple-element.500.refs_3_.dk_ref, ...), custom_call_target="tpu_custom_call" | custom-call | bytes 2380000 | tf_op jit(solution)/shard_map/pallas_call | solution.py:913
  395.2 7.6 %shard_map.308 = (bf16[2,192,1536]{2,1,0:T(8,128)(2,1)}, bf16[2,192,1536]{2,1,0:T(8,128)(2,1)}) custom-call(s32[1]{0:T(128)} %bitcast.2.core_ref, bf16[1536,768]{1,0:T(8,128)(2,1)} %get-tuple-element.504.hid_ref, bf16[1536,384]{1,0:T(8,128)(2,1)} %get-tuple-element.500.refs_3_.dk_ref, bf16[1536,384]{1,0:T(8,128)(2,1)} %get-tuple-element.501.refs_4_.dv_ref, ...), custom_call_target="tpu_custom_call" | custom-call | bytes 2720000 | tf_op jit(solution)/shard_map/pallas_call | solution.py:871
  402.8 2.6 shard_map.309.refs_2_
  405.8 2.9 shard_map.312
  414.3 7.4 %collective-permute-done.54 = f32[16,768]{1,0:T(8,128)S(1)} collective-permute-done((f32[16,768]{1,0:T(8,128)S(1)}, f32[16,768]{1,0:T(8,128)S(1)}, u32[]{:S(2)}, u32[]{:S(2)}) %collective-permute-start.54) | collective-permute-done | bytes 49184 | tf_op jit(solution)/shard_map/ppermute | solution.py:110
  421.7 6.5 %collective-permute-done.55.refs_0_ = bf16[2,192,1024]{2,1,0:T(8,128)(2,1)S(1)} collective-permute-done((bf16[2,192,1024]{2,1,0:T(8,128)(2,1)}, bf16[2,192,1024]{2,1,0:T(8,128)(2,1)S(1)}, u32[]{:S(2)}, u32[]{:S(2)}) %collective-permute-start.55) | collective-permute-done | bytes 786464 | tf_op jit(solution)/shard_map/ppermute | solution.py:40
  439.4 16.8 %collective-permute-done.58 = bf16[256,768]{1,0:T(8,128)(2,1)S(1)} collective-permute-done((bf16[256,768]{1,0:T(8,128)(2,1)S(1)}, bf16[256,768]{1,0:T(8,128)(2,1)S(1)}, u32[]{:S(2)}, u32[]{:S(2)}) %collective-permute-start.58) | collective-permute-done | bytes 393248 | tf_op jit(solution)/shard_map/ppermute | solution.py:66
  465.6 2.9 reshape.375
  470.9 8.0 %shard_map.316 = f32[8,192,1024]{2,1,0:T(8,128)} custom-call(s32[4]{0:T(128)} %pad_add_fusion.3.places_ref, bf16[2,192,1024]{2,1,0:T(8,128)(2,1)} %shard_map.298.refs_0_, bf16[2,192,1024]{2,1,0:T(8,128)(2,1)} %copy-done.28, bf16[2,192,1024]{2,1,0:T(8,128)(2,1)} %shard_map.309.refs_2_, bf16[2,192,1024]{2,1,0:T(8,128)(2,1)} %copy-done.30), custom_call_target="tpu_custom_call" | custom-call | bytes 1700000 | tf_op jit(solution)/shard_map/pallas_call | solution.py:944
  479.8 2.7 collective-permute-done.63
  488.7 2.8 collective-permute-start.69
  498.0 7.8 %shard_map.317 = f32[8,192,1024]{2,1,0:T(8,128)} custom-call(s32[4]{0:T(128)} %pad_add_fusion.3.places_ref, bf16[2,192,1024]{2,1,0:T(8,128)(2,1)} %shard_map.302.refs_0_, bf16[2,192,1024]{2,1,0:T(8,128)(2,1)} %collective-permute-done.49.refs_1_, bf16[2,192,1024]{2,1,0:T(8,128)(2,1)} %shard_map.311.refs_2_, bf16[2,192,1024]{2,1,0:T(8,128)(2,1)} %copy-done.29), custom_call_target="tpu_custom_call" | custom-call | bytes 1700000 | tf_op jit(solution)/shard_map/pallas_call | solution.py:944
  507.8 2.8 collective-permute-start.73
  513.0 7.8 %shard_map.319 = f32[8,192,1024]{2,1,0:T(8,128)} custom-call(s32[4]{0:T(128)} %pad_add_fusion.3.places_ref, bf16[2,192,1024]{2,1,0:T(8,128)(2,1)} %shard_map.304.refs_0_, bf16[2,192,1024]{2,1,0:T(8,128)(2,1)} %copy-done.27, bf16[2,192,1024]{2,1,0:T(8,128)(2,1)} %shard_map.313.refs_2_, bf16[2,192,1024]{2,1,0:T(8,128)(2,1)} %collective-permute-done.66.refs_3_), custom_call_target="tpu_custom_call" | custom-call | bytes 1700000 | tf_op jit(solution)/shard_map/pallas_call | solution.py:944
  (378 shorter events, 170.9 us)
Async XLA Ops:
  7.2 123.8 %all-gather.7.cloned.1.call-start = ((), (), s32[]{:S(2)}) async-start(), calls=%async_computation.2 | async-start | bytes 13762560 | tf_op jit(solution)/shard_map/all_gather | solution.py:1053
  32.4 220.5 %all-gather.9.cloned.1.call-start = ((), (), s32[]{:S(2)}) async-start(), calls=%async_computation.3 | async-start | bytes 11796480 | tf_op jit(solution)/shard_map/all_gather | solution.py:1137
  60.7 21.9 %collective-permute-start.13 = (bf16[272,768]{1,0:T(8,128)(2,1)S(1)}, bf16[272,768]{1,0:T(8,128)(2,1)S(1)}, u32[]{:S(2)}, u32[]{:S(2)}) collective-permute-start(bf16[272,768]{1,0:T(8,128)(2,1)S(1)} %copy-done.43), channel_id=1, source_target_pairs={{0,4},{2,6},{4,0},{6,2},{1,5},{3,7},{5,1},{7,3},{8,12},{10,14},{12... | collective-permute-start | bytes 1253384 | tf_op jit(solution)/shard_map/ppermute | solution.py:55
  61.5 21.1 %collective-permute-start.14 = (bf16[272,768]{1,0:T(8,128)(2,1)S(1)}, bf16[272,768]{1,0:T(8,128)(2,1)S(1)}, u32[]{:S(2)}, u32[]{:S(2)}) collective-permute-start(bf16[272,768]{1,0:T(8,128)(2,1)S(1)} %collective-permute-done.10.refs_6_), channel_id=1, source_target_pairs={{0,1},{1,0},{2,3},{3,2},{4,5},{5,4},{6,7},{7,6},{8,9},{9,8},{10,11... | collective-permute-start | bytes 1253384 | tf_op jit(solution)/shard_map/ppermute | solution.py:50
  131.0 178.4 %reduce-scatter.2.cloned.1.call-start = ((), (), s32[]{:S(2)}) async-start(), calls=%async_computation.1 | async-start | bytes 1966080 | tf_op jit(solution)/shard_map/reduce_scatter | solution.py:1230
  131.1 33.8 %collective-permute-start.24 = (bf16[272,768]{1,0:T(8,128)(2,1)S(1)}, bf16[272,768]{1,0:T(8,128)(2,1)}, u32[]{:S(2)}, u32[]{:S(2)}) collective-permute-start(bf16[272,768]{1,0:T(8,128)(2,1)S(1)} %collective-permute-done.13.refs_4_), channel_id=1, source_target_pairs={{0,1},{1,0},{2,3},{3,2},{4,5},{5,4},{6,7},{7,6},{8,9},{9,8},{10,11... | collective-permute-start | bytes 1253384 | tf_op jit(solution)/shard_map/ppermute | solution.py:50
  132.6 32.3 %collective-permute-start.25 = (bf16[272,768]{1,0:T(8,128)(2,1)}, bf16[272,768]{1,0:T(8,128)(2,1)}, u32[]{:S(2)}, u32[]{:S(2)}) collective-permute-start(bf16[272,768]{1,0:T(8,128)(2,1)} %collective-permute-done.16.refs_6_), channel_id=1, source_target_pairs={{0,1},{1,0},{2,3},{3,2},{4,5},{5,4},{6,7},{7,6},{8,9},{9,8},{10,11... | collective-permute-start | bytes 1253384 | tf_op jit(solution)/shard_map/ppermute | solution.py:50
  133.2 31.7 %collective-permute-start.23 = (bf16[256,768]{1,0:T(8,128)(2,1)}, bf16[256,768]{1,0:T(8,128)(2,1)}, u32[]{:S(2)}, u32[]{:S(2)}) collective-permute-start(bf16[256,768]{1,0:T(8,128)(2,1)} %collective-permute-done.21.refs_2_), channel_id=1, source_target_pairs={{0,1},{1,0},{2,3},{3,2},{4,5},{5,4},{6,7},{7,6},{8,9},{9,8},{10,11... | collective-permute-start | bytes 1179656 | tf_op jit(solution)/shard_map/ppermute | solution.py:50
  165.9 30.8 %collective-permute-start.26 = (bf16[272,768]{1,0:T(8,128)(2,1)}, bf16[272,768]{1,0:T(8,128)(2,1)S(1)}, u32[]{:S(2)}, u32[]{:S(2)}) collective-permute-start(bf16[272,768]{1,0:T(8,128)(2,1)} %dynamic-slice_bitcast_fusion.4), channel_id=1, source_target_pairs={{0,1},{1,0},{2,3},{3,2},{4,5},{5,4},{6,7},{7,6},{8,9},{9,8},{10,11... | collective-permute-start | bytes 1253384 | tf_op jit(solution)/shard_map/ppermute | solution.py:50
  167.7 29.1 %collective-permute-start.27 = (bf16[272,768]{1,0:T(8,128)(2,1)}, bf16[272,768]{1,0:T(8,128)(2,1)}, u32[]{:S(2)}, u32[]{:S(2)}) collective-permute-start(bf16[272,768]{1,0:T(8,128)(2,1)} %dynamic-slice_bitcast_fusion.3), channel_id=1, source_target_pairs={{0,1},{1,0},{2,3},{3,2},{4,5},{5,4},{6,7},{7,6},{8,9},{9,8},{10,11... | collective-permute-start | bytes 1253384 | tf_op jit(solution)/shard_map/ppermute | solution.py:50
  214.4 22.1 %collective-permute-start.31 = (bf16[2,2,192,1024]{3,2,1,0:T(8,128)(2,1)}, bf16[2,2,192,1024]{3,2,1,0:T(8,128)(2,1)S(1)}, u32[]{:S(2)}, u32[]{:S(2)}) collective-permute-start(bf16[2,2,192,1024]{3,2,1,0:T(8,128)(2,1)} %get-tuple-element.431), channel_id=1, source_target_pairs={{0,8},{8,0},{16,24},{24,16},{1,9},{9,1},{17,25},{25,17},{2,10},{10... | collective-permute-start | bytes 4718600 | tf_op jit(solution)/shard_map/ppermute | solution.py:33
  214.5 22.0 %collective-permute-start.34 = (bf16[272,768]{1,0:T(8,128)(2,1)S(1)}, bf16[272,768]{1,0:T(8,128)(2,1)S(1)}, u32[]{:S(2)}, u32[]{:S(2)}) collective-permute-start(bf16[272,768]{1,0:T(8,128)(2,1)S(1)} %fusion.3), channel_id=1, source_target_pairs={{0,4},{2,6},{4,0},{6,2},{1,5},{3,7},{5,1},{7,3},{8,12},{10,14},{12... | collective-permute-start | bytes 1253384 | tf_op jit(solution)/shard_map/ppermute | solution.py:55
  215.8 20.7 %collective-permute-start.32 = (bf16[2,192,768]{2,1,0:T(8,128)(2,1)S(1)}, bf16[2,192,768]{2,1,0:T(8,128)(2,1)S(1)}, u32[]{:S(2)}, u32[]{:S(2)}) collective-permute-start(bf16[2,192,768]{2,1,0:T(8,128)(2,1)S(1)} %copy-done.68), channel_id=1, source_target_pairs={{0,8},{8,0},{16,24},{24,16},{1,9},{9,1},{17,25},{25,17},{2,10},{10... | collective-permute-start | bytes 1769480 | tf_op jit(solution)/shard_map/ppermute | solution.py:33
  216.4 20.1 %collective-permute-start.30 = (bf16[272,768]{1,0:T(8,128)(2,1)S(1)}, bf16[272,768]{1,0:T(8,128)(2,1)S(1)}, u32[]{:S(2)}, u32[]{:S(2)}) collective-permute-start(bf16[272,768]{1,0:T(8,128)(2,1)S(1)} %dynamic-slice_bitcast_fusion.1), channel_id=1, source_target_pairs={{0,1},{1,0},{2,3},{3,2},{4,5},{5,4},{6,7},{7,6},{8,9},{9,8},{10,11... | collective-permute-start | bytes 1253384 | tf_op jit(solution)/shard_map/ppermute | solution.py:50
  218.1 18.3 %collective-permute-start.33 = (bf16[256,768]{1,0:T(8,128)(2,1)S(1)}, bf16[256,768]{1,0:T(8,128)(2,1)S(1)}, u32[]{:S(2)}, u32[]{:S(2)}) collective-permute-start(bf16[256,768]{1,0:T(8,128)(2,1)S(1)} %dynamic-slice_bitcast_fusion.8), channel_id=1, source_target_pairs={{0,1},{1,0},{2,3},{3,2},{4,5},{5,4},{6,7},{7,6},{8,9},{9,8},{10,11... | collective-permute-start | bytes 1179656 | tf_op jit(solution)/shard_map/ppermute | solution.py:50
  238.0 34.3 %collective-permute-start.35 = (bf16[2,2,192,1024]{3,2,1,0:T(8,128)(2,1)}, bf16[2,2,192,1024]{3,2,1,0:T(8,128)(2,1)S(1)}, u32[]{:S(2)}, u32[]{:S(2)}) collective-permute-start(bf16[2,2,192,1024]{3,2,1,0:T(8,128)(2,1)} %get-tuple-element.439), channel_id=1, source_target_pairs={{0,8},{8,0},{16,24},{24,16},{1,9},{9,1},{17,25},{25,17},{2,10},{10... | collective-permute-start | bytes 4718600 | tf_op jit(solution)/shard_map/ppermute | solution.py:33
  240.4 31.9 %collective-permute-start.39 = (bf16[3,256,768]{2,1,0:T(8,128)(2,1)}, bf16[3,256,768]{2,1,0:T(8,128)(2,1)}, u32[]{:S(2)}, u32[]{:S(2)}) collective-permute-start(bf16[3,256,768]{2,1,0:T(8,128)(2,1)} %dynamic-slice_bitcast_fusion), channel_id=1, source_target_pairs={{0,1},{1,0},{2,3},{3,2},{4,5},{5,4},{6,7},{7,6},{8,9},{9,8},{10,11... | collective-permute-start | bytes 3538952 | tf_op jit(solution)/shard_map/ppermute | solution.py:50
  244.4 27.9 %collective-permute-start.36 = (bf16[2,192,1024]{2,1,0:T(8,128)(2,1)}, bf16[2,192,1024]{2,1,0:T(8,128)(2,1)}, u32[]{:S(2)}, u32[]{:S(2)}) collective-permute-start(bf16[2,192,1024]{2,1,0:T(8,128)(2,1)} %shard_map.293), channel_id=1, source_target_pairs={{0,16},{8,24},{16,0},{24,8},{1,17},{9,25},{17,1},{25,9},{2,18},{10... | collective-permute-start | bytes 2359304 | tf_op jit(solution)/shard_map/ppermute | solution.py:40
  245.6 26.7 %collective-permute-start.38 = (bf16[272,768]{1,0:T(8,128)(2,1)}, bf16[272,768]{1,0:T(8,128)(2,1)}, u32[]{:S(2)}, u32[]{:S(2)}) collective-permute-start(bf16[272,768]{1,0:T(8,128)(2,1)} %fusion.2), channel_id=1, source_target_pairs={{0,6},{2,0},{4,2},{6,4},{1,7},{3,1},{5,3},{7,5},{8,14},{10,8},{12,... | collective-permute-start | bytes 1253384 | tf_op jit(solution)/shard_map/ppermute | solution.py:55
  251.2 21.1 %collective-permute-start.37 = (bf16[192,768]{1,0:T(8,128)(2,1)}, bf16[192,768]{1,0:T(8,128)(2,1)S(1)}, u32[]{:S(2)}, u32[]{:S(2)}) collective-permute-start(bf16[192,768]{1,0:T(8,128)(2,1)} %shard_map.294), channel_id=1, source_target_pairs={{0,16},{8,24},{16,0},{24,8},{1,17},{9,25},{17,1},{25,9},{2,18},{10... | collective-permute-start | bytes 884744 | tf_op jit(solution)/shard_map/ppermute | solution.py:40
  275.8 104.7 %all-gather.11.cloned.1.call-start = ((), (), s32[]{:S(2)}) async-start(), calls=%async_computation.4 | async-start | bytes 1474560 | tf_op jit(solution)/shard_map/all_gather | solution.py:1241
  275.9 26.8 %collective-permute-start.40 = (bf16[2,2,192,1024]{3,2,1,0:T(8,128)(2,1)}, bf16[2,2,192,1024]{3,2,1,0:T(8,128)(2,1)S(1)}, u32[]{:S(2)}, u32[]{:S(2)}) collective-permute-start(bf16[2,2,192,1024]{3,2,1,0:T(8,128)(2,1)} %get-tuple-element.460), channel_id=1, source_target_pairs={{0,8},{8,0},{16,24},{24,16},{1,9},{9,1},{17,25},{25,17},{2,10},{10... | collective-permute-start | bytes 4718600 | tf_op jit(solution)/shard_map/ppermute | solution.py:33
  278.7 24.0 %collective-permute-start.41 = (bf16[2,192,1024]{2,1,0:T(8,128)(2,1)}, bf16[2,192,1024]{2,1,0:T(8,128)(2,1)}, u32[]{:S(2)}, u32[]{:S(2)}) collective-permute-start(bf16[2,192,1024]{2,1,0:T(8,128)(2,1)} %shard_map.299), channel_id=1, source_target_pairs={{0,16},{8,24},{16,0},{24,8},{1,17},{9,25},{17,1},{25,9},{2,18},{10... | collective-permute-start | bytes 2359304 | tf_op jit(solution)/shard_map/ppermute | solution.py:40
  309.4 42.6 %collective-permute-start.42 = (bf16[2,2,192,1024]{3,2,1,0:T(8,128)(2,1)}, bf16[2,2,192,1024]{3,2,1,0:T(8,128)(2,1)}, u32[]{:S(2)}, u32[]{:S(2)}) collective-permute-start(bf16[2,2,192,1024]{3,2,1,0:T(8,128)(2,1)} %get-tuple-element.475), channel_id=1, source_target_pairs={{0,8},{8,0},{16,24},{24,16},{1,9},{9,1},{17,25},{25,17},{2,10},{10... | collective-permute-start | bytes 4718600 | tf_op jit(solution)/shard_map/ppermute | solution.py:33
  311.7 20.1 %collective-permute-start.43 = (bf16[2,192,1024]{2,1,0:T(8,128)(2,1)}, bf16[2,192,1024]{2,1,0:T(8,128)(2,1)S(1)}, u32[]{:S(2)}, u32[]{:S(2)}) collective-permute-start(bf16[2,192,1024]{2,1,0:T(8,128)(2,1)} %shard_map.303), channel_id=1, source_target_pairs={{0,16},{8,24},{16,0},{24,8},{1,17},{9,25},{17,1},{25,9},{2,18},{10... | collective-permute-start | bytes 2359304 | tf_op jit(solution)/shard_map/ppermute | solution.py:40
  313.2 38.8 %collective-permute-start.45 = (bf16[2,192,1024]{2,1,0:T(8,128)(2,1)}, bf16[2,192,1024]{2,1,0:T(8,128)(2,1)S(1)}, u32[]{:S(2)}, u32[]{:S(2)}) collective-permute-start(bf16[2,192,1024]{2,1,0:T(8,128)(2,1)} %shard_map.298.refs_0_), channel_id=1, source_target_pairs={{0,2},{2,0},{4,6},{6,4},{1,3},{3,1},{5,7},{7,5},{8,10},{10,8},{12,... | collective-permute-start | bytes 2359304 | tf_op jit(solution)/shard_map/ppermute | solution.py:60
  352.9 27.6 %collective-permute-start.46 = (bf16[2,2,192,1024]{3,2,1,0:T(8,128)(2,1)}, bf16[2,2,192,1024]{3,2,1,0:T(8,128)(2,1)}, u32[]{:S(2)}, u32[]{:S(2)}) collective-permute-start(bf16[2,2,192,1024]{3,2,1,0:T(8,128)(2,1)} %get-tuple-element.487), channel_id=1, source_target_pairs={{0,8},{8,0},{16,24},{24,16},{1,9},{9,1},{17,25},{25,17},{2,10},{10... | collective-permute-start | bytes 4718600 | tf_op jit(solution)/shard_map/ppermute | solution.py:33
  352.9 27.6 %collective-permute-start.48 = (bf16[2,2,192,1024]{3,2,1,0:T(8,128)(2,1)}, bf16[2,2,192,1024]{3,2,1,0:T(8,128)(2,1)S(1)}, u32[]{:S(2)}, u32[]{:S(2)}) collective-permute-start(bf16[2,2,192,1024]{3,2,1,0:T(8,128)(2,1)} %get-tuple-element.498), channel_id=1, source_target_pairs={{0,8},{8,0},{16,24},{24,16},{1,9},{9,1},{17,25},{25,17},{2,10},{10... | collective-permute-start | bytes 4718600 | tf_op jit(solution)/shard_map/ppermute | solution.py:33
  355.6 24.9 %collective-permute-start.47 = (bf16[2,192,1024]{2,1,0:T(8,128)(2,1)}, bf16[2,192,1024]{2,1,0:T(8,128)(2,1)}, u32[]{:S(2)}, u32[]{:S(2)}) collective-permute-start(bf16[2,192,1024]{2,1,0:T(8,128)(2,1)} %shard_map.306), channel_id=1, source_target_pairs={{0,16},{8,24},{16,0},{24,8},{1,17},{9,25},{17,1},{25,9},{2,18},{10... | collective-permute-start | bytes 2359304 | tf_op jit(solution)/shard_map/ppermute | solution.py:40
  355.7 24.8 %collective-permute-start.49 = (bf16[2,192,1024]{2,1,0:T(8,128)(2,1)S(1)}, bf16[2,192,1024]{2,1,0:T(8,128)(2,1)}, u32[]{:S(2)}, u32[]{:S(2)}) collective-permute-start(bf16[2,192,1024]{2,1,0:T(8,128)(2,1)S(1)} %copy-done.15), channel_id=1, source_target_pairs={{0,2},{2,0},{4,6},{6,4},{1,3},{3,1},{5,7},{7,5},{8,10},{10,8},{12,... | collective-permute-start | bytes 2359304 | tf_op jit(solution)/shard_map/ppermute | solution.py:60
  383.3 22.4 %collective-permute-start.50 = (bf16[2,192,1024]{2,1,0:T(8,128)(2,1)}, bf16[2,192,1024]{2,1,0:T(8,128)(2,1)}, u32[]{:S(2)}, u32[]{:S(2)}) collective-permute-start(bf16[2,192,1024]{2,1,0:T(8,128)(2,1)} %shard_map.310), channel_id=1, source_target_pairs={{0,16},{8,24},{16,0},{24,8},{1,17},{9,25},{17,1},{25,9},{2,18},{10... | collective-permute-start | bytes 2359304 | tf_op jit(solution)/shard_map/ppermute | solution.py:40
  385.3 20.5 %collective-permute-start.51 = (bf16[2,192,1024]{2,1,0:T(8,128)(2,1)S(1)}, bf16[2,192,1024]{2,1,0:T(8,128)(2,1)S(1)}, u32[]{:S(2)}, u32[]{:S(2)}) collective-permute-start(bf16[2,192,1024]{2,1,0:T(8,128)(2,1)S(1)} %copy-done.16), channel_id=1, source_target_pairs={{0,2},{2,0},{4,6},{6,4},{1,3},{3,1},{5,7},{7,5},{8,10},{10,8},{12,... | collective-permute-start | bytes 2359304 | tf_op jit(solution)/shard_map/ppermute | solution.py:60
  405.8 23.4 %collective-permute-start.52 = (bf16[2,192,1536]{2,1,0:T(8,128)(2,1)}, bf16[2,192,1536]{2,1,0:T(8,128)(2,1)S(1)}, u32[]{:S(2)}, u32[]{:S(2)}) collective-permute-start(bf16[2,192,1536]{2,1,0:T(8,128)(2,1)} %get-tuple-element.515), channel_id=1, source_target_pairs={{0,8},{8,0},{16,24},{24,16},{1,9},{9,1},{17,25},{25,17},{2,10},{10... | collective-permute-start | bytes 3538952 | tf_op jit(solution)/shard_map/ppermute | solution.py:33
  408.7 19.5 %collective-permute-start.55 = (bf16[2,192,1024]{2,1,0:T(8,128)(2,1)}, bf16[2,192,1024]{2,1,0:T(8,128)(2,1)S(1)}, u32[]{:S(2)}, u32[]{:S(2)}) collective-permute-start(bf16[2,192,1024]{2,1,0:T(8,128)(2,1)} %shard_map.312), channel_id=1, source_target_pairs={{0,16},{8,24},{16,0},{24,8},{1,17},{9,25},{17,1},{25,9},{2,18},{10... | collective-permute-start | bytes 2359304 | tf_op jit(solution)/shard_map/ppermute | solution.py:40
  408.8 19.4 %collective-permute-start.56 = (bf16[2,192,1024]{2,1,0:T(8,128)(2,1)S(1)}, bf16[2,192,1024]{2,1,0:T(8,128)(2,1)S(1)}, u32[]{:S(2)}, u32[]{:S(2)}) collective-permute-start(bf16[2,192,1024]{2,1,0:T(8,128)(2,1)S(1)} %copy-done.17), channel_id=1, source_target_pairs={{0,2},{2,0},{4,6},{6,4},{1,3},{3,1},{5,7},{7,5},{8,10},{10,8},{12,... | collective-permute-start | bytes 2359304 | tf_op jit(solution)/shard_map/ppermute | solution.py:60
  429.2 27.1 %collective-permute-start.61 = (bf16[2,192,1024]{2,1,0:T(8,128)(2,1)}, bf16[2,192,1024]{2,1,0:T(8,128)(2,1)S(1)}, u32[]{:S(2)}, u32[]{:S(2)}) collective-permute-start(bf16[2,192,1024]{2,1,0:T(8,128)(2,1)} %shard_map.311.refs_2_), channel_id=1, source_target_pairs={{0,2},{2,0},{4,6},{6,4},{1,3},{3,1},{5,7},{7,5},{8,10},{10,8},{12,... | collective-permute-start | bytes 2359304 | tf_op jit(solution)/shard_map/ppermute | solution.py:60
  432.4 23.8 %collective-permute-start.59 = (bf16[192,1536]{1,0:T(8,128)(2,1)}, bf16[192,1536]{1,0:T(8,128)(2,1)S(1)}, u32[]{:S(2)}, u32[]{:S(2)}) collective-permute-start(bf16[192,1536]{1,0:T(8,128)(2,1)} %shard_map.314), channel_id=1, source_target_pairs={{0,16},{8,24},{16,0},{24,8},{1,17},{9,25},{17,1},{25,9},{2,18},{10... | collective-permute-start | bytes 1769480 | tf_op jit(solution)/shard_map/ppermute | solution.py:40
  433.9 22.3 %collective-permute-start.58 = (bf16[256,768]{1,0:T(8,128)(2,1)S(1)}, bf16[256,768]{1,0:T(8,128)(2,1)S(1)}, u32[]{:S(2)}, u32[]{:S(2)}) collective-permute-start(bf16[256,768]{1,0:T(8,128)(2,1)S(1)} %fusion.17), channel_id=1, source_target_pairs={{2,0},{4,2},{6,4},{3,1},{5,3},{7,5},{10,8},{12,10},{14,12},{11,9},... | collective-permute-start | bytes 1179656 | tf_op jit(solution)/shard_map/ppermute | solution.py:66
  435.3 20.9 %collective-permute-start.57 = (bf16[256,768]{1,0:T(8,128)(2,1)S(1)}, bf16[256,768]{1,0:T(8,128)(2,1)S(1)}, u32[]{:S(2)}, u32[]{:S(2)}) collective-permute-start(bf16[256,768]{1,0:T(8,128)(2,1)S(1)} %dynamic-slice_bitcast_fusion.6), channel_id=1, source_target_pairs={{0,1},{1,0},{2,3},{3,2},{4,5},{5,4},{6,7},{7,6},{8,9},{9,8},{10,11... | collective-permute-start | bytes 1179656 | tf_op jit(solution)/shard_map/ppermute | solution.py:50
  456.2 26.3 %collective-permute-start.66 = (bf16[2,192,1024]{2,1,0:T(8,128)(2,1)}, bf16[2,192,1024]{2,1,0:T(8,128)(2,1)}, u32[]{:S(2)}, u32[]{:S(2)}) collective-permute-start(bf16[2,192,1024]{2,1,0:T(8,128)(2,1)} %shard_map.313.refs_2_), channel_id=1, source_target_pairs={{0,2},{2,0},{4,6},{6,4},{1,3},{3,1},{5,7},{7,5},{8,10},{10,8},{12,... | collective-permute-start | bytes 2359304 | tf_op jit(solution)/shard_map/ppermute | solution.py:60
  457.3 22.5 %collective-permute-start.65 = (bf16[256,768]{1,0:T(8,128)(2,1)}, bf16[256,768]{1,0:T(8,128)(2,1)}, u32[]{:S(2)}, u32[]{:S(2)}) collective-permute-start(bf16[256,768]{1,0:T(8,128)(2,1)} %add_convert_fusion), channel_id=1, source_target_pairs={{0,1},{1,0},{2,3},{3,2},{4,5},{5,4},{6,7},{7,6},{8,9},{9,8},{10,11... | collective-permute-start | bytes 1179656 | tf_op jit(solution)/shard_map/ppermute | solution.py:50
  459.7 22.9 %collective-permute-start.63 = (bf16[256,768]{1,0:T(8,128)(2,1)}, bf16[256,768]{1,0:T(8,128)(2,1)}, u32[]{:S(2)}, u32[]{:S(2)}) collective-permute-start(bf16[256,768]{1,0:T(8,128)(2,1)} %fusion.16), channel_id=1, source_target_pairs={{2,0},{4,2},{6,4},{3,1},{5,3},{7,5},{10,8},{12,10},{14,12},{11,9},... | collective-permute-start | bytes 1179656 | tf_op jit(solution)/shard_map/ppermute | solution.py:66
  461.7 20.8 %collective-permute-start.62 = (bf16[256,768]{1,0:T(8,128)(2,1)}, bf16[256,768]{1,0:T(8,128)(2,1)}, u32[]{:S(2)}, u32[]{:S(2)}) collective-permute-start(bf16[256,768]{1,0:T(8,128)(2,1)} %dynamic-slice_bitcast_fusion.5), channel_id=1, source_target_pairs={{0,1},{1,0},{2,3},{3,2},{4,5},{5,4},{6,7},{7,6},{8,9},{9,8},{10,11... | collective-permute-start | bytes 1179656 | tf_op jit(solution)/shard_map/ppermute | solution.py:50
  485.6 20.3 %collective-permute-start.70 = (bf16[256,768]{1,0:T(8,128)(2,1)S(1)}, bf16[256,768]{1,0:T(8,128)(2,1)S(1)}, u32[]{:S(2)}, u32[]{:S(2)}) collective-permute-start(bf16[256,768]{1,0:T(8,128)(2,1)S(1)} %fusion.11), channel_id=1, source_target_pairs={{0,1},{1,0},{2,3},{3,2},{4,5},{5,4},{6,7},{7,6},{8,9},{9,8},{10,11... | collective-permute-start | bytes 1179656 | tf_op jit(solution)/shard_map/ppermute | solution.py:50
  487.3 18.5 %collective-permute-start.67 = (bf16[56,1536]{1,0:T(8,128)(2,1)S(1)}, bf16[56,1536]{1,0:T(8,128)(2,1)S(1)}, u32[]{:S(2)}, u32[]{:S(2)}) collective-permute-start(bf16[56,1536]{1,0:T(8,128)(2,1)S(1)} %get-tuple-element.587), channel_id=1, source_target_pairs={{0,2},{2,4},{4,6},{6,0},{1,3},{3,5},{5,7},{7,1},{8,10},{10,12},{12... | collective-permute-start | bytes 516104 | tf_op jit(solution)/shard_map/ppermute | solution.py:55
  487.4 18.4 %collective-permute-start.68 = (bf16[56,1536]{1,0:T(8,128)(2,1)S(1)}, bf16[56,1536]{1,0:T(8,128)(2,1)S(1)}, u32[]{:S(2)}, u32[]{:S(2)}) collective-permute-start(bf16[56,1536]{1,0:T(8,128)(2,1)S(1)} %get-tuple-element.586), channel_id=1, source_target_pairs={{0,4},{2,6},{4,0},{6,2},{1,5},{3,7},{5,1},{7,3},{8,12},{10,14},{12... | collective-permute-start | bytes 516104 | tf_op jit(solution)/shard_map/ppermute | solution.py:55
  488.7 17.1 %collective-permute-start.69 = (bf16[56,1536]{1,0:T(8,128)(2,1)S(1)}, bf16[56,1536]{1,0:T(8,128)(2,1)S(1)}, u32[]{:S(2)}, u32[]{:S(2)}) collective-permute-start(bf16[56,1536]{1,0:T(8,128)(2,1)S(1)} %get-tuple-element.585), channel_id=1, source_target_pairs={{0,6},{2,0},{4,2},{6,4},{1,7},{3,1},{5,3},{7,5},{8,14},{10,8},{12,... | collective-permute-start | bytes 516104 | tf_op jit(solution)/shard_map/ppermute | solution.py:55
  505.9 15.9 %collective-permute-start.71 = (bf16[56,1536]{1,0:T(8,128)(2,1)S(1)}, bf16[56,1536]{1,0:T(8,128)(2,1)S(1)}, u32[]{:S(2)}, u32[]{:S(2)}) collective-permute-start(bf16[56,1536]{1,0:T(8,128)(2,1)S(1)} %add_convert_fusion.1.mine_ref), channel_id=1, source_target_pairs={{0,2},{2,4},{4,6},{6,0},{1,3},{3,5},{5,7},{7,1},{8,10},{10,12},{12... | collective-permute-start | bytes 516104 | tf_op jit(solution)/shard_map/ppermute | solution.py:55
  (99 other events, 1039.9 us)
Sparse Core Ops, SparseCore 0:
  32.5 74.2 all-gather.6
  131.1 61.4 all-gather.8
  275.9 33.4 reduce-scatter.1
  315.1 36.9 all-gather.10
